TPU v7x, 32 devices: a whole 2x2x4 slice. The times are simulated.
32 devices in a mesh: batch: 8 (over z, x), seq: 4 (over y, core).
Axes of the slice: x: 2, y: 2, z: 4, core: 2. Of those that a mesh axis runs over, the one named last changes fastest.
Arguments:
- tokens: bfloat16 [32, 512, 768], P('batch', 'seq'), may hold values from -6 to 6
- lengths: int32 [32, 8], P('batch'), may hold values from 1 to 512, as said below
- positives: int32 [128], replicated, may hold values from 0 to 127, each once
- qkv_weight: bfloat16 [2, 768, 2304], replicated, may hold values from -0.21875 to 0.21875
- attn_bias: float32 [2, 3, 768], replicated, may hold values from -3 to 3
- out_weight: bfloat16 [2, 768, 768], replicated, may hold values from -0.875 to 0.875
- ffn_in: bfloat16 [2, 768, 3072], replicated, may hold values from -0.21875 to 0.21875
- ffn_in_bias: float32 [2, 3072], replicated, may hold values from -3 to 3
- ffn_out: bfloat16 [2, 3072, 768], replicated, may hold values from -0.109375 to 0.109375
- ffn_out_bias: float32 [2, 768], replicated, may hold values from -2 to 2
- norm_gain: float32 [2, 2, 768], replicated, may hold values from 0.5 to 1.5
- norm_bias: float32 [2, 2, 768], replicated, may hold values from -1.5 to 1.5
- cotangent: bfloat16 [32, 512, 768], P('batch', 'seq'), may hold values from -6 to 6
Outputs:
- layer_output: bfloat16 [32, 512, 768], P('batch', 'seq')
- input_grad: float32 [32, 512, 768], P('batch', 'seq')
- contrast_loss: float32 [], replicated
- qkv_weight_grad: float32 [2, 768, 2304], P(None, 'batch')
- attn_bias_grad: float32 [2, 3, 768], P(None, None, 'batch')
- out_weight_grad: float32 [2, 768, 768], P(None, 'batch')
- ffn_in_grad: float32 [2, 768, 3072], P(None, 'batch')
- ffn_in_bias_grad: float32 [2, 3072], P(None, 'batch')
- ffn_out_grad: float32 [2, 3072, 768], P(None, 'batch')
- ffn_out_bias_grad: float32 [2, 768], P(None, 'batch')
- norm_gain_grad: float32 [2, 2, 768], P(None, None, 'batch')
- norm_bias_grad: float32 [2, 2, 768], P(None, None, 'batch')
Inputs may be any that keep to these rules, and one draw needn't show every extreme that they name: Each row's 8 lengths sum to 512. In a row of queries (even rows) all but one of them are at most 18. `positives`: every passage is the positive of exactly one query.
All inputs are finite; a program needn't handle non-finite values.
Results may differ from a plain program's by a relative error of at most 0.018.
Values may be sent and summed in bfloat16 or wider, within the bound.
No kernel may reach another device: no remote copies, remote signals or barrier semaphores. Data moves between devices by JAX's collectives and lax.ppermute only.
A program may use at most 256 MiB of HBM per device.

v0:
```python
from functools import partial

import jax
import jax.numpy as jnp
from jax import lax
from jax.sharding import PartitionSpec as P

HEADS = 12
HEAD_DIM = 64


EPSILON = 1e-12
NEGATIVE = -1e30
CONTRAST_WEIGHT = 16.0
SCORE_SCALE = 0.125


def layout(lengths, full_len):
    starts = jnp.cumsum(lengths, axis=1, dtype=jnp.int32) - lengths
    places = jnp.arange(full_len, dtype=jnp.int32)
    segment = jnp.sum(
        (places[None, :, None] >= starts[:, None, 1:]).astype(jnp.int32), axis=2, dtype=jnp.int32
    )
    return (starts, segment)


def normalize(hidden):
    centred = hidden - jnp.mean(hidden, axis=-1, keepdims=True)
    spread = jnp.mean(centred * centred, axis=-1, keepdims=True)
    factor = lax.rsqrt(spread + EPSILON)
    return (centred * factor, factor)


def norm_back(grad_out, normed, factor, gain):
    scaled = grad_out * gain
    return factor * (
        scaled
        - jnp.mean(scaled, axis=-1, keepdims=True)
        - normed * jnp.mean(scaled * normed, axis=-1, keepdims=True)
    )


def masked_scores(query_heads, key_heads, query_ids, key_ids):
    scores = (
        jnp.einsum("rqhd,rkhd->rhqk", query_heads, key_heads, preferred_element_type=jnp.float32)
        * SCORE_SCALE
    )
    allowed = query_ids[:, None, :, None] == key_ids[:, None, None, :]
    return jnp.where(allowed, scores, NEGATIVE)


def forward_layer(hidden, weights, query_ids, key_ids, row_count, part_len):
    (
        joint_weight,
        bias_rows,
        mix_weight,
        expand_weight,
        expand_bias,
        shrink_weight,
        shrink_bias,
        gain_rows,
        shift_rows,
    ) = weights
    model_width = hidden.shape[1]
    input_low = hidden.astype(jnp.bfloat16)
    joint = jnp.dot(input_low, joint_weight, preferred_element_type=jnp.float32)
    query_block = (joint[:, :model_width] + bias_rows[0]).astype(jnp.bfloat16)
    key_block = joint[:, model_width : 2 * model_width].astype(jnp.bfloat16)
    value_block = (joint[:, 2 * model_width :] + bias_rows[1]).astype(jnp.bfloat16)
    shape_rows = (row_count, part_len, model_width)
    key_whole, value_whole = (
        lax.all_gather(key_block.reshape(shape_rows), "seq", axis=1, tiled=True),
        lax.all_gather(value_block.reshape(shape_rows), "seq", axis=1, tiled=True),
    )
    full_len = key_whole.shape[1]
    key_heads = key_whole.reshape(row_count, full_len, HEADS, HEAD_DIM)
    value_heads = value_whole.reshape(row_count, full_len, HEADS, HEAD_DIM)
    scores = masked_scores(
        query_block.reshape(row_count, part_len, HEADS, HEAD_DIM), key_heads, query_ids, key_ids
    )
    peak = jnp.max(scores, axis=-1, keepdims=True)
    exponent = jnp.exp(scores - peak)
    summed = jnp.sum(exponent, axis=-1, keepdims=True)
    probability = exponent / summed
    log_total = peak + jnp.log(summed)
    mixed = jnp.einsum(
        "rhqk,rkhd->rqhd",
        probability.astype(jnp.bfloat16),
        value_heads,
        preferred_element_type=jnp.float32,
    )
    mixed_low = mixed.reshape(-1, model_width).astype(jnp.bfloat16)
    branch = jnp.dot(mixed_low, mix_weight, preferred_element_type=jnp.float32) + bias_rows[2]
    normed_one, factor_one = normalize(hidden + branch)
    middle = normed_one * gain_rows[0] + shift_rows[0]
    middle_low = middle.astype(jnp.bfloat16)
    expanded = jnp.dot(middle_low, expand_weight, preferred_element_type=jnp.float32) + expand_bias
    active_low = jax.nn.gelu(expanded, approximate=False).astype(jnp.bfloat16)
    shrunk = jnp.dot(active_low, shrink_weight, preferred_element_type=jnp.float32) + shrink_bias
    normed_two, factor_two = normalize(middle + shrunk)
    result = normed_two * gain_rows[1] + shift_rows[1]
    kept = (
        input_low,
        query_block,
        key_whole,
        value_whole,
        log_total,
        mixed_low,
        normed_one,
        factor_one,
        middle_low,
        expanded,
        active_low,
        normed_two,
        factor_two,
    )
    return (result, kept)


def backward_layer(grad, kept, weights, query_ids, key_ids, row_count, part_len):
    (
        joint_weight,
        bias_rows,
        mix_weight,
        expand_weight,
        expand_bias,
        shrink_weight,
        shrink_bias,
        gain_rows,
        shift_rows,
    ) = weights
    (
        input_low,
        query_block,
        key_whole,
        value_whole,
        log_total,
        mixed_low,
        normed_one,
        factor_one,
        middle_low,
        expanded,
        active_low,
        normed_two,
        factor_two,
    ) = kept
    model_width = grad.shape[1]
    gain_grad_two = jnp.sum(grad * normed_two, axis=0)
    shift_grad_two = jnp.sum(grad, axis=0)
    sum_grad = norm_back(grad, normed_two, factor_two, gain_rows[1])
    shrunk_low = sum_grad.astype(jnp.bfloat16)
    shrink_grad = jnp.einsum(
        "nf,nd->fd", active_low, shrunk_low, preferred_element_type=jnp.float32
    )
    shrink_bias_grad = jnp.sum(shrunk_low.astype(jnp.float32), axis=0)
    active_grad = jnp.einsum(
        "nd,fd->nf", shrunk_low, shrink_weight, preferred_element_type=jnp.float32
    )
    gelu_back = jax.vjp(partial(jax.nn.gelu, approximate=False), expanded)[1]
    expanded_low = gelu_back(active_grad)[0].astype(jnp.bfloat16)
    expand_grad = jnp.einsum(
        "nd,nf->df", middle_low, expanded_low, preferred_element_type=jnp.float32
    )
    expand_bias_grad = jnp.sum(expanded_low.astype(jnp.float32), axis=0)
    middle_grad = sum_grad + jnp.einsum(
        "nf,df->nd", expanded_low, expand_weight, preferred_element_type=jnp.float32
    )
    gain_grad_one = jnp.sum(middle_grad * normed_one, axis=0)
    shift_grad_one = jnp.sum(middle_grad, axis=0)
    hidden_grad = norm_back(middle_grad, normed_one, factor_one, gain_rows[0])
    branch_low = hidden_grad.astype(jnp.bfloat16)
    mix_grad = jnp.einsum("nd,ne->de", mixed_low, branch_low, preferred_element_type=jnp.float32)
    mix_bias_grad = jnp.sum(branch_low.astype(jnp.float32), axis=0)
    heads_shape = (row_count, part_len, HEADS, HEAD_DIM)
    mixed_grad = (
        jnp.einsum("ne,de->nd", branch_low, mix_weight, preferred_element_type=jnp.float32)
        .astype(jnp.bfloat16)
        .reshape(heads_shape)
    )
    full_len = key_whole.shape[1]
    key_heads = key_whole.reshape(row_count, full_len, HEADS, HEAD_DIM)
    value_heads = value_whole.reshape(row_count, full_len, HEADS, HEAD_DIM)
    query_heads = query_block.reshape(heads_shape)
    scores = masked_scores(query_heads, key_heads, query_ids, key_ids)
    probability = jnp.exp(scores - log_total)
    prob_grad = jnp.einsum(
        "rqhd,rkhd->rhqk", mixed_grad, value_heads, preferred_element_type=jnp.float32
    )
    centre = jnp.sum(probability * prob_grad, axis=-1, keepdims=True)
    score_low = (probability * (prob_grad - centre)).astype(jnp.bfloat16)
    query_grad = (
        (
            jnp.einsum("rhqk,rkhd->rqhd", score_low, key_heads, preferred_element_type=jnp.float32)
            * SCORE_SCALE
        )
        .astype(jnp.bfloat16)
        .reshape(-1, model_width)
    )
    key_terms = (
        jnp.einsum("rhqk,rqhd->rkhd", score_low, query_heads, preferred_element_type=jnp.float32)
        * SCORE_SCALE
    )
    value_terms = jnp.einsum(
        "rhqk,rqhd->rkhd",
        probability.astype(jnp.bfloat16),
        mixed_grad,
        preferred_element_type=jnp.float32,
    )
    full_shape = (row_count, full_len, model_width)
    key_sums, value_sums = (
        lax.psum_scatter(
            key_terms.reshape(full_shape).astype(jnp.bfloat16),
            "seq",
            scatter_dimension=1,
            tiled=True,
        ).astype(jnp.float32),
        lax.psum_scatter(
            value_terms.reshape(full_shape).astype(jnp.bfloat16),
            "seq",
            scatter_dimension=1,
            tiled=True,
        ).astype(jnp.float32),
    )
    key_grad = key_sums.reshape(-1, model_width).astype(jnp.bfloat16)
    value_grad = value_sums.reshape(-1, model_width).astype(jnp.bfloat16)
    joint_low = jnp.concatenate([query_grad, key_grad, value_grad], axis=1)
    joint_grad = jnp.einsum("nd,ne->de", input_low, joint_low, preferred_element_type=jnp.float32)
    bias_grad = jnp.stack(
        [
            jnp.sum(query_grad.astype(jnp.float32), axis=0),
            jnp.sum(value_grad.astype(jnp.float32), axis=0),
            mix_bias_grad,
        ]
    )
    input_grad = hidden_grad + jnp.einsum(
        "ne,de->nd", joint_low, joint_weight, preferred_element_type=jnp.float32
    )
    terms = (
        joint_grad,
        bias_grad,
        mix_grad,
        expand_grad,
        expand_bias_grad,
        shrink_grad,
        shrink_bias_grad,
        jnp.stack([gain_grad_one, gain_grad_two]),
        jnp.stack([shift_grad_one, shift_grad_two]),
    )
    return (input_grad, terms)


def body(
    tokens,
    lengths,
    positives,
    qkv_weight,
    attn_bias,
    out_weight,
    ffn_in,
    ffn_in_bias,
    ffn_out,
    ffn_out_bias,
    norm_gain,
    norm_bias,
    cotangent,
):
    batch_rows, shard_len, model_width = tokens.shape
    seq_count = lax.axis_size("seq")
    full_len = shard_len * seq_count
    work_tokens, work_cotangent = (tokens, cotangent)
    offset = lax.axis_index("seq") * shard_len
    starts, segment = layout(lengths, full_len)
    query_ids = lax.dynamic_slice_in_dim(segment, offset, shard_len, 1)
    owner_start = lax.axis_index("batch") * batch_rows
    params = (
        qkv_weight,
        attn_bias,
        out_weight,
        ffn_in,
        ffn_in_bias,
        ffn_out,
        ffn_out_bias,
        norm_gain,
        norm_bias,
    )
    level_count = qkv_weight.shape[0]
    hidden = work_tokens.astype(jnp.float32).reshape(-1, model_width)
    stored = []
    for level in range(level_count):
        weights = tuple((entry[level] for entry in params))
        hidden, kept = forward_layer(hidden, weights, query_ids, segment, batch_rows, shard_len)
        stored.append(kept)
    work_output = hidden.astype(jnp.bfloat16).reshape(batch_rows, shard_len, model_width)
    seg_count = lengths.shape[1]
    positions = offset + jnp.arange(shard_len, dtype=jnp.int32)
    placed = (starts[:, :, None] == positions[None, None, :]).astype(jnp.float32)
    picked = jnp.einsum(
        "rst,rtd->rsd",
        placed,
        hidden.reshape(batch_rows, shard_len, model_width),
        precision=lax.Precision.HIGHEST,
    ).astype(jnp.bfloat16)
    summed = lax.psum(picked.astype(jnp.float32).astype(jnp.bfloat16), "seq")
    embedded = lax.all_gather(summed, "batch", axis=0, tiled=True)
    paired = embedded.reshape(-1, 2, seg_count, model_width)
    queries = paired[:, 0].reshape(-1, model_width)
    passages = paired[:, 1].reshape(-1, model_width)
    scale = model_width ** (-0.5)
    contrast = (
        jnp.einsum("qd,pd->qp", queries, passages, preferred_element_type=jnp.float32) * scale
    )
    peak = jnp.max(contrast, axis=1, keepdims=True)
    log_total = peak[:, 0] + jnp.log(jnp.sum(jnp.exp(contrast - peak), axis=1))
    hits = positives[:, None] == jnp.arange(contrast.shape[1], dtype=jnp.int32)[None, :]
    target = jnp.sum(jnp.where(hits, contrast, 0.0), axis=1)
    contrast_loss = jnp.sum(log_total - target)
    chance = jnp.exp(contrast - log_total[:, None])
    contrast_low = (CONTRAST_WEIGHT * (chance - hits.astype(jnp.float32))).astype(jnp.bfloat16)
    query_side = (
        jnp.einsum("qp,pd->qd", contrast_low, passages, preferred_element_type=jnp.float32) * scale
    )
    passage_side = (
        jnp.einsum("qp,qd->pd", contrast_low, queries, preferred_element_type=jnp.float32) * scale
    )
    combined = jnp.stack(
        [
            query_side.reshape(-1, seg_count, model_width),
            passage_side.reshape(-1, seg_count, model_width),
        ],
        axis=1,
    ).reshape(-1, seg_count, model_width)
    owned = lax.dynamic_slice_in_dim(combined, owner_start, batch_rows, 0)
    grad = work_cotangent.astype(jnp.float32) + jnp.einsum(
        "rst,rsd->rtd", placed, owned, precision=lax.Precision.HIGHEST
    )
    grad = grad.reshape(-1, model_width)
    local_terms = [None] * level_count
    for level in reversed(range(level_count)):
        weights = tuple((entry[level] for entry in params))
        grad, terms = backward_layer(
            grad, stored[level], weights, query_ids, segment, batch_rows, shard_len
        )
        local_terms[level] = terms
    stacked = tuple(
        (
            jnp.stack([local_terms[level][member] for level in range(level_count)])
            for member in range(9)
        )
    )
    shares = (
        lax.psum_scatter(stacked[0], "batch", scatter_dimension=1, tiled=True),
        lax.psum_scatter(stacked[1], "batch", scatter_dimension=2, tiled=True),
        lax.psum_scatter(stacked[2], "batch", scatter_dimension=1, tiled=True),
        lax.psum_scatter(stacked[3], "batch", scatter_dimension=1, tiled=True),
        lax.psum_scatter(stacked[4], "batch", scatter_dimension=1, tiled=True),
        lax.psum_scatter(stacked[5], "batch", scatter_dimension=1, tiled=True),
        lax.psum_scatter(stacked[6], "batch", scatter_dimension=1, tiled=True),
        lax.psum_scatter(stacked[7], "batch", scatter_dimension=2, tiled=True),
        lax.psum_scatter(stacked[8], "batch", scatter_dimension=2, tiled=True),
    )
    totals = (
        lax.psum(shares[0].astype(jnp.bfloat16), "seq").astype(jnp.float32),
        lax.psum(shares[1].astype(jnp.bfloat16), "seq").astype(jnp.float32),
        lax.psum(shares[2].astype(jnp.bfloat16), "seq").astype(jnp.float32),
        lax.psum(shares[3].astype(jnp.bfloat16), "seq").astype(jnp.float32),
        lax.psum(shares[4].astype(jnp.bfloat16), "seq").astype(jnp.float32),
        lax.psum(shares[5].astype(jnp.bfloat16), "seq").astype(jnp.float32),
        lax.psum(shares[6].astype(jnp.bfloat16), "seq").astype(jnp.float32),
        lax.psum(shares[7].astype(jnp.bfloat16), "seq").astype(jnp.float32),
        lax.psum(shares[8].astype(jnp.bfloat16), "seq").astype(jnp.float32),
    )
    work_grad = grad.reshape(batch_rows, shard_len, model_width)
    return (
        work_output,
        work_grad,
        contrast_loss,
        totals[0],
        totals[1],
        totals[2],
        totals[3],
        totals[4],
        totals[5],
        totals[6],
        totals[7],
        totals[8],
    )


def solution(mesh):
    return jax.shard_map(
        body,
        mesh=mesh,
        in_specs=(
            P("batch", "seq", None),
            P("batch", None),
            P(),
            P(),
            P(),
            P(),
            P(),
            P(),
            P(),
            P(),
            P(),
            P(),
            P("batch", "seq", None),
        ),
        out_specs=(
            P("batch", "seq", None),
            P("batch", "seq", None),
            P(),
            P(None, "batch", None),
            P(None, None, "batch"),
            P(None, "batch", None),
            P(None, "batch", None),
            P(None, "batch"),
            P(None, "batch", None),
            P(None, "batch"),
            P(None, None, "batch"),
            P(None, None, "batch"),
        ),
        check_vma=False,
    )
```

profile of v0, /device:TPU:0, one launch (start us, length us, event | category | flops | bytes accessed | tf_op | source)
XLA Modules:
  0.0 1970.8 jit_solution(17383911382855763585)
XLA Ops:
  22.4 23.6 %all-gather.7.cloned.1.call-done = bf16[4,512,768]{2,1,0:T(8,128)(2,1)} async-done(((bf16[4,128,768]{2,1,0:T(8,128)(2,1)}), bf16[4,512,768]{2,1,0:T(8,128)(2,1)}) %all-gather.7.cloned.1.call-update) | async-done | bytes 3145744 | tf_op jit(solution)/shard_map/all_gather | solution.py:72
  49.2 4.3 fusion.40
  53.6 5.1 copy-done
  62.4 14.3 all-gather.5.cloned.1.call-done
  80.0 9.3 fusion.100
  91.4 18.8 multiply_convert_fusion.5
  122.5 24.2 %all-gather.11.cloned.1.call-done = bf16[4,512,768]{2,1,0:T(8,128)(2,1)} async-done(((bf16[4,128,768]{2,1,0:T(8,128)(2,1)}), bf16[4,512,768]{2,1,0:T(8,128)(2,1)}) %all-gather.11.cloned.1.call-update) | async-done | bytes 3145744 | tf_op jit(solution)/shard_map/all_gather | solution.py:72
  153.8 5.2 copy-done.1
  162.7 14.6 all-gather.9.cloned.1.call-done
  177.2 4.7 copy.111
  181.9 7.7 fusion.101
  191.9 19.0 multiply_convert_fusion.4
  216.7 11.3 psum.70
  228.0 31.6 %all_gather.19 = bf16[32,8,768]{2,1,0:T(8,128)(2,1)S(1)} all-gather(bf16[4,8,768]{2,1,0:T(8,128)(2,1)} %psum.70), channel_id=1, replica_groups=mesh['batch'=8,'seq'=4] {'batch'}, dimensions={0}, use_global_device_ids=true | all-gather | bytes 442368 | tf_op jit(solution)/shard_map/all_gather | solution.py:304
  267.2 9.1 convert_reduce_fusion
  288.7 8.6 multiply_reduce_fusion.1
  297.3 7.0 multiply_convert_fusion.1
  307.9 4.7 copy.121
  312.9 9.5 fusion.66
  322.4 4.8 copy.123
  327.3 5.1 convert_reduce_fusion.6
  334.2 17.4 reduce-scatter.23.cloned.1.call-done
  353.8 38.3 %reduce-scatter.25.cloned.1.call-done = bf16[4,128,768]{2,1,0:T(8,128)(2,1)} async-done(((bf16[4,512,768]{2,1,0:T(8,128)(2,1)}), bf16[4,128,768]{2,1,0:T(8,128)(2,1)}) %reduce-scatter.25.cloned.1.call-update) | async-done | bytes 786448 | tf_op jit(solution)/shard_map/reduce_scatter | solution.py:217
  394.5 5.5 multiply_reduce_fusion.3
  400.8 8.4 convert_reduce_fusion.1
  417.4 7.6 fusion.69
  425.1 4.8 copy.132
  430.0 8.3 multiply_reduce_fusion
  438.3 7.3 multiply_convert_fusion
  458.4 4.8 convolution_bitcast_fusion.2
  465.9 6.8 pad_maximum_fusion.1
  474.2 5.1 convolution_bitcast_fusion.4
  482.2 7.1 pad_maximum_fusion
  492.5 6.3 convolution_bitcast_fusion
  498.9 5.2 convert_reduce_fusion.9
  515.0 6.3 convolution_bitcast_fusion.1
  521.3 11.0 pad_maximum_fusion.2
  532.3 21.7 %copy.136 = f32[2,768,2304]{2,0,1:T(2,128)} copy(f32[2,768,2304]{1,2,0:T(8,128)} %pad_maximum_fusion.2) | data formatting | bytes 28311552 | tf_op jit(solution)/shard_map/stack | solution.py:346
  554.0 685.5 %all-reduce.7 = bf16[2,768,2304]{2,0,1:T(2,128)(2,1)} all-reduce(f32[2,768,2304]{2,0,1:T(2,128)} %copy.136), channel_id=6, replica_groups=mesh['batch'=8,'seq'=4] {'batch'}, use_global_device_ids=true, to_apply=%region_33.34.clone | all-reduce | flops 3538944 | bytes 21233664
  1248.7 305.6 %reduce-scatter.33.cloned.1.call-done = f32[2,96,3072]{2,1,0:T(8,128)} async-done(((f32[2,768,3072]{2,1,0:T(8,128)}), f32[2,96,3072]{2,1,0:T(8,128)}) %reduce-scatter.33.cloned.1.call-update) | async-done | bytes 2359312 | tf_op jit(solution)/shard_map/reduce_scatter | solution.py:354
  1557.2 60.9 %reduce-scatter.41.cloned.1.call-done = f32[96,2]{1,0:T(8,128)} async-done(((f32[768,2]{1,0:T(8,128)}), f32[96,2]{1,0:T(8,128)}) %reduce-scatter.41.cloned.1.call-update) | async-done | bytes 784
  1618.9 62.9 %reduce-scatter.45.cloned.1.call-done = f32[96,4]{1,0:T(8,128)} async-done(((f32[768,4]{1,0:T(8,128)}), f32[96,4]{1,0:T(8,128)}) %reduce-scatter.45.cloned.1.call-update) | async-done | bytes 1552
  1682.8 62.6 %reduce-scatter.43.cloned.1.call-done = f32[96,4]{1,0:T(8,128)} async-done(((f32[768,4]{1,0:T(8,128)}), f32[96,4]{1,0:T(8,128)}) %reduce-scatter.43.cloned.1.call-update) | async-done | bytes 1552
  1746.4 66.7 %reduce-scatter.39.cloned.1.call-done = f32[384,2]{1,0:T(8,128)} async-done(((f32[3072,2]{1,0:T(8,128)}), f32[384,2]{1,0:T(8,128)}) %reduce-scatter.39.cloned.1.call-update) | async-done | bytes 3088
  1814.1 5.5 fusion.77
  1819.6 57.9 %reduce-scatter.37.cloned.1.call-done = f32[96,6]{1,0:T(8,128)} async-done(((f32[768,6]{1,0:T(8,128)}), f32[96,6]{1,0:T(8,128)}) %reduce-scatter.37.cloned.1.call-update) | async-done | bytes 2320
  1878.5 5.7 all-reduce.1
  1887.1 68.6 %all-reduce.6.cloned.1.call-done = (bf16[2,96,2304]{2,0,1:T(2,128)(2,1)}, bf16[2,96,768]{2,1,0:T(8,128)(2,1)}, bf16[2,96,3072]{2,1,0:T(8,128)(2,1)}, bf16[2,384,768]{2,1,0:T(8,128)(2,1)}) async-done(((bf16[2,96,2304]{2,0,1:T(2,128)(2,1)}, bf16[2,96,768]{2,1,0:T(8,128)(2,1)}, bf16[2,96,3072]{2,1,0:T(8,128)(2,1)}, bf16[2,384,768]{2,1,0:T(8,128)(2,1)}), (bf16[2,96,2304]{2,0,1:T(2,128)(2,1)}, ...) | async-done | bytes 3538960 | tf_op jit(solution)/shard_map/psum | solution.py:362
  (479 shorter events, 157.2 us)
Async XLA Ops:
  7.2 38.8 %all-gather.7.cloned.1.call-start = ((), (), s32[]{:S(2)}) async-start(), calls=%async_computation.13 | async-start | bytes 3932160 | tf_op jit(solution)/shard_map/all_gather | solution.py:72
  14.6 62.1 %all-gather.5.cloned.1.call-start = ((), (), s32[]{:S(2)}) async-start(), calls=%async_computation.12 | async-start | bytes 3932160 | tf_op jit(solution)/shard_map/all_gather | solution.py:73
  18.3 128.3 %all-gather.11.cloned.1.call-start = ((), (), s32[]{:S(2)}) async-start(), calls=%async_computation.15 | async-start | bytes 3932160 | tf_op jit(solution)/shard_map/all_gather | solution.py:72
  22.1 88.1 %copy-start.69 = (f32[768]{0:T(1024)}, f32[768]{0:T(1024)S(1)}, u32[]{:S(2)}) copy-start(f32[768]{0:T(1024)S(1)} %get-tuple-element.158) | copy-start | bytes 9220
  22.1 88.1 %copy-start.96 = (f32[768]{0:T(1024)}, f32[768]{0:T(1024)S(1)}, u32[]{:S(2)}) copy-start(f32[768]{0:T(1024)S(1)} %get-tuple-element.90) | copy-start | bytes 9220
  22.1 168.1 %copy-start.67 = (f32[768]{0:T(1024)}, f32[768]{0:T(1024)S(1)}, u32[]{:S(2)}) copy-start(f32[768]{0:T(1024)S(1)} %get-tuple-element.159) | copy-start | bytes 9220
  22.1 168.1 %copy-start.94 = (f32[768]{0:T(1024)}, f32[768]{0:T(1024)S(1)}, u32[]{:S(2)}) copy-start(f32[768]{0:T(1024)S(1)} %get-tuple-element.89) | copy-start | bytes 9220
  22.1 188.7 %copy-start.71 = (f32[768]{0:T(1024)}, f32[768]{0:T(1024)S(1)}, u32[]{:S(2)}) copy-start(f32[768]{0:T(1024)S(1)} %get-tuple-element.157) | copy-start | bytes 9220
  22.4 68.9 %copy-start.81 = (f32[1,3072]{1,0:T(1,128)}, f32[1,3072]{1,0:T(1,128)S(1)}, u32[]{:S(2)}) copy-start(f32[1,3072]{1,0:T(1,128)S(1)} %get-tuple-element.124) | copy-start | bytes 36868
  22.4 169.4 %copy-start.83 = (f32[1,3072]{1,0:T(1,128)}, f32[1,3072]{1,0:T(1,128)S(1)}, u32[]{:S(2)}) copy-start(f32[1,3072]{1,0:T(1,128)S(1)} %get-tuple-element.123) | copy-start | bytes 36868
  53.6 26.4 %copy-start.46 = (f32[4,12,128]{2,1,0:T(8,128)}, f32[4,12,128]{2,1,0:T(8,128)S(1)}, u32[]{:S(2)}) copy-start(f32[4,12,128]{2,1,0:T(8,128)S(1)} %get-tuple-element.125) | copy-start | bytes 73732
  62.4 26.9 %copy-start.49 = (f32[4,12,128]{2,1,0:T(8,128)}, f32[4,12,128]{2,1,0:T(8,128)S(1)}, u32[]{:S(2)}) copy-start(f32[4,12,128]{2,1,0:T(8,128)S(1)} %fusion) | copy-start | bytes 73732
  90.0 20.3 %slice-start = ((s8[9437184]{0:T(1024)(128)(4,1)}), s8[4194304]{0:T(1024)(128)(4,1)S(1)}, s32[]{:S(2)}) async-start(s8[9437184]{0:T(1024)(128)(4,1)} %bitcast.308), calls=%async_computation.29 | async-start | bytes 8388608
  90.0 23.4 %slice-start.21 = ((s8[7077888]{0:T(1024)(128)(4,1)}), s8[4194304]{0:T(1024)(128)(4,1)S(1)}, s32[]{:S(2)}) async-start(s8[7077888]{0:T(1024)(128)(4,1)} %bitcast.322), calls=%async_computation.50 | async-start | bytes 8388608
  90.9 19.3 copy-start.20
  91.4 22.1 %slice-start.22 = ((s8[7077888]{0:T(1024)(128)(4,1)}), s8[2883584]{0:T(1024)(128)(4,1)S(1)}, s32[]{:S(2)}) async-start(s8[7077888]{0:T(1024)(128)(4,1)} %bitcast.322), calls=%async_computation.51 | async-start | bytes 5767168
  113.1 77.2 %copy-start.60 = (f32[512]{0:T(512)}, f32[512]{0:T(512)S(1)}, u32[]{:S(2)}) copy-start(f32[512]{0:T(512)S(1)} %broadcast_multiply_fusion.9) | copy-start | bytes 6148
  113.4 76.9 %copy-start.85 = (f32[512]{0:T(512)}, f32[512]{0:T(512)S(1)}, u32[]{:S(2)}) copy-start(f32[512]{0:T(512)S(1)} %add_rsqrt_fusion.2) | copy-start | bytes 6148
  118.0 59.2 %all-gather.9.cloned.1.call-start = ((), (), s32[]{:S(2)}) async-start(), calls=%async_computation.14 | async-start | bytes 3932160 | tf_op jit(solution)/shard_map/all_gather | solution.py:73
  121.0 230.5 %reduce-scatter.23.cloned.1.call-start = ((), (), s32[]{:S(2)}) async-start(), calls=%async_computation.16 | async-start | bytes 3932160 | tf_op jit(solution)/shard_map/reduce_scatter | solution.py:211
  121.1 95.0 %copy-start.104 = (s32[128]{0:T(128)}, s32[128]{0:T(128)S(1)}, u32[]{:S(2)}) copy-start(s32[128]{0:T(128)S(1)} %iota_add_fusion) | copy-start | bytes 1540
  190.3 20.5 %slice-start.3 = ((s8[9437184]{0:T(1024)(128)(4,1)}), s8[4194304]{0:T(1024)(128)(4,1)S(1)}, s32[]{:S(2)}) async-start(s8[9437184]{0:T(1024)(128)(4,1)} %bitcast.310), calls=%async_computation.32 | async-start | bytes 8388608
  191.4 19.4 copy-start.23
  191.5 19.4 copy-start.64
  213.7 46.1 %copy-start.93 = (s32[128]{0:T(128)S(1)}, s32[128]{0:T(128)}, u32[]{:S(2)}) copy-start(s32[128]{0:T(128)} %param.15) | copy-start | bytes 1540
  213.8 47.0 %copy-start.53 = (f32[512]{0:T(512)}, f32[512]{0:T(512)S(1)}, u32[]{:S(2)}) copy-start(f32[512]{0:T(512)S(1)} %broadcast_multiply_fusion.7) | copy-start | bytes 6148
  214.1 46.7 %copy-start.57 = (f32[512]{0:T(512)}, f32[512]{0:T(512)S(1)}, u32[]{:S(2)}) copy-start(f32[512]{0:T(512)S(1)} %add_rsqrt_fusion) | copy-start | bytes 6148
  228.0 33.2 %copy-start.45 = (bf16[4,128,768]{2,1,0:T(8,128)(2,1)S(1)}, bf16[4,128,768]{2,1,0:T(8,128)(2,1)}, u32[]{:S(2)}) copy-start(bf16[4,128,768]{2,1,0:T(8,128)(2,1)} %param.25) | copy-start | bytes 2359300
  228.0 33.2 %copy-start.105 = (s32[128]{0:T(128)S(1)}, s32[128]{0:T(128)}, u32[]{:S(2)}) copy-start(s32[128]{0:T(128)} %copy-done.104) | copy-start | bytes 1540
  228.0 36.0 %copy-start.7 = (f32[512,768]{1,0:T(8,128)S(1)}, f32[512,768]{1,0:T(8,128)}, u32[]{:S(2)}) copy-start(f32[512,768]{1,0:T(8,128)} %copy-done.6) | copy-start | bytes 4718596
  312.6 79.5 %reduce-scatter.25.cloned.1.call-start = ((), (), s32[]{:S(2)}) async-start(), calls=%async_computation.17 | async-start | bytes 3932160 | tf_op jit(solution)/shard_map/reduce_scatter | solution.py:217
  327.2 183.6 %reduce-scatter.29.cloned.1.call-start = ((), (), s32[]{:S(2)}) async-start(), calls=%async_computation.19 | async-start | bytes 3932160 | tf_op jit(solution)/shard_map/reduce_scatter | solution.py:217
  332.5 61.9 %copy-start.18 = (f32[512,768]{1,0:T(8,128)S(1)}, f32[512,768]{1,0:T(8,128)}, u32[]{:S(2)}) copy-start(f32[512,768]{1,0:T(8,128)} %copy-done.16) | copy-start | bytes 4718596
  332.5 61.9 %copy-start.30 = (f32[512,768]{1,0:T(8,128)S(1)}, f32[512,768]{1,0:T(8,128)}, u32[]{:S(2)}) copy-start(f32[512,768]{1,0:T(8,128)} %copy-done.29) | copy-start | bytes 4718596
  332.5 61.9 %copy-start.61 = (f32[512]{0:T(512)S(1)}, f32[512]{0:T(512)}, u32[]{:S(2)}) copy-start(f32[512]{0:T(512)} %copy-done.60) | copy-start | bytes 6148
  332.5 61.9 %copy-start.68 = (f32[768]{0:T(1024)S(1)}, f32[768]{0:T(1024)}, u32[]{:S(2)}) copy-start(f32[768]{0:T(1024)} %copy-done.67) | copy-start | bytes 9220
  332.5 61.9 %copy-start.86 = (f32[512]{0:T(512)S(1)}, f32[512]{0:T(512)}, u32[]{:S(2)}) copy-start(f32[512]{0:T(512)} %copy-done.85) | copy-start | bytes 6148
  429.9 82.2 %reduce-scatter.27.cloned.1.call-start = ((), (), s32[]{:S(2)}) async-start(), calls=%async_computation.18 | async-start | bytes 3932160 | tf_op jit(solution)/shard_map/reduce_scatter | solution.py:211
  451.1 792.9 %reduce-scatter.31.cloned.1.call-start = ((), (), s32[]{:S(2)}) async-start(), calls=%async_computation.20 | async-start | bytes 5308416 | tf_op jit(solution)/shard_map/reduce_scatter | solution.py:353
  457.0 788.8 %reduce-scatter.35.cloned.1.call-start = ((), (), s32[]{:S(2)}) async-start(), calls=%async_computation.22 | async-start | bytes 21233664 | tf_op jit(solution)/shard_map/reduce_scatter | solution.py:356
  472.8 1081.5 %reduce-scatter.33.cloned.1.call-start = ((), (), s32[]{:S(2)}) async-start(), calls=%async_computation.21 | async-start | bytes 21233664 | tf_op jit(solution)/shard_map/reduce_scatter | solution.py:354
  489.4 1128.6 %reduce-scatter.41.cloned.1.call-start = ((), (), s32[]{:S(2)}) async-start(), calls=%async_computation.25 | async-start | bytes 442368
  504.1 1177.7 %reduce-scatter.45.cloned.1.call-start = ((), (), s32[]{:S(2)}) async-start(), calls=%async_computation.27 | async-start | bytes 442368
  505.9 1239.5 %reduce-scatter.43.cloned.1.call-start = ((), (), s32[]{:S(2)}) async-start(), calls=%async_computation.26 | async-start | bytes 442368
  507.7 1305.4 %reduce-scatter.39.cloned.1.call-start = ((), (), s32[]{:S(2)}) async-start(), calls=%async_computation.24 | async-start | bytes 1769472
  510.8 1366.8 %reduce-scatter.37.cloned.1.call-start = ((), (), s32[]{:S(2)}) async-start(), calls=%async_computation.23 | async-start | bytes 442368
  1241.2 714.5 %all-reduce.6.cloned.1.call-start = ((), (), s32[]{:S(2)}) async-start(), calls=%async_computation.28 | async-start | bytes 7077888 | tf_op jit(solution)/shard_map/psum | solution.py:362
  1245.8 568.3 %copy-start.28 = (f32[512,768]{1,0:T(8,128)S(1)}, f32[512,768]{1,0:T(8,128)}, u32[]{:S(2)}) copy-start(f32[512,768]{1,0:T(8,128)} %copy-done.26) | copy-start | bytes 4718596
  (109 other events, 713.8 us)
Sparse Core Ops, SparseCore 0:
  14.7 31.2 all-gather.6
  48.1 28.5 all-gather.4
  118.1 28.5 all-gather.10
  148.6 28.5 all-gather.8
  312.7 38.7 reduce-scatter.22
  354.1 37.9 reduce-scatter.24
  430.0 37.9 reduce-scatter.28
  470.7 37.9 reduce-scatter.26
  512.4 146.5 reduce-scatter.30
  662.6 576.5 reduce-scatter.34
  1243.1 311.1 reduce-scatter.32
  1557.5 60.5 reduce-scatter.40
  1621.3 60.4 reduce-scatter.44
  1684.9 60.4 reduce-scatter.42
  1749.2 63.8 reduce-scatter.38
  1817.1 60.3 reduce-scatter.36
  1881.3 74.4 all-reduce.5
where the time goes:
time: 1980 us; the launch traced here: 1970 us
  waiting for transfers between devices  818 us (41%)
  blocking collectives  734 us (37%)
  matrix products  198 us (10%)
  local copies, waits for them, and re-layouts  120 us (6%)
  other arithmetic  82.2 us (4%)
    unnamed x1, blocking collectives  685 us
    unnamed x22, waiting for transfers between devices  311 us
    reduce_scatter x1, waiting for transfers between devices, body(): lax.psum_scatter(stacked[3], 'batch', scatter_dimension=1, tiled=True)  306 us
    psum x1, waiting for transfers between devices, body(): lax.psum(shares[0].astype(jnp.bfloat16), 'seq').astype(jnp.float32)  68.6 us
    all_gather x2, waiting for transfers between devices, forward_layer(): lax.all_gather(key_block.reshape(shape_rows), 'seq', axis=1, tiled=True)  47.7 us
    unnamed x301, local copies, waits for them, and re-layouts  41.6 us
  transfers between devices with their start and end apart: 17, of which 13 were waited for; matrix products, arithmetic and copies ran while one was open for 10% of the time, Pallas kernels for 0%

commit v1 on v0

v1 whole, which is shorter than its diff:
```python
from functools import partial

import jax
import jax.numpy as jnp
from jax import lax
from jax.experimental import pallas as pl
from jax.experimental.pallas import tpu as pltpu
from jax.sharding import PartitionSpec as P

HEADS = 12
HEAD_DIM = 64
PAIR = 2 * HEAD_DIM

EPSILON = 1e-12
NEGATIVE = -1e30
CONTRAST_WEIGHT = 16.0
SCORE_SCALE = 0.125
MIB = 1024 * 1024
VMEM = {
    "attention_forward": 24,
    "shrink_backward": 63,
    "expand_backward": 63,
    "joint_backward": 63,
    "add_blocks": 63,
    "assemble": 56,
    "contrast_part": 56,
}


def cost(microseconds):
    return pl.CostEstimate(
        flops=int(microseconds * 1e9), bytes_accessed=int(microseconds * 2e6), transcendentals=0
    )


GROUPS = (
    ((1, "shrink"), (1, "expand"), (1, "joint")),
    ((0, "shrink"), (0, "expand")),
    ((0, "joint"),),
)

NT = (((1,), (1,)), ((), ()))
TN = (((0,), (0,)), ((), ()))


def dot(a, b, dims=(((1,), (0,)), ((), ()))):
    return lax.dot_general(a, b, dims, preferred_element_type=jnp.float32)


def attention_forward_kernel(step, qkv_ref, column_ids_ref, row_ids_ref, out_ref, lse_ref):
    full_len = qkv_ref.shape[0]
    width = out_ref.shape[1]

    def pair(h, carry):
        offset = pl.multiple_of(h * PAIR, PAIR)
        k = qkv_ref[:, pl.ds(width + offset, PAIR)]
        v_turned = qkv_ref[:, pl.ds(2 * width + offset, PAIR)].T
        for i in range(full_len // step):
            rows = slice(i * step, (i + 1) * step)
            q = qkv_ref[rows, pl.ds(offset, PAIR)]
            q = (q.astype(jnp.float32) * SCORE_SCALE).astype(jnp.bfloat16)
            allowed = column_ids_ref[...] == row_ids_ref[:, rows]
            mixed = []
            for a in range(2):
                cols = slice(a * HEAD_DIM, (a + 1) * HEAD_DIM)
                scores = jnp.where(allowed, dot(k[:, cols], q[:, cols], NT), NEGATIVE)
                peak = jnp.max(scores, axis=0, keepdims=True)
                exponent = jnp.exp(scores - peak)
                summed = jnp.sum(exponent, axis=0, keepdims=True)
                mixed.append(dot(v_turned[cols, :], exponent.astype(jnp.bfloat16)) * (1.0 / summed))
                lse_ref[h, a : a + 1, rows] = peak + jnp.log(summed)
            turned = jnp.concatenate(mixed, axis=0).T
            out_ref[rows, pl.ds(offset, PAIR)] = turned.astype(jnp.bfloat16)
        return carry

    lax.fori_loop(0, width // PAIR, pair, 0)


def attention_forward(qkv, column_ids, row_ids, step):
    full_len = qkv.shape[0]
    width = qkv.shape[1] // 3
    pairs = width // PAIR
    return pl.pallas_call(
        partial(attention_forward_kernel, step),
        out_shape=(
            jax.ShapeDtypeStruct((full_len, width), jnp.bfloat16),
            jax.ShapeDtypeStruct((pairs, 8, full_len), jnp.float32),
        ),
        compiler_params=pltpu.CompilerParams(vmem_limit_bytes=VMEM["attention_forward"] * MIB),
        cost_estimate=cost(8),
    )(qkv, column_ids, row_ids)


def norm_back(grad_out, normed, factor, gain):
    scaled = grad_out * gain
    return factor * (
        scaled
        - jnp.mean(scaled, axis=-1, keepdims=True)
        - normed * jnp.mean(scaled * normed, axis=-1, keepdims=True)
    )


def as_column(row_ref):
    return jnp.broadcast_to(row_ref[...], (128, row_ref.shape[1])).T[:, 0:1]


def store_sums(sums_ref, row, array):
    sums_ref[row : row + 1, :] = jnp.sum(array, axis=0, keepdims=True)


def shrink_backward_kernel(
    shard_columns, bit_ref, grad_ref, normed_ref, factor_ref, gain_ref, active_ref,
    send_ref, keep_ref, sum_grad_ref, low_ref, sums_ref, turned,
):
    @pl.when(pl.program_id(0) == 0)
    def _():
        grad = grad_ref[...]
        normed = normed_ref[...]
        sum_grad = norm_back(grad, normed, as_column(factor_ref), gain_ref[...])
        low = sum_grad.astype(jnp.bfloat16)
        sum_grad_ref[...] = sum_grad
        low_ref[...] = low
        turned[...] = low.T
        sums_ref[...] = jnp.zeros_like(sums_ref)
        store_sums(sums_ref, 0, grad * normed)
        store_sums(sums_ref, 1, grad)
        store_sums(sums_ref, 2, low.astype(jnp.float32))

    half = turned.shape[0] // 2
    bit = bit_ref[0]
    for which, out_ref in ((1 - bit, send_ref), (bit, keep_ref)):
        rows = turned[pl.ds(pl.multiple_of(which * half, half), half), :]
        product = dot(rows, active_ref[...]).astype(jnp.bfloat16)
        if out_ref.shape == product.shape:
            out_ref[...] = product
            continue
        blocks = out_ref.shape[1] // shard_columns
        size = half // blocks
        for shard in range(product.shape[1] // shard_columns):
            columns = slice(shard * shard_columns, (shard + 1) * shard_columns)
            for j in range(blocks):
                out_ref[
                    shard * size : (shard + 1) * size, j * shard_columns : (j + 1) * shard_columns
                ] = product[j * size : (j + 1) * size, columns]


def shrink_backward(bit, grad, normed, factor, gain, active, shards):
    count, width = grad.shape
    inner = active.shape[1]
    steps = inner // width
    shard_columns = inner // shards
    aligned = shard_columns % 128 == 0
    tall, wide = (width, inner // 2) if aligned else (width // 2, inner)
    out_spec = (
        pl.BlockSpec((width // steps, inner // 2), lambda i, bit_ref: (i, 0))
        if aligned
        else pl.BlockSpec((width // 2, width), lambda i, bit_ref: (0, i))
    )

    def whole(*shape):
        return pl.BlockSpec(shape, lambda i, bit_ref: (0, 0))

    send, keep, *others = pl.pallas_call(
        partial(shrink_backward_kernel, shard_columns),
        grid_spec=pltpu.PrefetchScalarGridSpec(
            num_scalar_prefetch=1,
            grid=(steps,),
            in_specs=[
                whole(count, width), whole(count, width), whole(1, count), whole(1, width),
                pl.BlockSpec((count, width), lambda i, bit_ref: (0, i)),
            ],
            out_specs=[
                out_spec, out_spec, whole(count, width), whole(count, width), whole(8, width),
            ],
            scratch_shapes=[pltpu.VMEM((width, count), jnp.bfloat16)],
        ),
        out_shape=[
            jax.ShapeDtypeStruct((tall, wide), jnp.bfloat16),
            jax.ShapeDtypeStruct((tall, wide), jnp.bfloat16),
            jax.ShapeDtypeStruct((count, width), jnp.float32),
            jax.ShapeDtypeStruct((count, width), jnp.bfloat16),
            jax.ShapeDtypeStruct((8, width), jnp.float32),
        ],
        compiler_params=pltpu.CompilerParams(vmem_limit_bytes=VMEM["shrink_backward"] * MIB),
        cost_estimate=cost(6),
    )(bit, grad, normed, factor, gain, active)
    if not aligned:
        shape = (width // 2, shards, shard_columns)
        send, keep = (
            x.reshape(shape).transpose(1, 0, 2).reshape(width, inner // 2) for x in (send, keep)
        )
    return send, keep, *others


def shrink_share(x, shard_columns):
    if shard_columns % 128:
        return x.reshape(-1, shard_columns).T
    size, wide = x.shape
    blocks = wide // shard_columns
    return x.reshape(size, blocks, shard_columns).transpose(2, 1, 0).reshape(shard_columns, -1)


def expand_backward_kernel(
    steps, level, bit_ref, low_ref, sum_grad_ref, slope_ref, middle_ref, shrink_ref, expand_ref,
    normed_ref, factor_ref, gain_ref, mix_ref,
    send_ref, keep_ref, hidden_grad_ref, branch_ref, mixed_grad_ref, sums_ref,
    middle_turned, total, normed_held, sum_grad_held, mix_held, arrived,
):
    step = pl.program_id(0)
    bit = bit_ref[0]
    per_half = steps // 2
    late = (
        pltpu.make_async_copy(normed_ref, normed_held, arrived.at[0]),
        pltpu.make_async_copy(sum_grad_ref, sum_grad_held, arrived.at[1]),
        pltpu.make_async_copy(mix_ref.at[level], mix_held, arrived.at[2]),
    )

    @pl.when(step == 0)
    def _():
        for copy in late:
            copy.start()
        middle_turned[...] = middle_ref[...].T
        total[...] = jnp.zeros_like(total)
        sums_ref[...] = jnp.zeros_like(sums_ref)

    active_grad = dot(low_ref[...], shrink_ref[...], NT)
    expanded = (slope_ref[...].astype(jnp.float32) * active_grad).astype(jnp.bfloat16)
    tile = jnp.where(step < per_half, 1 - bit, bit) * per_half + lax.rem(step, per_half)
    sums_ref[pl.ds(3 + tile, 1), :] = jnp.sum(expanded.astype(jnp.float32), axis=0, keepdims=True)
    weight_grad = dot(middle_turned[...], expanded).astype(jnp.bfloat16)

    @pl.when(step < per_half)
    def _():
        send_ref[...] = weight_grad

    @pl.when(step >= per_half)
    def _():
        keep_ref[...] = weight_grad

    total[...] += dot(expanded, expand_ref[...], NT)

    @pl.when(step == steps - 1)
    def _():
        for copy in late:
            copy.wait()
        grad = total[...] + sum_grad_held[...]
        normed = normed_held[...]
        hidden_grad = norm_back(grad, normed, as_column(factor_ref), gain_ref[...])
        branch = hidden_grad.astype(jnp.bfloat16)
        hidden_grad_ref[...] = hidden_grad
        branch_ref[...] = branch
        store_sums(sums_ref, 0, grad * normed)
        store_sums(sums_ref, 1, grad)
        store_sums(sums_ref, 2, branch.astype(jnp.float32))
        mixed_grad_ref[...] = dot(branch, mix_held[...], NT).astype(jnp.bfloat16)


def expand_backward(
    bit, low, sum_grad, slope, middle, shrink_w, expand_w, normed, factor, gain, mix_w, level
):
    count, width = low.shape
    inner = slope.shape[1]
    steps = inner // width
    per_half = steps // 2

    def whole(*shape):
        return pl.BlockSpec(shape, lambda i, bit_ref: (0, 0))

    anywhere = pl.BlockSpec(memory_space=pl.ANY)

    def tile(i, bit_ref):
        bit = bit_ref[0]
        return jnp.where(i < per_half, 1 - bit, bit) * per_half + lax.rem(i, per_half)

    return pl.pallas_call(
        partial(expand_backward_kernel, steps, level),
        grid_spec=pltpu.PrefetchScalarGridSpec(
            num_scalar_prefetch=1,
            grid=(steps,),
            in_specs=[
                whole(count, width), anywhere,
                pl.BlockSpec((count, width), lambda i, b: (0, tile(i, b))),
                whole(count, width),
                pl.BlockSpec((None, width, width), lambda i, b: (level, tile(i, b), 0)),
                pl.BlockSpec((None, width, width), lambda i, b: (level, 0, tile(i, b))),
                anywhere, whole(1, count), whole(1, width), anywhere,
            ],
            out_specs=[
                pl.BlockSpec((width, width), lambda i, b: (0, jnp.minimum(i, per_half - 1))),
                pl.BlockSpec((width, width), lambda i, b: (0, jnp.maximum(i - per_half, 0))),
                whole(count, width), whole(count, width), whole(count, width), whole(8, width),
            ],
            scratch_shapes=[
                pltpu.VMEM((width, count), jnp.bfloat16),
                pltpu.VMEM((count, width), jnp.float32),
                pltpu.VMEM((count, width), jnp.float32),
                pltpu.VMEM((count, width), jnp.float32),
                pltpu.VMEM((width, width), jnp.bfloat16),
                pltpu.SemaphoreType.DMA((3,)),
            ],
        ),
        out_shape=[
            jax.ShapeDtypeStruct((width, inner // 2), jnp.bfloat16),
            jax.ShapeDtypeStruct((width, inner // 2), jnp.bfloat16),
            jax.ShapeDtypeStruct((count, width), jnp.float32),
            jax.ShapeDtypeStruct((count, width), jnp.bfloat16),
            jax.ShapeDtypeStruct((count, width), jnp.bfloat16),
            jax.ShapeDtypeStruct((8, width), jnp.float32),
        ],
        compiler_params=pltpu.CompilerParams(vmem_limit_bytes=VMEM["expand_backward"] * MIB),
        cost_estimate=cost(16),
    )(bit, low, sum_grad, slope, middle, shrink_w, expand_w, normed, factor, gain, mix_w)


def fetch_all(pairs, semaphores):
    copies = [
        pltpu.make_async_copy(source, target, semaphores.at[i])
        for i, (source, target) in enumerate(pairs)
    ]
    for copy in copies:
        copy.start()
    return copies


def joint_half(half, hidden_ref, mixed_ref, joint_ref, branch_ref, out_ref):
    joint_size, mix_size = joint_ref.shape[1] // 2, branch_ref.shape[1] // 2
    joint = joint_ref[:, pl.ds(pl.multiple_of(half * joint_size, 128), joint_size)]
    branch = branch_ref[:, pl.ds(pl.multiple_of(half * mix_size, 128), mix_size)]
    out_ref[:, :joint_size] = dot(hidden_ref[...].T, joint).astype(jnp.bfloat16)
    out_ref[:, joint_size:] = dot(mixed_ref[...].T, branch).astype(jnp.bfloat16)


def attention_backward_kernel(
    half_ref, lse_ref, column_ids_ref, row_ids_ref, qkv_any, grad_any, mixed_any, hidden_any,
    branch_any, joint_any, half_any, sums_ref,
    qkv_ref, grad_ref, mixed_ref, hidden_ref, branch_ref, joint_ref, out_ref, arrived, left,
):
    fetches = fetch_all(
        (
            (qkv_any, qkv_ref), (grad_any, grad_ref), (mixed_any, mixed_ref),
            (hidden_any, hidden_ref), (branch_any, branch_ref),
        ),
        arrived,
    )
    for fetch in fetches[:3]:
        fetch.wait()
    width = mixed_ref.shape[1]
    lane = lax.broadcasted_iota(jnp.int32, (8, PAIR), 1) // HEAD_DIM
    picker = (lane == lax.broadcasted_iota(jnp.int32, (8, PAIR), 0)).astype(jnp.float32)
    allowed = column_ids_ref[...] == row_ids_ref[...]

    def pair(h, carry):
        offset = pl.multiple_of(h * PAIR, PAIR)
        q = qkv_ref[:, pl.ds(offset, PAIR)]
        k = qkv_ref[:, pl.ds(width + offset, PAIR)]
        v = qkv_ref[:, pl.ds(2 * width + offset, PAIR)]
        grad = grad_ref[:, pl.ds(offset, PAIR)]
        mixed = mixed_ref[:, pl.ds(offset, PAIR)]
        product = grad.astype(jnp.float32) * mixed.astype(jnp.float32)
        centres = lax.dot_general(
            picker, product, NT, precision=lax.Precision.HIGHEST,
            preferred_element_type=jnp.float32,
        )
        q = (q.astype(jnp.float32) * SCORE_SCALE).astype(jnp.bfloat16)
        query_parts, key_parts, value_parts = [], [], []
        for a in range(2):
            cols = slice(a * HEAD_DIM, (a + 1) * HEAD_DIM)
            scores = jnp.where(allowed, dot(k[:, cols], q[:, cols], NT), NEGATIVE)
            probability = jnp.exp(scores - lse_ref[h, a : a + 1, :])
            prob_grad = dot(v[:, cols], grad[:, cols], NT)
            score_low = (probability * (prob_grad - centres[a : a + 1, :])).astype(jnp.bfloat16)
            value_parts.append(dot(probability.astype(jnp.bfloat16), grad[:, cols]))
            key_parts.append(dot(score_low, q[:, cols]))
            query_parts.append(dot(k[:, cols], score_low, TN))
        turned = jnp.concatenate(query_parts, axis=0) * SCORE_SCALE
        for place, part in (
            (0, turned.T),
            (width, jnp.concatenate(key_parts, axis=1)),
            (2 * width, jnp.concatenate(value_parts, axis=1)),
        ):
            joint_ref[:, pl.ds(place + offset, PAIR)] = part.astype(jnp.bfloat16)
        return carry

    lax.fori_loop(0, width // PAIR, pair, 0)
    store_joint = pltpu.make_async_copy(joint_ref, joint_any, left.at[0])
    store_joint.start()
    for fetch in fetches[3:]:
        fetch.wait()
    joint_half(half_ref[0], hidden_ref, mixed_ref, joint_ref, branch_ref, out_ref)
    store_half = pltpu.make_async_copy(out_ref, half_any, left.at[1])
    store_half.start()
    sums_ref[...] = jnp.zeros_like(sums_ref)
    store_sums(sums_ref, 0, joint_ref[:, :width].astype(jnp.float32))
    store_sums(sums_ref, 1, joint_ref[:, 2 * width :].astype(jnp.float32))
    store_joint.wait()
    store_half.wait()


def attention_backward(half, lse, column_ids, row_ids, qkv, grad, mixed, hidden, branch):
    count, width = hidden.shape

    def whole(shape):
        return pl.BlockSpec(shape, lambda i, half_ref: (0,) * len(shape))

    anywhere = pl.BlockSpec(memory_space=pl.ANY)
    return pl.pallas_call(
        attention_backward_kernel,
        grid_spec=pltpu.PrefetchScalarGridSpec(
            num_scalar_prefetch=1,
            grid=(1,),
            in_specs=[whole(lse.shape), whole(column_ids.shape), whole(row_ids.shape)]
            + [anywhere] * 5,
            out_specs=[anywhere] * 2 + [whole((8, width))],
            scratch_shapes=[
                pltpu.VMEM(x.shape, x.dtype) for x in (qkv, grad, mixed, hidden, branch, qkv)
            ]
            + [
                pltpu.VMEM((width, 2 * width), jnp.bfloat16),
                pltpu.SemaphoreType.DMA((5,)),
                pltpu.SemaphoreType.DMA((2,)),
            ],
        ),
        out_shape=[
            low_shape(count, 3 * width),
            low_shape(width, 2 * width),
            jax.ShapeDtypeStruct((8, width), jnp.float32),
        ],
        compiler_params=pltpu.CompilerParams(vmem_limit_bytes=VMEM["joint_backward"] * MIB),
        cost_estimate=cost(14),
    )(half, lse, column_ids, row_ids, qkv, grad, mixed, hidden, branch)


def joint_backward_kernel(
    level, half_ref, mixed_any, hidden_any, joint_any, branch_any, weight_any, hidden_grad_any,
    half_any, out_any,
    mixed_ref, hidden_ref, joint_ref, branch_ref, weight_ref, hidden_grad_ref, part_ref, out_ref,
    arrived, left,
):
    fetches = fetch_all(
        (
            (hidden_any, hidden_ref), (mixed_any, mixed_ref), (joint_any, joint_ref),
            (branch_any, branch_ref), (weight_any.at[level], weight_ref),
            (hidden_grad_any, hidden_grad_ref),
        ),
        arrived,
    )
    for fetch in fetches[:4]:
        fetch.wait()
    joint_half(half_ref[0], hidden_ref, mixed_ref, joint_ref, branch_ref, part_ref)
    store_half = pltpu.make_async_copy(part_ref, half_any, left.at[0])
    store_half.start()
    for fetch in fetches[4:]:
        fetch.wait()
    out_ref[...] = (hidden_grad_ref[...] + dot(joint_ref[...], weight_ref[...], NT)).astype(
        out_ref.dtype
    )
    store_out = pltpu.make_async_copy(out_ref, out_any, left.at[1])
    store_out.start()
    store_half.wait()
    store_out.wait()


def joint_backward(half, mixed, hidden, joint, branch, weight, hidden_grad, level, dtype):
    count, width = hidden.shape
    anywhere = pl.BlockSpec(memory_space=pl.ANY)
    return pl.pallas_call(
        partial(joint_backward_kernel, level),
        grid_spec=pltpu.PrefetchScalarGridSpec(
            num_scalar_prefetch=1,
            grid=(1,),
            in_specs=[anywhere] * 6,
            out_specs=[anywhere] * 2,
            scratch_shapes=[
                pltpu.VMEM(x.shape, x.dtype) for x in (mixed, hidden, joint, branch)
            ]
            + [
                pltpu.VMEM(weight.shape[1:], jnp.bfloat16),
                pltpu.VMEM((count, width), jnp.float32),
                pltpu.VMEM((width, 2 * width), jnp.bfloat16),
                pltpu.VMEM((count, width), dtype),
                pltpu.SemaphoreType.DMA((6,)),
                pltpu.SemaphoreType.DMA((2,)),
            ],
        ),
        out_shape=[low_shape(width, 2 * width), jax.ShapeDtypeStruct((count, width), dtype)],
        compiler_params=pltpu.CompilerParams(vmem_limit_bytes=VMEM["joint_backward"] * MIB),
        cost_estimate=cost(7),
    )(half, mixed, hidden, joint, branch, weight, hidden_grad)


def normalize(hidden):
    centred = hidden - jnp.mean(hidden, axis=-1, keepdims=True)
    spread = jnp.mean(centred * centred, axis=-1, keepdims=True)
    factor = lax.rsqrt(spread + EPSILON)
    return (centred * factor, factor.reshape(1, -1))


def gelu_parts(z):
    phi = 0.5 * (1.0 + lax.erf(z * (0.5**0.5)))
    density = jnp.exp(-0.5 * z * z) * 0.3989422804014327
    return (z * phi, phi + z * density)


def forward_layer(hidden, weights, column_ids, row_ids, step):
    joint_w, bias_rows, mix_w, expand_w, expand_b, shrink_w, shrink_b, gain, shift = weights
    hidden_low = hidden.astype(jnp.bfloat16)
    joint_bias = jnp.concatenate([bias_rows[0], jnp.zeros_like(bias_rows[0]), bias_rows[1]])
    qkv = (dot(hidden_low, joint_w) + joint_bias).astype(jnp.bfloat16)
    mixed, lse = attention_forward(qkv, column_ids, row_ids, step)
    branch = dot(mixed, mix_w) + bias_rows[2]
    normed_one, factor_one = normalize(hidden + branch)
    middle = normed_one * gain[0] + shift[0]
    middle_low = middle.astype(jnp.bfloat16)
    active, slope = gelu_parts(dot(middle_low, expand_w) + expand_b)
    active_low = active.astype(jnp.bfloat16)
    slope = slope.astype(jnp.bfloat16)
    shrunk = dot(active_low, shrink_w) + shrink_b
    normed_two, factor_two = normalize(middle + shrunk)
    result = normed_two * gain[1] + shift[1]
    kept = (
        hidden_low, qkv, lse, mixed, normed_one, factor_one, middle_low, active_low, slope,
        normed_two, factor_two,
    )
    return (result, kept)


def backward_layer(grad, kept, params, column_ids, row_ids, flow, level):
    qkv_weight, out_weight, ffn_in, ffn_out, norm_gain = params
    (
        hidden_low, qkv, lse, mixed, normed_one, factor_one, middle_low, active_low, slope,
        normed_two, factor_two,
    ) = kept
    bit = own_bit("seq", 0).reshape(1)
    send, keep, sum_grad, shrunk_low, sums_two = shrink_backward(
        bit, grad, normed_two, factor_two, norm_gain[level, 1:2], active_low,
        lax.axis_size("batch"),
    )
    shrunk_low, send, keep = flow.tick((shrunk_low, send, keep))
    shrink_keep = keep
    flow.begin((level, "shrink"), reduce_first(send, lambda: shrink_keep, level == 0))
    send, keep, hidden_grad, branch_low, mixed_grad, sums_one = expand_backward(
        bit, shrunk_low, sum_grad, slope, middle_low, ffn_out, ffn_in, normed_one, factor_one,
        norm_gain[level, 0:1], out_weight, level,
    )
    mixed_grad, send, keep = flow.tick((mixed_grad, send, keep))
    expand_keep = keep
    flow.begin((level, "expand"), reduce_first(send, lambda: expand_keep, level == 0))
    joint_low, send, sums_zero = attention_backward(
        1 - bit, lse, column_ids, row_ids, qkv, mixed_grad, mixed, hidden_low, branch_low
    )
    joint_low, send = flow.tick((joint_low, send))
    own_half = Later()
    flow.begin((level, "joint"), reduce_first(send, own_half.get, level == 0))
    own_half.value, input_grad = joint_backward(
        bit, mixed, hidden_low, joint_low, branch_low, qkv_weight, hidden_grad, level,
        jnp.float32 if level else jnp.bfloat16,
    )
    return input_grad, jnp.concatenate([sums_two, sums_one, sums_zero])


def flip(x, axis, bit):
    count = lax.axis_size(axis)
    return lax.ppermute(x, axis, [(i, i ^ (1 << bit)) for i in range(count)])


def own_bit(axis, bit):
    return (lax.axis_index(axis) >> bit) & 1


def add_low(a, b):
    return a + b


def bits_of(axis):
    return (lax.axis_size(axis) - 1).bit_length()


def exchange_rows(pieces):
    count = lax.axis_size("seq")
    own = lax.axis_index("seq")
    arrivals = []
    for k in range(1, count):
        sent = lax.dynamic_index_in_dim(pieces, own ^ k, 0, keepdims=True)
        arrivals.append(lax.ppermute(sent, "seq", [(i, i ^ k) for i in range(count)]))
    arrivals = yield tuple(arrivals)
    result = jnp.zeros_like(pieces)
    mine = lax.dynamic_index_in_dim(pieces, own, 0, keepdims=True)
    result = lax.dynamic_update_slice_in_dim(result, mine, own, 0)
    for k in range(1, count):
        result = lax.dynamic_update_slice_in_dim(result, arrivals[k - 1], own ^ k, 0)
    return result


def swap_rows(pieces):
    return (yield lax.all_to_all(pieces, "seq", 0, 0, tiled=True))


def flip_all(x, mask):
    count = lax.axis_size("batch") * lax.axis_size("seq")
    return lax.ppermute(x, ("batch", "seq"), [(i, i ^ mask) for i in range(count)])


def gather_all(x):
    masks = [0]
    bit = bits_of("batch") + bits_of("seq")
    while bit > 1:
        low = bit - 1
        steps = [m << low for m in range(1 << (bit - low))]
        pieces = [x] + [flip_all(x, m) for m in steps[1:]]
        x = jnp.concatenate(pieces, axis=0)
        masks = [m ^ n for m in steps for n in masks]
        bit = low
    return x, flip_all(x, 1), masks


class Later:
    value = None

    def get(self):
        return self.value


class Flow:
    def __init__(self):
        self.chains = {}
        self.waiting = {}
        self.results = {}

    def begin(self, name, chain):
        self.chains[name] = chain
        self.waiting[name] = next(chain)

    def tick(self, value=()):
        names = list(self.waiting)
        if not names:
            return value
        value, arrived = lax.optimization_barrier((value, [self.waiting[n] for n in names]))
        self.waiting = {}
        for name, array in zip(names, arrived):
            try:
                self.waiting[name] = self.chains[name].send(array)
            except StopIteration as stop:
                self.results[name] = stop.value
        for group in GROUPS:
            if group in self.chains or any(name not in self.results for name in group):
                continue
            chunks = [self.results[name] for name in group]
            self.begin(group, reduce_rest(chunks, group[0][0] == 0, group == GROUPS[-1]))
        return value

    def finish(self):
        while self.waiting:
            self.tick()


def add_blocks_kernel(kernel, counts, bits_ref, *refs):
    ins, outs = counts
    sources, targets = refs[:ins], refs[ins : ins + outs]
    held, made = refs[ins + outs : 2 * ins + outs], refs[2 * ins + outs : 2 * (ins + outs)]
    arrived, left = refs[-2:]
    steps = sources[0].shape[0]
    fetches = [
        [
            pltpu.make_async_copy(source.at[i], target.at[i], arrived.at[j, i])
            for j, (source, target) in enumerate(zip(sources, held))
        ]
        for i in range(steps)
    ]
    for step in fetches:
        for fetch in step:
            fetch.start()
    stores = []
    for i in range(steps):
        for fetch in fetches[i]:
            fetch.wait()
        kernel(bits_ref, *(ref.at[i : i + 1] for ref in (*held, *made)))
        for j, (source, target) in enumerate(zip(made, targets)):
            stores.append(pltpu.make_async_copy(source.at[i], target.at[i], left.at[j, i]))
            stores[-1].start()
    for store in stores:
        store.wait()


def add_blocks(kernel, bits, ins, outs, steps):
    anywhere = pl.BlockSpec(memory_space=pl.ANY)
    return pl.pallas_call(
        partial(add_blocks_kernel, kernel, (len(ins), len(outs))),
        grid_spec=pltpu.PrefetchScalarGridSpec(
            num_scalar_prefetch=1,
            grid=(1,),
            in_specs=[anywhere] * len(ins),
            out_specs=[anywhere] * len(outs),
            scratch_shapes=[pltpu.VMEM(x.shape, jnp.bfloat16) for x in (*ins, *outs)]
            + [
                pltpu.SemaphoreType.DMA((len(ins), steps)),
                pltpu.SemaphoreType.DMA((len(outs), steps)),
            ],
        ),
        out_shape=outs,
        compiler_params=pltpu.CompilerParams(vmem_limit_bytes=VMEM["add_blocks"] * MIB),
        cost_estimate=cost(2),
    )(bits, *ins)


def low_shape(*shape):
    return jax.ShapeDtypeStruct(shape, jnp.bfloat16)


def first_add_kernel(bits_ref, keep_ref, got_ref, send_a, keep_a, send_b, keep_b):
    seq_bit, batch_bit = bits_ref[0], bits_ref[1]
    early = send_a.shape[-1]

    def total(i, j, side):
        columns = slice(early, None) if side else slice(0, early)
        return add_low(keep_ref[o, i, j, :, columns], got_ref[o, i, j, :, columns])

    for o in range(keep_ref.shape[0]):
        for i in range(2):
            send_a[o, i] = total(i, 1 - seq_bit, 0)
            keep_a[o, i] = total(i, seq_bit, 0)
            send_b[o, i] = total(1 - batch_bit, i, 1)
            keep_b[o, i] = total(batch_bit, i, 1)


def second_add_kernel(bits_ref, *refs):
    count = len(refs) // 4 - 1
    outs = refs[4 * count :]
    for chunk in range(count):
        for side in range(2):
            keep_ref, got_ref = refs[4 * chunk + 2 * side : 4 * chunk + 2 * side + 2]
            send_out, keep_out = outs[2 * side : 2 * side + 2]
            bit = bits_ref[1 - side]
            send_out[0, chunk] = add_low(keep_ref[0, 1 - bit], got_ref[0, 1 - bit])
            keep_out[0, chunk] = add_low(keep_ref[0, bit], got_ref[0, bit])


def merge_add_kernel(bits_ref, *refs):
    send_out, keep_out = refs[-2:]
    early = refs[0].shape[-1]
    bit = bits_ref[0]
    place = 0
    for i in range(0, len(refs) - 2, 4):
        chunks = slice(place, place + refs[i].shape[2])
        place = chunks.stop
        for keep_ref, got_ref, columns in (
            (*refs[i : i + 2], slice(0, early)), (*refs[i + 2 : i + 4], slice(early, None)),
        ):
            send_out[0, chunks, :, columns] = add_low(keep_ref[0, 1 - bit], got_ref[0, 1 - bit])
            keep_out[0, chunks, :, columns] = add_low(keep_ref[0, bit], got_ref[0, bit])


def late_add_kernel(bits_ref, keep_ref, got_ref, send_out, keep_out):
    bit = bits_ref[0]
    send_out[0] = add_low(keep_ref[0, 1 - bit], got_ref[0, 1 - bit])
    keep_out[0] = add_low(keep_ref[0, bit], got_ref[0, bit])


def reduce_first(send, get_keep, second=False):
    assert bits_of("seq") == 2
    shards = lax.axis_size("batch")
    rows, columns = send.shape
    outer = shards // 2
    own_rows = rows // shards // 2
    seq_bit, batch_bit = own_bit("seq", 1), own_bit("batch", 0)
    bits = jnp.stack([seq_bit, batch_bit])
    got = yield flip(send, "seq", 0)
    keep = get_keep()
    shape = (outer, 2, 2, own_rows, columns)
    early = columns * 5 // 12
    outs = [low_shape(outer, 2, own_rows, n) for n in (early, early, columns - early, columns - early)]
    send_a, keep_a, send_b, keep_b = add_blocks(
        first_add_kernel, bits, [keep.reshape(shape), got.reshape(shape)], outs, outer
    )
    got_a, got_b = yield (flip(send_a, "seq", 1), flip(send_b, "batch", 0))
    chunk = [keep_a, got_a, keep_b, got_b]
    if second:
        chunk = yield from reduce_second([chunk])
    return chunk


def reduce_second(chunks):
    outer, _, own_rows, early = chunks[0][0].shape
    count = len(chunks)
    late = chunks[0][2].shape[3]
    bits = jnp.stack([own_bit("seq", 1), own_bit("batch", 0)])
    outs = [low_shape(outer, count, own_rows, n) for n in (early, early, late, late)]
    ins = [part for chunk in chunks for part in chunk]
    send_a, keep_a, send_b, keep_b = add_blocks(second_add_kernel, bits, ins, outs, outer)
    got_a, got_b = yield (flip(send_a, "batch", 0), flip(send_b, "seq", 1))
    return [keep_a, got_a, keep_b, got_b]


def reduce_rest(chunks, second, at_once):
    if not second:
        chunks = [(yield from reduce_second(chunks))]
        yield ()
    outer, _, own_rows, early = chunks[0][0].shape
    count = sum(chunk[0].shape[1] for chunk in chunks)
    columns = early + chunks[0][2].shape[3]
    parts = [part for chunk in chunks for part in chunk]
    for bit in range(1, bits_of("batch")):
        outer //= 2
        bits = own_bit("batch", bit).reshape(1)
        ins = [part.reshape((outer, 2) + part.shape[1:]) for part in parts]
        out = low_shape(outer, count, own_rows, columns)
        send, keep = add_blocks(
            merge_add_kernel if bit == 1 else late_add_kernel, bits, ins, [out] * 2, outer
        )
        got = yield flip(send, "batch", bit)
        parts = [keep, got]
    x = add_low(*parts).reshape(count, own_rows, columns)
    if at_once:
        across = lax.ppermute(x, "seq", [(i, i ^ 3) for i in range(lax.axis_size("seq"))])
        got, other, far = yield (flip(x, "seq", 1), flip(x, "seq", 0), across)
        return (x, got), (other, far)
    got = yield flip(x, "seq", 1)
    both = in_order(own_bit("seq", 1), (x, got), 1)
    got = yield flip(both, "seq", 0)
    return both, got


def in_order(bit, pieces, axis):
    own, other = pieces
    upper = bit == 1
    return jnp.concatenate([jnp.where(upper, other, own), jnp.where(upper, own, other)], axis=axis)


def assemble_kernel(
    level_count, shard_columns, bits_ref, tall, tall_got, low, low_got, own, own_got, other,
    other_got, joint_ref, mix_ref, expand_ref, shrink_ref,
):
    core, row_half = bits_ref[0], bits_ref[1]
    joint_size, mix_size = joint_ref.shape[2] // 2, mix_ref.shape[2] // 2
    expand_size = expand_ref.shape[2] // 2
    own_rows = own.shape[1]
    last = level_count - 1

    def columns(side, size):
        return pl.ds(pl.multiple_of(side * size, 128), size)

    def put_shrink(level, value, side):
        blocks = value.shape[1] // shard_columns
        rows = [value[:, j * shard_columns : (j + 1) * shard_columns] for j in range(blocks)]
        turned = jnp.concatenate(rows, axis=0).astype(jnp.float32).T
        shrink_ref[level, :, columns(side, turned.shape[1])] = turned

    def put_expand(level, value, side):
        expand_ref[level, :, columns(side, expand_size)] = value.astype(jnp.float32)

    def put_joint(level, rows, value, side):
        value = value.astype(jnp.float32)
        joint_ref[level, rows, columns(side, joint_size)] = value[:, :joint_size]
        mix_ref[level, rows, columns(side, mix_size)] = value[:, joint_size:]

    for source, partner, side in ((tall, low, core), (tall_got, low_got, 1 - core)):
        put_shrink(last, source[0], side)
        put_expand(last, source[1], side)
        put_joint(last, slice(None), source[2], side)
        put_shrink(0, partner[0], side)
        put_expand(0, partner[1], side)
    for source, half, side in (
        (own, row_half, core), (own_got, 1 - row_half, core),
        (other, row_half, 1 - core), (other_got, 1 - row_half, 1 - core),
    ):
        rows = pl.ds(pl.multiple_of(half * own_rows, own_rows), own_rows)
        put_joint(0, rows, source[0], side)


def assemble(results, level_count, width, inner, shares):
    core, row_half = own_bit("seq", 0), own_bit("seq", 1)
    (tall, tall_got), (low, low_got), last = (results[group] for group in GROUPS)
    (own, own_got), (other, other_got) = last
    rows = width // shares
    shard_columns = inner // shares
    shapes = [
        jax.ShapeDtypeStruct((level_count,) + shape, jnp.float32)
        for shape in ((rows, 3 * width), (rows, width), (rows, inner), (shard_columns, width))
    ]
    if shard_columns % 128 == 0 and rows % 32 == 0:
        return pl.pallas_call(
            partial(assemble_kernel, level_count, shard_columns),
            in_specs=[pl.BlockSpec(memory_space=pltpu.SMEM)]
            + [pl.BlockSpec(memory_space=pltpu.VMEM)] * 8,
            out_shape=shapes,
            compiler_params=pltpu.CompilerParams(vmem_limit_bytes=VMEM["assemble"] * MIB),
            cost_estimate=cost(5),
        )(
            jnp.stack([core, row_half]), tall, tall_got, low, low_got, own, own_got, other,
            other_got,
        )
    joint_size, mix_size = 3 * width // 2, width // 2
    joints = [in_order(row_half, pair, 1)[0] for pair in ((own, own_got), (other, other_got))]
    levels = []
    for shrinks, expands, joints in (
        ((low[0], low_got[0]), (low[1], low_got[1]), joints),
        ((tall[0], tall_got[0]), (tall[1], tall_got[1]), (tall[2], tall_got[2])),
    ):
        levels.append((
            in_order(core, [x[:, :joint_size] for x in joints], 1),
            in_order(core, [x[:, joint_size:] for x in joints], 1),
            in_order(core, expands, 1),
            in_order(core, [shrink_share(x, shard_columns) for x in shrinks], 1),
        ))
    return [jnp.stack(pair).astype(jnp.float32) for pair in zip(*levels)]


def reduce_small(x):
    for axis in ("seq", "batch"):
        for bit in range(bits_of(axis)):
            got = yield flip(x, axis, bit)
            x = x + got
    return x


def contrast_kernel(
    masks, place_ref, starts_ref, same_ref, other_ref, positives_ref, own_cot_ref, *refs
):
    *cot_refs, loss_ref, grad_ref, same, other, rows = refs
    place = place_ref[0]
    pair = place // 2
    seg_count = starts_ref.shape[0]
    width = same_ref.shape[1]
    scale = width ** (-0.5)
    for source, sorted_rows in ((same_ref, same), (other_ref, other)):
        values = source[...].astype(jnp.float32)
        for k, mask in enumerate(masks):
            begin = pl.multiple_of((pair ^ (mask >> 1)) * seg_count, seg_count)
            sorted_rows[pl.ds(begin, seg_count), :] = values[k * seg_count : (k + 1) * seg_count]
    even = place % 2 == 0
    same_rows, other_rows = same[...], other[...]
    queries = jnp.where(even, same_rows, other_rows).astype(jnp.bfloat16)
    passages = jnp.where(even, other_rows, same_rows).astype(jnp.bfloat16)
    contrast = dot(queries, passages, NT) * scale
    peak = jnp.max(contrast, axis=1, keepdims=True)
    log_total = peak + jnp.log(jnp.sum(jnp.exp(contrast - peak), axis=1, keepdims=True))
    turned_hits = positives_ref[...] == lax.broadcasted_iota(jnp.int32, contrast.shape, 0)
    hits = turned_hits.astype(jnp.float32).T
    target = jnp.sum(hits * contrast, axis=1, keepdims=True)
    loss_ref[...] = jnp.sum(log_total - target, axis=0, keepdims=True)
    chance = jnp.exp(contrast - log_total)
    contrast_grad = CONTRAST_WEIGHT * (chance - hits)
    rows[...] = jnp.where(even, contrast_grad, contrast_grad.T)
    begin = pl.multiple_of(pair * seg_count, seg_count)
    own = rows[pl.ds(begin, seg_count), :].astype(jnp.bfloat16)
    owned = dot(own, other_rows.astype(jnp.bfloat16)) * scale
    seq_count, part_len = own_cot_ref.shape[0], own_cot_ref.shape[1]
    at = lax.rem(place, seq_count)
    for k in range(seq_count):
        piece = own_cot_ref[at] if k == 0 else cot_refs[k - 1][0]
        begin = pl.multiple_of((at ^ k) * part_len, part_len)
        grad_ref[pl.ds(begin, part_len), :] = piece.astype(jnp.float32)
    for k in range(seg_count):
        grad_ref[pl.ds(starts_ref[k], 1), :] += owned[k : k + 1, :]


def contrast_part(place, low, starts, positives, cotangent, arrivals):
    full_len, width = low.shape
    seg_count = starts.shape[0]
    places = jnp.arange(full_len, dtype=jnp.int32)
    placed = (starts[:, None] == places[None, :]).astype(jnp.bfloat16)
    picked = dot(placed, low).astype(jnp.bfloat16)
    same, other, masks = gather_all(picked)
    count = same.shape[0]
    ins = [same, other, positives[None, :], cotangent, *arrivals]

    def whole(shape):
        return pl.BlockSpec(shape, lambda i, *_: (0,) * len(shape))

    loss, grad = pl.pallas_call(
        partial(contrast_kernel, masks),
        grid_spec=pltpu.PrefetchScalarGridSpec(
            num_scalar_prefetch=2,
            grid=(1,),
            in_specs=[whole(x.shape) for x in ins],
            out_specs=[whole((1, 1)), whole((full_len, width))],
            scratch_shapes=[
                pltpu.VMEM((count, width), jnp.float32),
                pltpu.VMEM((count, width), jnp.float32),
                pltpu.VMEM((count, count), jnp.float32),
            ],
        ),
        out_shape=[
            jax.ShapeDtypeStruct((1, 1), jnp.float32),
            jax.ShapeDtypeStruct((full_len, width), jnp.float32),
        ],
        compiler_params=pltpu.CompilerParams(vmem_limit_bytes=VMEM["contrast_part"] * MIB),
        cost_estimate=cost(4),
    )(place, starts, *ins)
    return loss[0, 0], grad


def body(
    tokens, lengths, positives, qkv_weight, attn_bias, out_weight, ffn_in, ffn_in_bias, ffn_out,
    ffn_out_bias, norm_gain, norm_bias, cotangent,
):
    batch_rows, part_len, width = tokens.shape
    seq_count = lax.axis_size("seq")
    assert batch_rows == seq_count
    full_len = part_len * seq_count
    own = lax.axis_index("seq")
    own_lengths = lax.dynamic_index_in_dim(lengths, own, 0, keepdims=False)
    starts = jnp.cumsum(own_lengths, dtype=jnp.int32) - own_lengths
    places = jnp.arange(full_len, dtype=jnp.int32)
    segment = jnp.sum(
        (places[:, None] >= starts[None, 1:]).astype(jnp.int32), axis=1, dtype=jnp.int32
    )
    column_ids, row_ids = segment[:, None], segment[None, :]
    params = (
        qkv_weight, attn_bias, out_weight, ffn_in, ffn_in_bias, ffn_out, ffn_out_bias, norm_gain,
        norm_bias,
    )
    level_count = qkv_weight.shape[0]
    flow = Flow()
    flow.begin("tokens", exchange_rows(tokens))
    flow.finish()
    hidden = flow.results["tokens"].reshape(full_len, width).astype(jnp.float32)
    stored = []
    for level in range(level_count):
        weights = tuple(entry[level] for entry in params)
        hidden, kept = forward_layer(hidden, weights, column_ids, row_ids, full_len)
        stored.append(kept)
        if level == 0:
            hidden, cotangent = lax.optimization_barrier((hidden, cotangent))
            arrivals = next(exchange_rows(cotangent))
    low = hidden.astype(jnp.bfloat16)
    place = (lax.axis_index("batch") * seq_count + own).reshape(1)
    loss, grad = contrast_part(place, low, starts, positives, cotangent, arrivals)
    params = (qkv_weight, out_weight, ffn_in, ffn_out, norm_gain)
    sums = [None] * level_count
    for level in reversed(range(level_count)):
        grad, sums[level] = backward_layer(
            grad, stored[level], params, column_ids, row_ids, flow, level
        )
    grad = flow.tick(grad)
    flow.begin("small", reduce_small(jnp.stack(sums)))
    grad = flow.tick(grad)
    flow.begin("input", swap_rows(grad.reshape(batch_rows, part_len, width)))
    flow.tick()
    low = flow.tick(low)
    flow.begin("output", swap_rows(low.reshape(batch_rows, part_len, width)))
    flow.finish()
    layer_output = flow.results["output"]
    returned = flow.results["input"]
    shares = lax.axis_size("batch")
    share = lax.axis_index("batch")
    joint_grad, mix_grad, expand_grad, shrink_grad = assemble(
        flow.results, level_count, width, ffn_in.shape[2], shares
    )
    sums = flow.results["small"]
    inner = ffn_in.shape[2]
    own_sums = lax.dynamic_slice_in_dim(sums, share * (width // shares), width // shares, 2)
    own_inner = lax.dynamic_slice_in_dim(
        sums[:, 11 : 11 + inner // width].reshape(level_count, inner),
        share * (inner // shares), inner // shares, 1,
    )
    bias_grad = jnp.stack([own_sums[:, 16], own_sums[:, 17], own_sums[:, 10]], axis=1)
    expand_bias, shrink_bias = own_inner, own_sums[:, 2]
    gain_grad = jnp.stack([own_sums[:, 8], own_sums[:, 0]], axis=1)
    shift_grad = jnp.stack([own_sums[:, 9], own_sums[:, 1]], axis=1)
    return (
        layer_output, returned.astype(jnp.float32), loss, joint_grad, bias_grad, mix_grad,
        expand_grad, expand_bias, shrink_grad, shrink_bias, gain_grad, shift_grad,
    )


def solution(mesh):
    return jax.shard_map(
        body,
        mesh=mesh,
        in_specs=(
            P("batch", "seq", None), P("batch", None), P(), P(), P(), P(), P(), P(), P(), P(), P(),
            P(), P("batch", "seq", None),
        ),
        out_specs=(
            P("batch", "seq", None),
            P("batch", "seq", None),
            P(),
            P(None, "batch", None),
            P(None, None, "batch"),
            P(None, "batch", None),
            P(None, "batch", None),
            P(None, "batch"),
            P(None, "batch", None),
            P(None, "batch"),
            P(None, None, "batch"),
            P(None, None, "batch"),
        ),
        check_vma=False,
    )
```

time: 1980 us -> 396 us (0.20)
  blocking collectives: 734 us -> 0 us
  waiting for transfers between devices: 818 us -> 86.9 us
  Pallas kernels: 0 us -> 189 us
  matrix products: 198 us -> 27.3 us
  local copies, waits for them, and re-layouts: 120 us -> 7.84 us
  other arithmetic: 82.2 us -> 17.4 us
  starting transfers between devices: 1.17 us -> 62.2 us
    unnamed x1 -> x0, blocking collectives: 685 us -> none
    reduce_scatter x7 -> x0, waiting for transfers between devices: 361 us -> none  [the longest x1 306 us: body(): lax.psum_scatter(stacked[3], 'batch', scatter_dimension=1, tiled=True)]
    unnamed x22 -> x0, waiting for transfers between devices: 311 us -> none
    pallas_call x0 -> x28, Pallas kernels: none -> 189 us  [the longest x16 56.2 us: add_blocks(): pl.pallas_call(partial(add_blocks_kernel, kernel, (len(ins), len(outs))),...]
    dot_general x41 -> x9, matrix products: 198 us -> 27.3 us  [dot(): return lax.dot_general(a, b, dims, preferred_element_type=jnp.float32)]
    ppermute x0 -> x55, waiting for transfers between devices: none -> 86.9 us  [the longest x43 67.2 us: flip(): return lax.ppermute(x, axis, [(i, i ^ 1 << bit) for i in range(count)])]
    all_gather x4 -> x0, waiting for transfers between devices: 76.6 us -> none  [the longest x2 47.7 us: forward_layer(): lax.all_gather(key_block.reshape(shape_rows), 'seq', axis=1, tiled=True)]
    psum x1 -> x0, waiting for transfers between devices: 68.6 us -> none  [body(): lax.psum(shares[0].astype(jnp.bfloat16), 'seq').astype(jnp.float32)]
  transfers between devices with their start and end apart: 17 -> 57, of which waited for: 13 -> 22; matrix products, arithmetic and copies ran while one was open for 10% -> 2% of each run, Pallas kernels for 0% -> 38%
where the time goes in v1:
time: 396 us; the launch traced here: 392 us
  Pallas kernels  189 us (48%)
  waiting for transfers between devices  86.9 us (22%)
  starting transfers between devices  62.2 us (16%)
  matrix products  27.3 us (7%)
  other arithmetic  17.4 us (4%)
  local copies, waits for them, and re-layouts  7.84 us (2%)
    ppermute x43, waiting for transfers between devices, flip(): return lax.ppermute(x, axis, [(i, i ^ 1 << bit) for i in range(count)])  67.2 us
    pallas_call x16, Pallas kernels, add_blocks(): pl.pallas_call(partial(add_blocks_kernel, kernel, (len(ins), len(outs))),...  56.2 us
    ppermute x43, starting transfers between devices, flip(): return lax.ppermute(x, axis, [(i, i ^ 1 << bit) for i in range(count)])  40.9 us
    pallas_call x2, Pallas kernels, expand_backward(): pl.pallas_call(partial(expand_backward_kernel, steps, level), grid_spec=p...  37.5 us
    pallas_call x2, Pallas kernels, attention_backward(): pl.pallas_call(attention_backward_kernel, grid_spec=pltpu.PrefetchScalarG...  36 us
    dot_general x9, matrix products, dot(): return lax.dot_general(a, b, dims, preferred_element_type=jnp.float32)  27.3 us
    pallas_call x2, Pallas kernels, shrink_backward(): pl.pallas_call(partial(shrink_backward_kernel, shard_columns), grid_spec=...  17 us
    pallas_call x2, Pallas kernels, joint_backward(): pl.pallas_call(partial(joint_backward_kernel, level), grid_spec=pltpu.Pre...  16.6 us
  transfers between devices with their start and end apart: 57, of which 22 were waited for; matrix products, arithmetic and copies ran while one was open for 2% of the time, Pallas kernels for 38%

profile of v1, /device:TPU:0, one launch (start us, length us, event | category | flops | bytes accessed | tf_op | source)
XLA Modules:
  0.0 392.5 jit_solution(3535887520700684828)
XLA Ops:
  6.6 4.3 %collective-permute-done.1 = bf16[1,128,768]{2,1,0:T(8,128)(2,1)S(1)} collective-permute-done((bf16[1,128,768]{2,1,0:T(8,128)(2,1)S(1)}, bf16[1,128,768]{2,1,0:T(8,128)(2,1)S(1)}, u32[]{:S(2)}, u32[]{:S(2)}) %collective-permute-start.1) | collective-permute-done | bytes 196640 | tf_op jit(solution)/shard_map/ppermute | solution.py:584
  10.9 3.7 collective-permute-done.2
  14.7 4.3 %fusion.22.qkv_ref.qkv_any = bf16[512,2304]{1,0:T(8,128)(2,1)S(1)} fusion(bf16[512,768]{1,0:T(8,128)(2,1)S(1)} %bitcast.137, bf16[2,768,2304]{2,1,0:T(8,128)(2,1)} %weight_any.3, f32[2304]{0:T(1024)S(1)} %get-tuple-element.426), kind=kOutput, calls=%fused_computation.30 | convolution fusion | flops 1814298624 | bytes 6693888 | tf_op jit(solution)/shard_map/dot_general | solution.py:47
  19.1 8.2 %shard_map.220 = (bf16[512,768]{1,0:T(8,128)(2,1)S(1)}, f32[6,8,512]{2,1,0:T(8,128)S(1)}) custom-call(bf16[512,2304]{1,0:T(8,128)(2,1)S(1)} %fusion.22.qkv_ref.qkv_any, s32[512,1]{1,0:T(8,128)S(1)} %copy.33.column_ids_ref, s32[1,512]{1,0:T(1,128)S(1)} %bitcast.132), custom_call_target="tpu_custom_call" | custom-call | flops 8000000000 | bytes 16000000 | tf_op jit(solution)/shard_map/pallas_call | solution.py:83
  29.1 6.1 %fusion.9 = (bf16[512,3072]{1,0:T(8,128)(2,1)}, bf16[512,3072]{1,0:T(8,128)(2,1)S(1)}) fusion(f32[3072]{0:T(1024)S(1)} %bitcast.143, bf16[512,768]{1,0:T(8,128)(2,1)S(1)} %get-tuple-element.392.middle_ref, bf16[2,768,3072]{2,1,0:T(8,128)(2,1)S(1)} %bitcast.150), kind=kOutput, calls=%fused_computation.11 | convolution fusion | flops 2434793472 | bytes 11808768 | tf_op jit(solution)/shard_map/dot_general | solution.py:47
  35.2 2.7 fusion.45
  42.0 7.7 %shard_map.221 = (bf16[512,768]{1,0:T(8,128)(2,1)S(1)}, f32[6,8,512]{2,1,0:T(8,128)S(1)}) custom-call(bf16[512,2304]{1,0:T(8,128)(2,1)S(1)} %fusion.23.qkv_ref.qkv_any, s32[512,1]{1,0:T(8,128)S(1)} %copy.33.column_ids_ref, s32[1,512]{1,0:T(1,128)S(1)} %bitcast.133), custom_call_target="tpu_custom_call" | custom-call | flops 8000000000 | bytes 16000000 | tf_op jit(solution)/shard_map/pallas_call | solution.py:83
  51.4 6.2 %fusion.4 = (bf16[512,3072]{1,0:T(8,128)(2,1)}, bf16[512,3072]{1,0:T(8,128)(2,1)S(1)}) fusion(f32[3072]{0:T(1024)S(1)} %bitcast.142, bf16[512,768]{1,0:T(8,128)(2,1)S(1)} %get-tuple-element.388.middle_ref, bf16[2,768,3072]{2,1,0:T(8,128)(2,1)S(1)} %bitcast.150), kind=kOutput, calls=%fused_computation.6 | convolution fusion | flops 2434793472 | bytes 11808768 | tf_op jit(solution)/shard_map/dot_general | solution.py:47
  57.6 2.7 fusion.47
  63.9 2.7 collective-permute-start.3
  78.3 3.1 collective-permute-done.6
  83.6 4.1 %shard_map.222 = (f32[1,1]{1,0:T(1,128)}, f32[512,768]{1,0:T(8,128)}) custom-call(s32[1]{0:T(128)} %bitcast.21.place_ref, s32[8]{0:T(128)} %copy-done.42, bf16[128,768]{1,0:T(8,128)(2,1)} %copy-done.43, bf16[128,768]{1,0:T(8,128)(2,1)} %copy-done.60, s32[1,128]{1,0:T(1,128)} %bitcast.161, bf16[4,128,768]{2,1,0:T(8,128)(2,1)} %own_cot_ref, ...), custom_call_target="tpu_custom_call" | custom-call | flops 4000000000 | bytes 8000000 | tf_op jit(solution)/shard_map/pallas_call | solution.py:969
  87.7 8.4 %shard_map.223 = (bf16[768,1536]{1,0:T(8,128)(2,1)}, bf16[768,1536]{1,0:T(8,128)(2,1)}, f32[512,768]{1,0:T(8,128)}, bf16[512,768]{1,0:T(8,128)(2,1)}, f32[8,768]{1,0:T(8,128)}) custom-call(s32[1]{0:T(128)} %bitcast.20.bit_ref.half_ref, f32[512,768]{1,0:T(8,128)} %get-tuple-element.180.grad_ref, f32[512,768]{1,0:T(8,128)} %get-tuple-element.387.normed_ref, ...), custom_call_target="tpu_custom_call" | custom-call | flops 6000000000 | bytes 12000000 | tf_op jit(solution)/shard_map/pallas_call | solution.py:163
  96.3 18.6 %shard_map.224 = (bf16[768,1536]{1,0:T(8,128)(2,1)}, bf16[768,1536]{1,0:T(8,128)(2,1)}, f32[512,768]{1,0:T(8,128)}, bf16[512,768]{1,0:T(8,128)(2,1)}, bf16[512,768]{1,0:T(8,128)(2,1)}, /*index=5*/f32[8,768]{1,0:T(8,128)}) custom-call(s32[1]{0:T(128)} %bitcast.20.bit_ref.half_ref, bf16[512,768]{1,0:T(8,128)(2,1)} %get-tuple-element.182.low_ref, ...), custom_call_target="tpu_custom_call" | custom-call | flops 16000000000 | bytes 32000000 | tf_op jit(solution)/shard_map/pallas_call | solution.py:275
  115.9 4.2 %shard_map.225 = (bf16[4,2,48,640]{3,2,1,0:T(8,128)(2,1)}, bf16[4,2,48,640]{3,2,1,0:T(8,128)(2,1)}, bf16[4,2,48,896]{3,2,1,0:T(8,128)(2,1)}, bf16[4,2,48,896]{3,2,1,0:T(8,128)(2,1)}) custom-call(s32[2]{0:T(128)} %pad_add_fusion.bits_ref, bf16[4,2,2,48,1536]{4,3,2,1,0:T(8,128)(2,1)} %bitcast.165, bf16[4,2,2,48,1536]{4,3,2,1,0:T(8,128)(2,1)} %bitcast.28.refs_1_), custom_call_target="tpu_custom_call" | custom-call | flops 2000000000 | bytes 4000000 | tf_op jit(solution)/shard_map/pallas_call | solution.py:686
  123.2 17.9 %shard_map.226 = (bf16[512,2304]{1,0:T(8,128)(2,1)}, bf16[768,1536]{1,0:T(8,128)(2,1)}, f32[8,768]{1,0:T(8,128)}) custom-call(s32[1]{0:T(128)S(6)} %sub.48.half_ref, f32[6,8,512]{2,1,0:T(8,128)} %copy-done.7, s32[512,1]{1,0:T(8,128)} %copy-done, s32[1,512]{1,0:T(1,128)} %bitcast.134, bf16[512,2304]{1,0:T(8,128)(2,1)} %copy-done.5, ...), custom_call_target="tpu_custom_call" | custom-call | flops 14000000000 | bytes 28000000 | tf_op jit(solution)/shard_map/pallas_call | solution.py:406
  141.3 4.2 %shard_map.227 = (bf16[4,2,48,640]{3,2,1,0:T(8,128)(2,1)}, bf16[4,2,48,640]{3,2,1,0:T(8,128)(2,1)}, bf16[4,2,48,896]{3,2,1,0:T(8,128)(2,1)}, bf16[4,2,48,896]{3,2,1,0:T(8,128)(2,1)}) custom-call(s32[2]{0:T(128)} %pad_add_fusion.bits_ref, bf16[4,2,2,48,1536]{4,3,2,1,0:T(8,128)(2,1)} %bitcast.164, bf16[4,2,2,48,1536]{4,3,2,1,0:T(8,128)(2,1)} %bitcast.30.refs_1_), custom_call_target="tpu_custom_call" | custom-call | flops 2000000000 | bytes 4000000 | tf_op jit(solution)/shard_map/pallas_call | solution.py:686
  146.6 8.4 %shard_map.228 = (bf16[768,1536]{1,0:T(8,128)(2,1)}, f32[512,768]{1,0:T(8,128)}) custom-call(s32[1]{0:T(128)} %bitcast.20.bit_ref.half_ref, bf16[512,768]{1,0:T(8,128)(2,1)} %copy-done.2, bf16[512,768]{1,0:T(8,128)(2,1)} %copy-done.14, bf16[512,2304]{1,0:T(8,128)(2,1)} %get-tuple-element.204.joint_any, bf16[512,768]{1,0:T(8,128)(2,1)} %get-tuple-element.192.branch_any, ...), custom_call_target="tpu_custom_call" | custom-call | flops 7000000000 | bytes 14000000 | tf_op jit(solution)/shard_map/pallas_call | solution.py:466
  155.1 8.6 %shard_map.229 = (bf16[768,1536]{1,0:T(8,128)(2,1)}, bf16[768,1536]{1,0:T(8,128)(2,1)}, f32[512,768]{1,0:T(8,128)}, bf16[512,768]{1,0:T(8,128)(2,1)}, f32[8,768]{1,0:T(8,128)}) custom-call(s32[1]{0:T(128)} %bitcast.20.bit_ref.half_ref, f32[512,768]{1,0:T(8,128)} %get-tuple-element.206.grad_ref, f32[512,768]{1,0:T(8,128)} %get-tuple-element.391.normed_ref, ...), custom_call_target="tpu_custom_call" | custom-call | flops 6000000000 | bytes 12000000 | tf_op jit(solution)/shard_map/pallas_call | solution.py:163
  163.8 4.2 %shard_map.230 = (bf16[4,2,48,640]{3,2,1,0:T(8,128)(2,1)}, bf16[4,2,48,640]{3,2,1,0:T(8,128)(2,1)}, bf16[4,2,48,896]{3,2,1,0:T(8,128)(2,1)}, bf16[4,2,48,896]{3,2,1,0:T(8,128)(2,1)}) custom-call(s32[2]{0:T(128)} %pad_add_fusion.bits_ref, bf16[4,2,2,48,1536]{4,3,2,1,0:T(8,128)(2,1)} %bitcast.167, bf16[4,2,2,48,1536]{4,3,2,1,0:T(8,128)(2,1)} %bitcast.34.refs_1_), custom_call_target="tpu_custom_call" | custom-call | flops 2000000000 | bytes 4000000 | tf_op jit(solution)/shard_map/pallas_call | solution.py:686
  171.1 19.0 %shard_map.231 = (bf16[768,1536]{1,0:T(8,128)(2,1)}, bf16[768,1536]{1,0:T(8,128)(2,1)}, f32[512,768]{1,0:T(8,128)}, bf16[512,768]{1,0:T(8,128)(2,1)}, bf16[512,768]{1,0:T(8,128)(2,1)}, /*index=5*/f32[8,768]{1,0:T(8,128)}) custom-call(s32[1]{0:T(128)} %bitcast.20.bit_ref.half_ref, bf16[512,768]{1,0:T(8,128)(2,1)} %get-tuple-element.219.low_ref, ...), custom_call_target="tpu_custom_call" | custom-call | flops 16000000000 | bytes 32000000 | tf_op jit(solution)/shard_map/pallas_call | solution.py:275
  190.2 4.2 %shard_map.234 = (bf16[4,2,48,640]{3,2,1,0:T(8,128)(2,1)}, bf16[4,2,48,640]{3,2,1,0:T(8,128)(2,1)}, bf16[4,2,48,896]{3,2,1,0:T(8,128)(2,1)}, bf16[4,2,48,896]{3,2,1,0:T(8,128)(2,1)}) custom-call(s32[2]{0:T(128)} %pad_add_fusion.bits_ref, bf16[4,2,2,48,1536]{4,3,2,1,0:T(8,128)(2,1)} %bitcast.163, bf16[4,2,2,48,1536]{4,3,2,1,0:T(8,128)(2,1)} %bitcast.39.refs_1_), custom_call_target="tpu_custom_call" | custom-call | flops 2000000000 | bytes 4000000 | tf_op jit(solution)/shard_map/pallas_call | solution.py:686
  195.6 5.9 %shard_map.232 = (bf16[4,3,48,640]{3,2,1,0:T(8,128)(2,1)}, bf16[4,3,48,640]{3,2,1,0:T(8,128)(2,1)}, bf16[4,3,48,896]{3,2,1,0:T(8,128)(2,1)}, bf16[4,3,48,896]{3,2,1,0:T(8,128)(2,1)}) custom-call(s32[2]{0:T(128)} %pad_add_fusion.bits_ref, bf16[4,2,48,640]{3,2,1,0:T(8,128)(2,1)} %get-tuple-element.189.refs_0_, ...), custom_call_target="tpu_custom_call" | custom-call | flops 2000000000 | bytes 4000000 | tf_op jit(solution)/shard_map/pallas_call | solution.py:686
  204.6 18.0 %shard_map.233 = (bf16[512,2304]{1,0:T(8,128)(2,1)}, bf16[768,1536]{1,0:T(8,128)(2,1)}, f32[8,768]{1,0:T(8,128)}) custom-call(s32[1]{0:T(128)S(6)} %sub.48.half_ref, f32[6,8,512]{2,1,0:T(8,128)} %copy-done.6, s32[512,1]{1,0:T(8,128)} %copy-done, s32[1,512]{1,0:T(1,128)} %bitcast.135, bf16[512,2304]{1,0:T(8,128)(2,1)} %copy-done.4, ...), custom_call_target="tpu_custom_call" | custom-call | flops 14000000000 | bytes 28000000 | tf_op jit(solution)/shard_map/pallas_call | solution.py:406
  222.6 5.8 %collective-permute-done.23 = bf16[4,3,48,640]{3,2,1,0:T(8,128)(2,1)S(1)} collective-permute-done((bf16[4,3,48,640]{3,2,1,0:T(8,128)(2,1)}, bf16[4,3,48,640]{3,2,1,0:T(8,128)(2,1)S(1)}, u32[]{:S(2)}, u32[]{:S(2)}) %collective-permute-start.23) | collective-permute-done | bytes 737312 | tf_op jit(solution)/shard_map/ppermute | solution.py:563
  230.9 4.2 %shard_map.238 = (bf16[4,2,48,640]{3,2,1,0:T(8,128)(2,1)}, bf16[4,2,48,640]{3,2,1,0:T(8,128)(2,1)}, bf16[4,2,48,896]{3,2,1,0:T(8,128)(2,1)}, bf16[4,2,48,896]{3,2,1,0:T(8,128)(2,1)}) custom-call(s32[2]{0:T(128)} %pad_add_fusion.bits_ref, bf16[4,2,2,48,1536]{4,3,2,1,0:T(8,128)(2,1)} %bitcast.162, bf16[4,2,2,48,1536]{4,3,2,1,0:T(8,128)(2,1)} %bitcast.45.refs_1_), custom_call_target="tpu_custom_call" | custom-call | flops 2000000000 | bytes 4000000 | tf_op jit(solution)/shard_map/pallas_call | solution.py:686
  237.2 3.3 shard_map.237
  242.6 8.1 %shard_map.236 = (bf16[768,1536]{1,0:T(8,128)(2,1)}, bf16[512,768]{1,0:T(8,128)(2,1)}) custom-call(s32[1]{0:T(128)} %bitcast.20.bit_ref.half_ref, bf16[512,768]{1,0:T(8,128)(2,1)} %copy-done.3, bf16[512,768]{1,0:T(8,128)(2,1)} %bitcast.140, bf16[512,2304]{1,0:T(8,128)(2,1)} %get-tuple-element.247.joint_any, bf16[512,768]{1,0:T(8,128)(2,1)} %get-tuple-element.233.branch_any, ...), custom_call_target="tpu_custom_call" | custom-call | flops 7000000000 | bytes 14000000 | tf_op jit(solution)/shard_map/pallas_call | solution.py:466
  250.8 3.0 shard_map.235
  253.8 4.8 %collective-permute-done.26 = bf16[4,1,48,640]{3,2,1,0:T(8,128)(2,1)} collective-permute-done((bf16[4,1,48,640]{3,2,1,0:T(8,128)(2,1)}, bf16[4,1,48,640]{3,2,1,0:T(8,128)(2,1)}, u32[]{:S(2)}, u32[]{:S(2)}) %collective-permute-start.26) | collective-permute-done | bytes 245792 | tf_op jit(solution)/shard_map/ppermute | solution.py:563
  261.0 4.3 %shard_map.240 = (bf16[4,2,48,640]{3,2,1,0:T(8,128)(2,1)}, bf16[4,2,48,640]{3,2,1,0:T(8,128)(2,1)}, bf16[4,2,48,896]{3,2,1,0:T(8,128)(2,1)}, bf16[4,2,48,896]{3,2,1,0:T(8,128)(2,1)}) custom-call(s32[2]{0:T(128)} %pad_add_fusion.bits_ref, bf16[4,2,2,48,1536]{4,3,2,1,0:T(8,128)(2,1)} %bitcast.166, bf16[4,2,2,48,1536]{4,3,2,1,0:T(8,128)(2,1)} %bitcast.47.refs_1_), custom_call_target="tpu_custom_call" | custom-call | flops 2000000000 | bytes 4000000 | tf_op jit(solution)/shard_map/pallas_call | solution.py:686
  267.6 3.3 shard_map.239
  273.1 7.0 %collective-permute-done.31 = bf16[2,3,48,1536]{3,2,1,0:T(8,128)(2,1)} collective-permute-done((bf16[2,3,48,1536]{3,2,1,0:T(8,128)(2,1)}, bf16[2,3,48,1536]{3,2,1,0:T(8,128)(2,1)}, u32[]{:S(2)}, u32[]{:S(2)}) %collective-permute-start.31) | collective-permute-done | bytes 884768 | tf_op jit(solution)/shard_map/ppermute | solution.py:563
  280.1 7.5 %collective-permute-done.32 = bf16[4,1,48,640]{3,2,1,0:T(8,128)(2,1)S(1)} collective-permute-done((bf16[4,1,48,640]{3,2,1,0:T(8,128)(2,1)}, bf16[4,1,48,640]{3,2,1,0:T(8,128)(2,1)S(1)}, u32[]{:S(2)}, u32[]{:S(2)}) %collective-permute-start.32) | collective-permute-done | bytes 245792 | tf_op jit(solution)/shard_map/ppermute | solution.py:563
  289.1 2.9 shard_map.243
  292.5 3.5 all-to-all-start
  300.8 3.3 shard_map.242
  308.3 9.9 %collective-permute-done.40 = f32[2,24,768]{2,1,0:T(8,128)S(1)} collective-permute-done((f32[2,24,768]{2,1,0:T(8,128)S(1)}, f32[2,24,768]{2,1,0:T(8,128)S(1)}, u32[]{:S(2)}, u32[]{:S(2)}) %collective-permute-start.40) | collective-permute-done | bytes 147488 | tf_op jit(solution)/shard_map/ppermute | solution.py:563
  318.2 3.6 collective-permute-done.37
  330.0 3.4 collective-permute-start.44
  335.4 4.2 %collective-permute-done.43 = f32[2,24,768]{2,1,0:T(8,128)S(1)} collective-permute-done((f32[2,24,768]{2,1,0:T(8,128)S(1)}, f32[2,24,768]{2,1,0:T(8,128)S(1)}, u32[]{:S(2)}, u32[]{:S(2)}) %collective-permute-start.43) | collective-permute-done | bytes 147488 | tf_op jit(solution)/shard_map/ppermute | solution.py:563
  339.6 6.3 %collective-permute-done.44 = bf16[1,2,48,1536]{3,2,1,0:T(8,128)(2,1)S(1)} collective-permute-done((bf16[1,2,48,1536]{3,2,1,0:T(8,128)(2,1)}, bf16[1,2,48,1536]{3,2,1,0:T(8,128)(2,1)S(1)}, u32[]{:S(2)}, u32[]{:S(2)}) %collective-permute-start.44) | collective-permute-done | bytes 294944 | tf_op jit(solution)/shard_map/ppermute | solution.py:563
  348.0 3.5 all-to-all-start.1
  357.1 3.0 collective-permute-start.47
  360.1 5.8 %collective-permute-done.49 = bf16[1,1,48,1536]{3,2,1,0:T(8,128)(2,1)S(1)} collective-permute-done((bf16[1,1,48,1536]{3,2,1,0:T(8,128)(2,1)}, bf16[1,1,48,1536]{3,2,1,0:T(8,128)(2,1)S(1)}, u32[]{:S(2)}, u32[]{:S(2)}) %collective-permute-start.49) | collective-permute-done | bytes 147488 | tf_op jit(solution)/shard_map/ppermute | solution.py:563
  366.8 2.7 collective-permute-done.48
  380.0 2.9 collective-permute-done.50
  386.1 5.3 %shard_map.247 = (f32[2,96,2304]{2,1,0:T(8,128)}, f32[2,96,768]{2,1,0:T(8,128)}, f32[2,96,3072]{2,1,0:T(8,128)}, f32[2,384,768]{2,1,0:T(8,128)}) custom-call(s32[2]{0:T(128)} %pad_add_fusion.1.bits_ref, bf16[3,96,1536]{2,1,0:T(8,128)(2,1)} %pad_maximum_fusion.tall, bf16[3,96,1536]{2,1,0:T(8,128)(2,1)} %collective-permute-done.46.tall_got, ...), custom_call_target="tpu_custom_call" | custom-call | flops 5000000000 | bytes 10000000 | tf_op jit(solution)/shard_map/pallas_call | solution.py:880
  (320 shorter events, 100.6 us)
Async XLA Ops:
  2.6 8.3 %collective-permute-start.1 = (bf16[1,128,768]{2,1,0:T(8,128)(2,1)S(1)}, bf16[1,128,768]{2,1,0:T(8,128)(2,1)S(1)}, u32[]{:S(2)}, u32[]{:S(2)}) collective-permute-start(bf16[1,128,768]{2,1,0:T(8,128)(2,1)S(1)} %get-tuple-element.406), channel_id=1, source_target_pairs={{0,2},{1,3},{2,0},{3,1},{4,6},{5,7},{6,4},{7,5},{8,10},{9,11},{10,... | collective-permute-start | bytes 589832 | tf_op jit(solution)/shard_map/ppermute | solution.py:584
  5.2 9.4 %collective-permute-start.2 = (bf16[1,128,768]{2,1,0:T(8,128)(2,1)S(1)}, bf16[1,128,768]{2,1,0:T(8,128)(2,1)S(1)}, u32[]{:S(2)}, u32[]{:S(2)}) collective-permute-start(bf16[1,128,768]{2,1,0:T(8,128)(2,1)S(1)} %get-tuple-element.403), channel_id=1, source_target_pairs={{0,3},{1,2},{2,1},{3,0},{4,7},{5,6},{6,5},{7,4},{8,11},{9,10},{10,... | collective-permute-start | bytes 589832 | tf_op jit(solution)/shard_map/ppermute | solution.py:584
  66.6 14.9 %collective-permute-start.10 = (bf16[1,128,768]{2,1,0:T(8,128)(2,1)S(1)}, bf16[1,128,768]{2,1,0:T(8,128)(2,1)S(1)}, u32[]{:S(2)}, u32[]{:S(2)}) collective-permute-start(bf16[1,128,768]{2,1,0:T(8,128)(2,1)S(1)} %get-tuple-element.400), channel_id=1, source_target_pairs={{0,3},{1,2},{2,1},{3,0},{4,7},{5,6},{6,5},{7,4},{8,11},{9,10},{10,... | collective-permute-start | bytes 589832 | tf_op jit(solution)/shard_map/ppermute | solution.py:584
  67.8 13.8 %collective-permute-start.8 = (bf16[1,128,768]{2,1,0:T(8,128)(2,1)S(1)}, bf16[1,128,768]{2,1,0:T(8,128)(2,1)S(1)}, u32[]{:S(2)}, u32[]{:S(2)}) collective-permute-start(bf16[1,128,768]{2,1,0:T(8,128)(2,1)S(1)} %get-tuple-element.402), channel_id=1, source_target_pairs={{0,1},{1,0},{2,3},{3,2},{4,5},{5,4},{6,7},{7,6},{8,9},{9,8},{10,11... | collective-permute-start | bytes 589832 | tf_op jit(solution)/shard_map/ppermute | solution.py:584
  68.3 13.3 %collective-permute-start.9 = (bf16[1,128,768]{2,1,0:T(8,128)(2,1)S(1)}, bf16[1,128,768]{2,1,0:T(8,128)(2,1)S(1)}, u32[]{:S(2)}, u32[]{:S(2)}) collective-permute-start(bf16[1,128,768]{2,1,0:T(8,128)(2,1)S(1)} %get-tuple-element.401), channel_id=1, source_target_pairs={{0,2},{1,3},{2,0},{3,1},{4,6},{5,7},{6,4},{7,5},{8,10},{9,11},{10,... | collective-permute-start | bytes 589832 | tf_op jit(solution)/shard_map/ppermute | solution.py:584
  96.1 18.7 %collective-permute-start.11 = (bf16[768,1536]{1,0:T(8,128)(2,1)}, bf16[768,1536]{1,0:T(8,128)(2,1)}, u32[]{:S(2)}, u32[]{:S(2)}) collective-permute-start(bf16[768,1536]{1,0:T(8,128)(2,1)} %get-tuple-element.187), channel_id=1, source_target_pairs={{0,1},{1,0},{2,3},{3,2},{4,5},{5,4},{6,7},{7,6},{8,9},{9,8},{10,11... | collective-permute-start | bytes 7077896 | tf_op jit(solution)/shard_map/ppermute | solution.py:563
  114.9 26.4 %collective-permute-start.14 = (bf16[768,1536]{1,0:T(8,128)(2,1)}, bf16[768,1536]{1,0:T(8,128)(2,1)}, u32[]{:S(2)}, u32[]{:S(2)}) collective-permute-start(bf16[768,1536]{1,0:T(8,128)(2,1)} %get-tuple-element.197), channel_id=1, source_target_pairs={{0,1},{1,0},{2,3},{3,2},{4,5},{5,4},{6,7},{7,6},{8,9},{9,8},{10,11... | collective-permute-start | bytes 7077896 | tf_op jit(solution)/shard_map/ppermute | solution.py:563
  120.1 21.0 %collective-permute-start.13 = (bf16[4,2,48,896]{3,2,1,0:T(8,128)(2,1)}, bf16[4,2,48,896]{3,2,1,0:T(8,128)(2,1)S(1)}, u32[]{:S(2)}, u32[]{:S(2)}) collective-permute-start(bf16[4,2,48,896]{3,2,1,0:T(8,128)(2,1)} %get-tuple-element.196), channel_id=1, source_target_pairs={{0,4},{4,0},{8,12},{12,8},{16,20},{20,16},{24,28},{28,24},{1,5},{5... | collective-permute-start | bytes 2064392 | tf_op jit(solution)/shard_map/ppermute | solution.py:563
  121.7 19.5 %collective-permute-start.12 = (bf16[4,2,48,640]{3,2,1,0:T(8,128)(2,1)}, bf16[4,2,48,640]{3,2,1,0:T(8,128)(2,1)}, u32[]{:S(2)}, u32[]{:S(2)}) collective-permute-start(bf16[4,2,48,640]{3,2,1,0:T(8,128)(2,1)} %get-tuple-element.195), channel_id=1, source_target_pairs={{0,2},{1,3},{2,0},{3,1},{4,6},{5,7},{6,4},{7,5},{8,10},{9,11},{10,... | collective-permute-start | bytes 1474568 | tf_op jit(solution)/shard_map/ppermute | solution.py:563
  141.2 22.5 %collective-permute-start.17 = (bf16[768,1536]{1,0:T(8,128)(2,1)}, bf16[768,1536]{1,0:T(8,128)(2,1)}, u32[]{:S(2)}, u32[]{:S(2)}) collective-permute-start(bf16[768,1536]{1,0:T(8,128)(2,1)} %get-tuple-element.212), channel_id=1, source_target_pairs={{0,1},{1,0},{2,3},{3,2},{4,5},{5,4},{6,7},{7,6},{8,9},{9,8},{10,11... | collective-permute-start | bytes 7077896 | tf_op jit(solution)/shard_map/ppermute | solution.py:563
  145.5 18.1 %collective-permute-start.16 = (bf16[4,2,48,896]{3,2,1,0:T(8,128)(2,1)}, bf16[4,2,48,896]{3,2,1,0:T(8,128)(2,1)S(1)}, u32[]{:S(2)}, u32[]{:S(2)}) collective-permute-start(bf16[4,2,48,896]{3,2,1,0:T(8,128)(2,1)} %get-tuple-element.211), channel_id=1, source_target_pairs={{0,4},{4,0},{8,12},{12,8},{16,20},{20,16},{24,28},{28,24},{1,5},{5... | collective-permute-start | bytes 2064392 | tf_op jit(solution)/shard_map/ppermute | solution.py:563
  146.1 17.5 %collective-permute-start.15 = (bf16[4,2,48,640]{3,2,1,0:T(8,128)(2,1)}, bf16[4,2,48,640]{3,2,1,0:T(8,128)(2,1)}, u32[]{:S(2)}, u32[]{:S(2)}) collective-permute-start(bf16[4,2,48,640]{3,2,1,0:T(8,128)(2,1)} %get-tuple-element.210), channel_id=1, source_target_pairs={{0,2},{1,3},{2,0},{3,1},{4,6},{5,7},{6,4},{7,5},{8,10},{9,11},{10,... | collective-permute-start | bytes 1474568 | tf_op jit(solution)/shard_map/ppermute | solution.py:563
  163.7 26.4 %collective-permute-start.20 = (bf16[768,1536]{1,0:T(8,128)(2,1)}, bf16[768,1536]{1,0:T(8,128)(2,1)}, u32[]{:S(2)}, u32[]{:S(2)}) collective-permute-start(bf16[768,1536]{1,0:T(8,128)(2,1)} %get-tuple-element.226), channel_id=1, source_target_pairs={{0,1},{1,0},{2,3},{3,2},{4,5},{5,4},{6,7},{7,6},{8,9},{9,8},{10,11... | collective-permute-start | bytes 7077896 | tf_op jit(solution)/shard_map/ppermute | solution.py:563
  168.0 22.1 %collective-permute-start.19 = (bf16[4,2,48,896]{3,2,1,0:T(8,128)(2,1)}, bf16[4,2,48,896]{3,2,1,0:T(8,128)(2,1)S(1)}, u32[]{:S(2)}, u32[]{:S(2)}) collective-permute-start(bf16[4,2,48,896]{3,2,1,0:T(8,128)(2,1)} %get-tuple-element.225), channel_id=1, source_target_pairs={{0,4},{4,0},{8,12},{12,8},{16,20},{20,16},{24,28},{28,24},{1,5},{5... | collective-permute-start | bytes 2064392 | tf_op jit(solution)/shard_map/ppermute | solution.py:563
  169.6 20.5 %collective-permute-start.18 = (bf16[4,2,48,640]{3,2,1,0:T(8,128)(2,1)}, bf16[4,2,48,640]{3,2,1,0:T(8,128)(2,1)}, u32[]{:S(2)}, u32[]{:S(2)}) collective-permute-start(bf16[4,2,48,640]{3,2,1,0:T(8,128)(2,1)} %get-tuple-element.224), channel_id=1, source_target_pairs={{0,2},{1,3},{2,0},{3,1},{4,6},{5,7},{6,4},{7,5},{8,10},{9,11},{10,... | collective-permute-start | bytes 1474568 | tf_op jit(solution)/shard_map/ppermute | solution.py:563
  190.1 40.7 %collective-permute-start.25 = (bf16[768,1536]{1,0:T(8,128)(2,1)}, bf16[768,1536]{1,0:T(8,128)(2,1)}, u32[]{:S(2)}, u32[]{:S(2)}) collective-permute-start(bf16[768,1536]{1,0:T(8,128)(2,1)} %get-tuple-element.242), channel_id=1, source_target_pairs={{0,1},{1,0},{2,3},{3,2},{4,5},{5,4},{6,7},{7,6},{8,9},{9,8},{10,11... | collective-permute-start | bytes 7077896 | tf_op jit(solution)/shard_map/ppermute | solution.py:563
  194.5 28.1 %collective-permute-start.22 = (bf16[4,2,48,896]{3,2,1,0:T(8,128)(2,1)}, bf16[4,2,48,896]{3,2,1,0:T(8,128)(2,1)}, u32[]{:S(2)}, u32[]{:S(2)}) collective-permute-start(bf16[4,2,48,896]{3,2,1,0:T(8,128)(2,1)} %get-tuple-element.239), channel_id=1, source_target_pairs={{0,4},{4,0},{8,12},{12,8},{16,20},{20,16},{24,28},{28,24},{1,5},{5... | collective-permute-start | bytes 2064392 | tf_op jit(solution)/shard_map/ppermute | solution.py:563
  195.0 27.6 %collective-permute-start.21 = (bf16[4,2,48,640]{3,2,1,0:T(8,128)(2,1)}, bf16[4,2,48,640]{3,2,1,0:T(8,128)(2,1)}, u32[]{:S(2)}, u32[]{:S(2)}) collective-permute-start(bf16[4,2,48,640]{3,2,1,0:T(8,128)(2,1)} %get-tuple-element.238), channel_id=1, source_target_pairs={{0,2},{1,3},{2,0},{3,1},{4,6},{5,7},{6,4},{7,5},{8,10},{9,11},{10,... | collective-permute-start | bytes 1474568 | tf_op jit(solution)/shard_map/ppermute | solution.py:563
  201.5 29.3 %collective-permute-start.24 = (bf16[4,3,48,896]{3,2,1,0:T(8,128)(2,1)}, bf16[4,3,48,896]{3,2,1,0:T(8,128)(2,1)}, u32[]{:S(2)}, u32[]{:S(2)}) collective-permute-start(bf16[4,3,48,896]{3,2,1,0:T(8,128)(2,1)} %get-tuple-element.241), channel_id=1, source_target_pairs={{0,2},{1,3},{2,0},{3,1},{4,6},{5,7},{6,4},{7,5},{8,10},{9,11},{10,... | collective-permute-start | bytes 3096584 | tf_op jit(solution)/shard_map/ppermute | solution.py:563
  203.1 25.3 %collective-permute-start.23 = (bf16[4,3,48,640]{3,2,1,0:T(8,128)(2,1)}, bf16[4,3,48,640]{3,2,1,0:T(8,128)(2,1)S(1)}, u32[]{:S(2)}, u32[]{:S(2)}) collective-permute-start(bf16[4,3,48,640]{3,2,1,0:T(8,128)(2,1)} %get-tuple-element.240), channel_id=1, source_target_pairs={{0,4},{4,0},{8,12},{12,8},{16,20},{20,16},{24,28},{28,24},{1,5},{5... | collective-permute-start | bytes 2211848 | tf_op jit(solution)/shard_map/ppermute | solution.py:563
  230.8 29.4 %collective-permute-start.30 = (bf16[768,1536]{1,0:T(8,128)(2,1)}, bf16[768,1536]{1,0:T(8,128)(2,1)}, u32[]{:S(2)}, u32[]{:S(2)}) collective-permute-start(bf16[768,1536]{1,0:T(8,128)(2,1)} %get-tuple-element.260), channel_id=1, source_target_pairs={{0,1},{1,0},{2,3},{3,2},{4,5},{5,4},{6,7},{7,6},{8,9},{9,8},{10,11... | collective-permute-start | bytes 7077896 | tf_op jit(solution)/shard_map/ppermute | solution.py:563
  235.1 25.1 %collective-permute-start.29 = (bf16[4,2,48,896]{3,2,1,0:T(8,128)(2,1)}, bf16[4,2,48,896]{3,2,1,0:T(8,128)(2,1)S(1)}, u32[]{:S(2)}, u32[]{:S(2)}) collective-permute-start(bf16[4,2,48,896]{3,2,1,0:T(8,128)(2,1)} %get-tuple-element.259), channel_id=1, source_target_pairs={{0,4},{4,0},{8,12},{12,8},{16,20},{20,16},{24,28},{28,24},{1,5},{5... | collective-permute-start | bytes 2064392 | tf_op jit(solution)/shard_map/ppermute | solution.py:563
  236.7 23.5 %collective-permute-start.28 = (bf16[4,2,48,640]{3,2,1,0:T(8,128)(2,1)}, bf16[4,2,48,640]{3,2,1,0:T(8,128)(2,1)}, u32[]{:S(2)}, u32[]{:S(2)}) collective-permute-start(bf16[4,2,48,640]{3,2,1,0:T(8,128)(2,1)} %get-tuple-element.258), channel_id=1, source_target_pairs={{0,2},{1,3},{2,0},{3,1},{4,6},{5,7},{6,4},{7,5},{8,10},{9,11},{10,... | collective-permute-start | bytes 1474568 | tf_op jit(solution)/shard_map/ppermute | solution.py:563
  240.5 19.6 %collective-permute-start.27 = (bf16[4,1,48,896]{3,2,1,0:T(8,128)(2,1)}, bf16[4,1,48,896]{3,2,1,0:T(8,128)(2,1)}, u32[]{:S(2)}, u32[]{:S(2)}) collective-permute-start(bf16[4,1,48,896]{3,2,1,0:T(8,128)(2,1)} %get-tuple-element.255), channel_id=1, source_target_pairs={{0,2},{1,3},{2,0},{3,1},{4,6},{5,7},{6,4},{7,5},{8,10},{9,11},{10,... | collective-permute-start | bytes 1032200 | tf_op jit(solution)/shard_map/ppermute | solution.py:563
  242.1 16.4 %collective-permute-start.26 = (bf16[4,1,48,640]{3,2,1,0:T(8,128)(2,1)}, bf16[4,1,48,640]{3,2,1,0:T(8,128)(2,1)}, u32[]{:S(2)}, u32[]{:S(2)}) collective-permute-start(bf16[4,1,48,640]{3,2,1,0:T(8,128)(2,1)} %get-tuple-element.254), channel_id=1, source_target_pairs={{0,4},{4,0},{8,12},{12,8},{16,20},{20,16},{24,28},{28,24},{1,5},{5... | collective-permute-start | bytes 737288 | tf_op jit(solution)/shard_map/ppermute | solution.py:563
  258.6 21.6 %collective-permute-start.31 = (bf16[2,3,48,1536]{3,2,1,0:T(8,128)(2,1)}, bf16[2,3,48,1536]{3,2,1,0:T(8,128)(2,1)}, u32[]{:S(2)}, u32[]{:S(2)}) collective-permute-start(bf16[2,3,48,1536]{3,2,1,0:T(8,128)(2,1)} %get-tuple-element.262), channel_id=1, source_target_pairs={{0,8},{4,12},{8,0},{12,4},{16,24},{20,28},{24,16},{28,20},{1,9},{5... | collective-permute-start | bytes 2654216 | tf_op jit(solution)/shard_map/ppermute | solution.py:563
  265.4 23.7 %collective-permute-start.35 = (bf16[4,2,48,896]{3,2,1,0:T(8,128)(2,1)}, bf16[4,2,48,896]{3,2,1,0:T(8,128)(2,1)}, u32[]{:S(2)}, u32[]{:S(2)}) collective-permute-start(bf16[4,2,48,896]{3,2,1,0:T(8,128)(2,1)} %get-tuple-element.272), channel_id=1, source_target_pairs={{0,4},{4,0},{8,12},{12,8},{16,20},{20,16},{24,28},{28,24},{1,5},{5... | collective-permute-start | bytes 2064392 | tf_op jit(solution)/shard_map/ppermute | solution.py:563
  267.1 21.2 %collective-permute-start.34 = (bf16[4,2,48,640]{3,2,1,0:T(8,128)(2,1)}, bf16[4,2,48,640]{3,2,1,0:T(8,128)(2,1)S(1)}, u32[]{:S(2)}, u32[]{:S(2)}) collective-permute-start(bf16[4,2,48,640]{3,2,1,0:T(8,128)(2,1)} %get-tuple-element.271), channel_id=1, source_target_pairs={{0,2},{1,3},{2,0},{3,1},{4,6},{5,7},{6,4},{7,5},{8,10},{9,11},{10,... | collective-permute-start | bytes 1474568 | tf_op jit(solution)/shard_map/ppermute | solution.py:563
  271.0 17.3 %collective-permute-start.33 = (bf16[4,1,48,896]{3,2,1,0:T(8,128)(2,1)}, bf16[4,1,48,896]{3,2,1,0:T(8,128)(2,1)S(1)}, u32[]{:S(2)}, u32[]{:S(2)}) collective-permute-start(bf16[4,1,48,896]{3,2,1,0:T(8,128)(2,1)} %get-tuple-element.268), channel_id=1, source_target_pairs={{0,2},{1,3},{2,0},{3,1},{4,6},{5,7},{6,4},{7,5},{8,10},{9,11},{10,... | collective-permute-start | bytes 1032200 | tf_op jit(solution)/shard_map/ppermute | solution.py:563
  272.6 15.1 %collective-permute-start.32 = (bf16[4,1,48,640]{3,2,1,0:T(8,128)(2,1)}, bf16[4,1,48,640]{3,2,1,0:T(8,128)(2,1)S(1)}, u32[]{:S(2)}, u32[]{:S(2)}) collective-permute-start(bf16[4,1,48,640]{3,2,1,0:T(8,128)(2,1)} %get-tuple-element.267), channel_id=1, source_target_pairs={{0,4},{4,0},{8,12},{12,8},{16,20},{20,16},{24,28},{28,24},{1,5},{5... | collective-permute-start | bytes 737288 | tf_op jit(solution)/shard_map/ppermute | solution.py:563
  292.0 29.8 %collective-permute-start.41 = (bf16[2,2,48,1536]{3,2,1,0:T(8,128)(2,1)}, bf16[2,2,48,1536]{3,2,1,0:T(8,128)(2,1)}, u32[]{:S(2)}, u32[]{:S(2)}) collective-permute-start(bf16[2,2,48,1536]{3,2,1,0:T(8,128)(2,1)} %get-tuple-element.297), channel_id=1, source_target_pairs={{0,8},{4,12},{8,0},{12,4},{16,24},{20,28},{24,16},{28,20},{1,9},{5... | collective-permute-start | bytes 1769480 | tf_op jit(solution)/shard_map/ppermute | solution.py:563
  292.5 29.3 %all-to-all-start = ((bf16[4,128,768]{2,1,0:T(8,128)(2,1)}), bf16[4,128,768]{2,1,0:T(8,128)(2,1)S(1)}, u32[]{:S(2)}, u32[]{:S(2)}) async-start(bf16[4,128,768]{2,1,0:T(8,128)(2,1)} %bitcast.136), calls=%async_computation | async-start | bytes 1572864 | tf_op jit(solution)/shard_map/all_to_all | solution.py:595
  298.4 23.3 %collective-permute-start.37 = (bf16[1,3,48,1536]{3,2,1,0:T(8,128)(2,1)}, bf16[1,3,48,1536]{3,2,1,0:T(8,128)(2,1)}, u32[]{:S(2)}, u32[]{:S(2)}) collective-permute-start(bf16[1,3,48,1536]{3,2,1,0:T(8,128)(2,1)} %get-tuple-element.281), channel_id=1, source_target_pairs={{0,16},{4,20},{8,24},{12,28},{16,0},{20,4},{24,8},{28,12},{1,17},{... | collective-permute-start | bytes 1327112 | tf_op jit(solution)/shard_map/ppermute | solution.py:563
  304.2 13.9 %collective-permute-start.39 = (bf16[4,1,48,896]{3,2,1,0:T(8,128)(2,1)}, bf16[4,1,48,896]{3,2,1,0:T(8,128)(2,1)S(1)}, u32[]{:S(2)}, u32[]{:S(2)}) collective-permute-start(bf16[4,1,48,896]{3,2,1,0:T(8,128)(2,1)} %get-tuple-element.287), channel_id=1, source_target_pairs={{0,2},{1,3},{2,0},{3,1},{4,6},{5,7},{6,4},{7,5},{8,10},{9,11},{10,... | collective-permute-start | bytes 1032200 | tf_op jit(solution)/shard_map/ppermute | solution.py:563
  306.2 11.9 %collective-permute-start.38 = (bf16[4,1,48,640]{3,2,1,0:T(8,128)(2,1)}, bf16[4,1,48,640]{3,2,1,0:T(8,128)(2,1)S(1)}, u32[]{:S(2)}, u32[]{:S(2)}) collective-permute-start(bf16[4,1,48,640]{3,2,1,0:T(8,128)(2,1)} %get-tuple-element.286), channel_id=1, source_target_pairs={{0,4},{4,0},{8,12},{12,8},{16,20},{20,16},{24,28},{28,24},{1,5},{5... | collective-permute-start | bytes 737288 | tf_op jit(solution)/shard_map/ppermute | solution.py:563
  308.1 10.0 %collective-permute-start.40 = (f32[2,24,768]{2,1,0:T(8,128)S(1)}, f32[2,24,768]{2,1,0:T(8,128)S(1)}, u32[]{:S(2)}, u32[]{:S(2)}) collective-permute-start(f32[2,24,768]{2,1,0:T(8,128)S(1)} %fusion.42), channel_id=1, source_target_pairs={{0,2},{1,3},{2,0},{3,1},{4,6},{5,7},{6,4},{7,5},{8,10},{9,11},{10,... | collective-permute-start | bytes 442376 | tf_op jit(solution)/shard_map/ppermute | solution.py:563
  324.3 15.3 %collective-permute-start.45 = (bf16[2,1,48,1536]{3,2,0,1:T(8,128)(2,1)}, bf16[2,1,48,1536]{3,2,0,1:T(8,128)(2,1)}, u32[]{:S(2)}, u32[]{:S(2)}) collective-permute-start(bf16[2,1,48,1536]{3,2,0,1:T(8,128)(2,1)} %bitcast.158), channel_id=1, source_target_pairs={{0,8},{4,12},{8,0},{12,4},{16,24},{20,28},{24,16},{28,20},{1,9},{5... | collective-permute-start | bytes 884744 | tf_op jit(solution)/shard_map/ppermute | solution.py:563
  326.1 19.8 %collective-permute-start.42 = (bf16[3,48,1536]{2,1,0:T(8,128)(2,1)S(1)}, bf16[3,48,1536]{2,1,0:T(8,128)(2,1)}, u32[]{:S(2)}, u32[]{:S(2)}) collective-permute-start(bf16[3,48,1536]{2,1,0:T(8,128)(2,1)S(1)} %add_bitcast_fusion), channel_id=1, source_target_pairs={{0,2},{1,3},{2,0},{3,1},{4,6},{5,7},{6,4},{7,5},{8,10},{9,11},{10,... | collective-permute-start | bytes 1327112 | tf_op jit(solution)/shard_map/ppermute | solution.py:563
  330.0 15.9 %collective-permute-start.44 = (bf16[1,2,48,1536]{3,2,1,0:T(8,128)(2,1)}, bf16[1,2,48,1536]{3,2,1,0:T(8,128)(2,1)S(1)}, u32[]{:S(2)}, u32[]{:S(2)}) collective-permute-start(bf16[1,2,48,1536]{3,2,1,0:T(8,128)(2,1)} %get-tuple-element.303), channel_id=1, source_target_pairs={{0,16},{4,20},{8,24},{12,28},{16,0},{20,4},{24,8},{28,12},{1,17},{... | collective-permute-start | bytes 884744 | tf_op jit(solution)/shard_map/ppermute | solution.py:563
  347.9 21.6 %collective-permute-start.46 = (bf16[3,96,1536]{2,1,0:T(8,128)(2,1)}, bf16[3,96,1536]{2,1,0:T(8,128)(2,1)}, u32[]{:S(2)}, u32[]{:S(2)}) collective-permute-start(bf16[3,96,1536]{2,1,0:T(8,128)(2,1)} %pad_maximum_fusion.tall), channel_id=1, source_target_pairs={{0,1},{1,0},{2,3},{3,2},{4,5},{5,4},{6,7},{7,6},{8,9},{9,8},{10,11... | collective-permute-start | bytes 2654216 | tf_op jit(solution)/shard_map/ppermute | solution.py:563
  348.0 21.6 %all-to-all-start.1 = ((bf16[4,128,768]{2,1,0:T(8,128)(2,1)}), bf16[4,128,768]{2,1,0:T(8,128)(2,1)S(1)}, u32[]{:S(2)}, u32[]{:S(2)}) async-start(bf16[4,128,768]{2,1,0:T(8,128)(2,1)} %bitcast.71), calls=%async_computation.1 | async-start | bytes 1572864 | tf_op jit(solution)/shard_map/all_to_all | solution.py:595
  352.2 17.3 %collective-permute-start.48 = (bf16[2,48,1536]{2,1,0:T(8,128)(2,1)}, bf16[2,48,1536]{2,1,0:T(8,128)(2,1)}, u32[]{:S(2)}, u32[]{:S(2)}) collective-permute-start(bf16[2,48,1536]{2,1,0:T(8,128)(2,1)} %add_bitcast_fusion.1), channel_id=1, source_target_pairs={{0,2},{1,3},{2,0},{3,1},{4,6},{5,7},{6,4},{7,5},{8,10},{9,11},{10,... | collective-permute-start | bytes 884744 | tf_op jit(solution)/shard_map/ppermute | solution.py:563
  356.0 9.8 %collective-permute-start.49 = (bf16[1,1,48,1536]{3,2,1,0:T(8,128)(2,1)}, bf16[1,1,48,1536]{3,2,1,0:T(8,128)(2,1)S(1)}, u32[]{:S(2)}, u32[]{:S(2)}) collective-permute-start(bf16[1,1,48,1536]{3,2,1,0:T(8,128)(2,1)} %get-tuple-element.315), channel_id=1, source_target_pairs={{0,16},{4,20},{8,24},{12,28},{16,0},{20,4},{24,8},{28,12},{1,17},{... | collective-permute-start | bytes 442376 | tf_op jit(solution)/shard_map/ppermute | solution.py:563
  357.1 9.6 %collective-permute-start.47 = (f32[2,24,768]{2,1,0:T(8,128)S(1)}, f32[2,24,768]{2,1,0:T(8,128)S(1)}, u32[]{:S(2)}, u32[]{:S(2)}) collective-permute-start(f32[2,24,768]{2,1,0:T(8,128)S(1)} %add.313), channel_id=1, source_target_pairs={{0,8},{4,12},{8,0},{12,4},{16,24},{20,28},{24,16},{28,20},{1,9},{5... | collective-permute-start | bytes 442376 | tf_op jit(solution)/shard_map/ppermute | solution.py:563
  370.7 12.2 %collective-permute-start.51 = (bf16[2,96,1536]{2,1,0:T(8,128)(2,1)S(1)}, bf16[2,96,1536]{2,1,0:T(8,128)(2,1)S(1)}, u32[]{:S(2)}, u32[]{:S(2)}) collective-permute-start(bf16[2,96,1536]{2,1,0:T(8,128)(2,1)S(1)} %pad_maximum_fusion.1.low), channel_id=1, source_target_pairs={{0,1},{1,0},{2,3},{3,2},{4,5},{5,4},{6,7},{7,6},{8,9},{9,8},{10,11... | collective-permute-start | bytes 1769480 | tf_op jit(solution)/shard_map/ppermute | solution.py:563
  370.9 6.7 %collective-permute-start.52 = (bf16[1,48,1536]{2,1,0:T(8,128)(2,1)S(1)}, bf16[1,48,1536]{2,1,0:T(8,128)(2,1)S(1)}, u32[]{:S(2)}, u32[]{:S(2)}) collective-permute-start(bf16[1,48,1536]{2,1,0:T(8,128)(2,1)S(1)} %add_bitcast_fusion.2.own), channel_id=1, source_target_pairs={{0,2},{1,3},{2,0},{3,1},{4,6},{5,7},{6,4},{7,5},{8,10},{9,11},{10,... | collective-permute-start | bytes 442376 | tf_op jit(solution)/shard_map/ppermute | solution.py:563
  371.5 8.5 %collective-permute-start.54 = (bf16[1,48,1536]{2,1,0:T(8,128)(2,1)S(1)}, bf16[1,48,1536]{2,1,0:T(8,128)(2,1)}, u32[]{:S(2)}, u32[]{:S(2)}) collective-permute-start(bf16[1,48,1536]{2,1,0:T(8,128)(2,1)S(1)} %add_bitcast_fusion.2.own), channel_id=1, source_target_pairs={{0,3},{1,2},{2,1},{3,0},{4,7},{5,6},{6,5},{7,4},{8,11},{9,10},{10,... | collective-permute-start | bytes 442376 | tf_op jit(solution)/shard_map/ppermute | solution.py:813
  373.1 9.9 %collective-permute-start.50 = (f32[2,24,768]{2,1,0:T(8,128)S(1)}, f32[2,24,768]{2,1,0:T(8,128)S(1)}, u32[]{:S(2)}, u32[]{:S(2)}) collective-permute-start(f32[2,24,768]{2,1,0:T(8,128)S(1)} %add.315), channel_id=1, source_target_pairs={{0,16},{4,20},{8,24},{12,28},{16,0},{20,4},{24,8},{28,12},{1,17},{... | collective-permute-start | bytes 442376 | tf_op jit(solution)/shard_map/ppermute | solution.py:563
  (81 other events, 643.3 us)

commit v2 on v1

--- a/solution.py
+++ b/solution.py
@@ -1034,13 +1034,10 @@
     grad = flow.tick(grad)
     flow.begin("small", reduce_small(jnp.stack(sums)))
     grad = flow.tick(grad)
-    flow.begin("input", swap_rows(grad.reshape(batch_rows, part_len, width)))
-    flow.tick()
-    low = flow.tick(low)
-    flow.begin("output", swap_rows(low.reshape(batch_rows, part_len, width)))
+    pieces = [x.reshape(batch_rows, part_len, width) for x in (low, grad)]
+    flow.begin("rows", swap_rows(jnp.stack(pieces, axis=1)))
     flow.finish()
-    layer_output = flow.results["output"]
-    returned = flow.results["input"]
+    layer_output, returned = (flow.results["rows"][:, i] for i in range(2))
     shares = lax.axis_size("batch")
     share = lax.axis_index("batch")
     joint_grad, mix_grad, expand_grad, shrink_grad = assemble(

time: 396 us -> 390 us (0.985)
  starting transfers between devices: 62.2 us -> 57.5 us
  transfers between devices with their start and end apart: 57 -> 56, of which waited for: 22 -> 20; matrix products, arithmetic and copies ran while one was open for 2% -> 3% of each run, Pallas kernels for 38% -> 39%
where the time goes in v2:
time: 390 us; the launch traced here: 386 us
  Pallas kernels  188 us (48%)
  waiting for transfers between devices  84.3 us (22%)
  starting transfers between devices  57.5 us (15%)
  matrix products  26.6 us (7%)
  other arithmetic  21 us (5%)
  local copies, waits for them, and re-layouts  6.94 us (2%)
    ppermute x43, waiting for transfers between devices, flip(): return lax.ppermute(x, axis, [(i, i ^ 1 << bit) for i in range(count)])  64.7 us
    pallas_call x16, Pallas kernels, add_blocks(): pl.pallas_call(partial(add_blocks_kernel, kernel, (len(ins), len(outs))),...  55.7 us
    ppermute x43, starting transfers between devices, flip(): return lax.ppermute(x, axis, [(i, i ^ 1 << bit) for i in range(count)])  39.1 us
    pallas_call x2, Pallas kernels, expand_backward(): pl.pallas_call(partial(expand_backward_kernel, steps, level), grid_spec=p...  37.3 us
    pallas_call x2, Pallas kernels, attention_backward(): pl.pallas_call(attention_backward_kernel, grid_spec=pltpu.PrefetchScalarG...  36.1 us
    dot_general x9, matrix products, dot(): return lax.dot_general(a, b, dims, preferred_element_type=jnp.float32)  26.6 us
    pallas_call x2, Pallas kernels, shrink_backward(): pl.pallas_call(partial(shrink_backward_kernel, shard_columns), grid_spec=...  17 us
    pallas_call x2, Pallas kernels, joint_backward(): pl.pallas_call(partial(joint_backward_kernel, level), grid_spec=pltpu.Pre...  16.6 us
  transfers between devices with their start and end apart: 56, of which 20 were waited for; matrix products, arithmetic and copies ran while one was open for 3% of the time, Pallas kernels for 39%

profile of v2, /device:TPU:0, one launch (start us, length us, event | category | flops | bytes accessed | tf_op | source)
XLA Modules:
  0.0 386.5 jit_solution(11119281085655848280)
XLA Ops:
  2.6 2.6 collective-permute-start.1
  6.6 4.3 %collective-permute-done.1 = bf16[1,128,768]{2,1,0:T(8,128)(2,1)S(1)} collective-permute-done((bf16[1,128,768]{2,1,0:T(8,128)(2,1)S(1)}, bf16[1,128,768]{2,1,0:T(8,128)(2,1)S(1)}, u32[]{:S(2)}, u32[]{:S(2)}) %collective-permute-start.1) | collective-permute-done | bytes 196640 | tf_op jit(solution)/shard_map/ppermute | solution.py:584
  10.9 3.7 collective-permute-done.2
  14.7 4.3 %fusion.22.qkv_ref.qkv_any = bf16[512,2304]{1,0:T(8,128)(2,1)S(1)} fusion(bf16[512,768]{1,0:T(8,128)(2,1)S(1)} %bitcast.146, bf16[2,768,2304]{2,1,0:T(8,128)(2,1)} %weight_any.3, f32[2304]{0:T(1024)S(1)} %get-tuple-element.436), kind=kOutput, calls=%fused_computation.30 | convolution fusion | flops 1814298624 | bytes 6693888 | tf_op jit(solution)/shard_map/dot_general | solution.py:47
  19.1 8.0 %shard_map.220 = (bf16[512,768]{1,0:T(8,128)(2,1)S(1)}, f32[6,8,512]{2,1,0:T(8,128)S(1)}) custom-call(bf16[512,2304]{1,0:T(8,128)(2,1)S(1)} %fusion.22.qkv_ref.qkv_any, s32[512,1]{1,0:T(8,128)S(1)} %copy.41.column_ids_ref, s32[1,512]{1,0:T(1,128)S(1)} %bitcast.141), custom_call_target="tpu_custom_call" | custom-call | flops 8000000000 | bytes 16000000 | tf_op jit(solution)/shard_map/pallas_call | solution.py:83
  28.9 6.1 %fusion.9 = (bf16[512,3072]{1,0:T(8,128)(2,1)}, bf16[512,3072]{1,0:T(8,128)(2,1)S(1)}) fusion(f32[3072]{0:T(1024)S(1)} %bitcast.153, bf16[512,768]{1,0:T(8,128)(2,1)S(1)} %get-tuple-element.400.middle_ref, bf16[2,768,3072]{2,1,0:T(8,128)(2,1)S(1)} %bitcast.160), kind=kOutput, calls=%fused_computation.11 | convolution fusion | flops 2434793472 | bytes 11808768 | tf_op jit(solution)/shard_map/dot_general | solution.py:47
  35.1 2.7 fusion.45
  42.7 7.7 %shard_map.221 = (bf16[512,768]{1,0:T(8,128)(2,1)S(1)}, f32[6,8,512]{2,1,0:T(8,128)S(1)}) custom-call(bf16[512,2304]{1,0:T(8,128)(2,1)S(1)} %fusion.23.qkv_ref.qkv_any, s32[512,1]{1,0:T(8,128)S(1)} %copy.41.column_ids_ref, s32[1,512]{1,0:T(1,128)S(1)} %bitcast.142), custom_call_target="tpu_custom_call" | custom-call | flops 8000000000 | bytes 16000000 | tf_op jit(solution)/shard_map/pallas_call | solution.py:83
  52.1 6.7 %fusion.4 = (bf16[512,3072]{1,0:T(8,128)(2,1)}, bf16[512,3072]{1,0:T(8,128)(2,1)S(1)}) fusion(f32[3072]{0:T(1024)S(1)} %bitcast.152, bf16[512,768]{1,0:T(8,128)(2,1)S(1)} %get-tuple-element.396.middle_ref, bf16[2,768,3072]{2,1,0:T(8,128)(2,1)S(1)} %bitcast.160), kind=kOutput, calls=%fused_computation.6 | convolution fusion | flops 2434793472 | bytes 11808768 | tf_op jit(solution)/shard_map/dot_general | solution.py:47
  58.8 2.7 fusion.47
  63.6 2.6 collective-permute-start.3
  73.8 2.6 collective-permute-done.5
  78.0 3.1 collective-permute-done.6
  83.3 4.1 %shard_map.222 = (f32[1,1]{1,0:T(1,128)}, f32[512,768]{1,0:T(8,128)}) custom-call(s32[1]{0:T(128)} %bitcast.5.place_ref, s32[8]{0:T(128)} %copy-done.34, bf16[128,768]{1,0:T(8,128)(2,1)} %copy-done.35, bf16[128,768]{1,0:T(8,128)(2,1)} %copy-done.46, s32[1,128]{1,0:T(1,128)} %bitcast.170, bf16[4,128,768]{2,1,0:T(8,128)(2,1)} %own_cot_ref, ...), custom_call_target="tpu_custom_call" | custom-call | flops 4000000000 | bytes 8000000 | tf_op jit(solution)/shard_map/pallas_call | solution.py:969
  87.4 8.5 %shard_map.223 = (bf16[768,1536]{1,0:T(8,128)(2,1)}, bf16[768,1536]{1,0:T(8,128)(2,1)}, f32[512,768]{1,0:T(8,128)}, bf16[512,768]{1,0:T(8,128)(2,1)}, f32[8,768]{1,0:T(8,128)}) custom-call(s32[1]{0:T(128)} %bitcast.4.bit_ref.half_ref, f32[512,768]{1,0:T(8,128)} %get-tuple-element.178.grad_ref, f32[512,768]{1,0:T(8,128)} %get-tuple-element.395.normed_ref, ...), custom_call_target="tpu_custom_call" | custom-call | flops 6000000000 | bytes 12000000 | tf_op jit(solution)/shard_map/pallas_call | solution.py:163
  96.1 18.5 %shard_map.224 = (bf16[768,1536]{1,0:T(8,128)(2,1)}, bf16[768,1536]{1,0:T(8,128)(2,1)}, f32[512,768]{1,0:T(8,128)}, bf16[512,768]{1,0:T(8,128)(2,1)}, bf16[512,768]{1,0:T(8,128)(2,1)}, /*index=5*/f32[8,768]{1,0:T(8,128)}) custom-call(s32[1]{0:T(128)} %bitcast.4.bit_ref.half_ref, bf16[512,768]{1,0:T(8,128)(2,1)} %get-tuple-element.180.low_ref, ...), custom_call_target="tpu_custom_call" | custom-call | flops 16000000000 | bytes 32000000 | tf_op jit(solution)/shard_map/pallas_call | solution.py:275
  115.7 4.2 %shard_map.225 = (bf16[4,2,48,640]{3,2,1,0:T(8,128)(2,1)}, bf16[4,2,48,640]{3,2,1,0:T(8,128)(2,1)}, bf16[4,2,48,896]{3,2,1,0:T(8,128)(2,1)}, bf16[4,2,48,896]{3,2,1,0:T(8,128)(2,1)}) custom-call(s32[2]{0:T(128)} %pad_add_fusion.bits_ref, bf16[4,2,2,48,1536]{4,3,2,1,0:T(8,128)(2,1)} %bitcast.174, bf16[4,2,2,48,1536]{4,3,2,1,0:T(8,128)(2,1)} %bitcast.28.refs_1_), custom_call_target="tpu_custom_call" | custom-call | flops 2000000000 | bytes 4000000 | tf_op jit(solution)/shard_map/pallas_call | solution.py:686
  123.0 18.0 %shard_map.226 = (bf16[512,2304]{1,0:T(8,128)(2,1)}, bf16[768,1536]{1,0:T(8,128)(2,1)}, f32[8,768]{1,0:T(8,128)}) custom-call(s32[1]{0:T(128)S(6)} %sub.48.half_ref, f32[6,8,512]{2,1,0:T(8,128)} %copy-done.7, s32[512,1]{1,0:T(8,128)} %copy-done, s32[1,512]{1,0:T(1,128)} %bitcast.143, bf16[512,2304]{1,0:T(8,128)(2,1)} %copy-done.5, ...), custom_call_target="tpu_custom_call" | custom-call | flops 14000000000 | bytes 28000000 | tf_op jit(solution)/shard_map/pallas_call | solution.py:406
  141.1 4.2 %shard_map.227 = (bf16[4,2,48,640]{3,2,1,0:T(8,128)(2,1)}, bf16[4,2,48,640]{3,2,1,0:T(8,128)(2,1)}, bf16[4,2,48,896]{3,2,1,0:T(8,128)(2,1)}, bf16[4,2,48,896]{3,2,1,0:T(8,128)(2,1)}) custom-call(s32[2]{0:T(128)} %pad_add_fusion.bits_ref, bf16[4,2,2,48,1536]{4,3,2,1,0:T(8,128)(2,1)} %bitcast.173, bf16[4,2,2,48,1536]{4,3,2,1,0:T(8,128)(2,1)} %bitcast.30.refs_1_), custom_call_target="tpu_custom_call" | custom-call | flops 2000000000 | bytes 4000000 | tf_op jit(solution)/shard_map/pallas_call | solution.py:686
  146.4 8.5 %shard_map.228 = (bf16[768,1536]{1,0:T(8,128)(2,1)}, f32[512,768]{1,0:T(8,128)}) custom-call(s32[1]{0:T(128)} %bitcast.4.bit_ref.half_ref, bf16[512,768]{1,0:T(8,128)(2,1)} %copy-done.2, bf16[512,768]{1,0:T(8,128)(2,1)} %copy-done.12, bf16[512,2304]{1,0:T(8,128)(2,1)} %get-tuple-element.202.joint_any, bf16[512,768]{1,0:T(8,128)(2,1)} %get-tuple-element.190.branch_any, ...), custom_call_target="tpu_custom_call" | custom-call | flops 7000000000 | bytes 14000000 | tf_op jit(solution)/shard_map/pallas_call | solution.py:466
  154.9 8.5 %shard_map.229 = (bf16[768,1536]{1,0:T(8,128)(2,1)}, bf16[768,1536]{1,0:T(8,128)(2,1)}, f32[512,768]{1,0:T(8,128)}, bf16[512,768]{1,0:T(8,128)(2,1)}, f32[8,768]{1,0:T(8,128)}) custom-call(s32[1]{0:T(128)} %bitcast.4.bit_ref.half_ref, f32[512,768]{1,0:T(8,128)} %get-tuple-element.204.grad_ref, f32[512,768]{1,0:T(8,128)} %get-tuple-element.399.normed_ref, ...), custom_call_target="tpu_custom_call" | custom-call | flops 6000000000 | bytes 12000000 | tf_op jit(solution)/shard_map/pallas_call | solution.py:163
  163.5 4.2 %shard_map.230 = (bf16[4,2,48,640]{3,2,1,0:T(8,128)(2,1)}, bf16[4,2,48,640]{3,2,1,0:T(8,128)(2,1)}, bf16[4,2,48,896]{3,2,1,0:T(8,128)(2,1)}, bf16[4,2,48,896]{3,2,1,0:T(8,128)(2,1)}) custom-call(s32[2]{0:T(128)} %pad_add_fusion.bits_ref, bf16[4,2,2,48,1536]{4,3,2,1,0:T(8,128)(2,1)} %bitcast.176, bf16[4,2,2,48,1536]{4,3,2,1,0:T(8,128)(2,1)} %bitcast.34.refs_1_), custom_call_target="tpu_custom_call" | custom-call | flops 2000000000 | bytes 4000000 | tf_op jit(solution)/shard_map/pallas_call | solution.py:686
  170.8 18.8 %shard_map.231 = (bf16[768,1536]{1,0:T(8,128)(2,1)}, bf16[768,1536]{1,0:T(8,128)(2,1)}, f32[512,768]{1,0:T(8,128)}, bf16[512,768]{1,0:T(8,128)(2,1)}, bf16[512,768]{1,0:T(8,128)(2,1)}, /*index=5*/f32[8,768]{1,0:T(8,128)}) custom-call(s32[1]{0:T(128)} %bitcast.4.bit_ref.half_ref, bf16[512,768]{1,0:T(8,128)(2,1)} %get-tuple-element.217.low_ref, ...), custom_call_target="tpu_custom_call" | custom-call | flops 16000000000 | bytes 32000000 | tf_op jit(solution)/shard_map/pallas_call | solution.py:275
  189.7 4.2 %shard_map.234 = (bf16[4,2,48,640]{3,2,1,0:T(8,128)(2,1)}, bf16[4,2,48,640]{3,2,1,0:T(8,128)(2,1)}, bf16[4,2,48,896]{3,2,1,0:T(8,128)(2,1)}, bf16[4,2,48,896]{3,2,1,0:T(8,128)(2,1)}) custom-call(s32[2]{0:T(128)} %pad_add_fusion.bits_ref, bf16[4,2,2,48,1536]{4,3,2,1,0:T(8,128)(2,1)} %bitcast.172, bf16[4,2,2,48,1536]{4,3,2,1,0:T(8,128)(2,1)} %bitcast.39.refs_1_), custom_call_target="tpu_custom_call" | custom-call | flops 2000000000 | bytes 4000000 | tf_op jit(solution)/shard_map/pallas_call | solution.py:686
  195.1 5.9 %shard_map.232 = (bf16[4,3,48,640]{3,2,1,0:T(8,128)(2,1)}, bf16[4,3,48,640]{3,2,1,0:T(8,128)(2,1)}, bf16[4,3,48,896]{3,2,1,0:T(8,128)(2,1)}, bf16[4,3,48,896]{3,2,1,0:T(8,128)(2,1)}) custom-call(s32[2]{0:T(128)} %pad_add_fusion.bits_ref, bf16[4,2,48,640]{3,2,1,0:T(8,128)(2,1)} %get-tuple-element.187.refs_0_, ...), custom_call_target="tpu_custom_call" | custom-call | flops 2000000000 | bytes 4000000 | tf_op jit(solution)/shard_map/pallas_call | solution.py:686
  204.0 18.1 %shard_map.233 = (bf16[512,2304]{1,0:T(8,128)(2,1)}, bf16[768,1536]{1,0:T(8,128)(2,1)}, f32[8,768]{1,0:T(8,128)}) custom-call(s32[1]{0:T(128)S(6)} %sub.48.half_ref, f32[6,8,512]{2,1,0:T(8,128)} %copy-done.6, s32[512,1]{1,0:T(8,128)} %copy-done, s32[1,512]{1,0:T(1,128)} %bitcast.144, bf16[512,2304]{1,0:T(8,128)(2,1)} %copy-done.4, ...), custom_call_target="tpu_custom_call" | custom-call | flops 14000000000 | bytes 28000000 | tf_op jit(solution)/shard_map/pallas_call | solution.py:406
  222.1 5.8 %collective-permute-done.23 = bf16[4,3,48,640]{3,2,1,0:T(8,128)(2,1)} collective-permute-done((bf16[4,3,48,640]{3,2,1,0:T(8,128)(2,1)}, bf16[4,3,48,640]{3,2,1,0:T(8,128)(2,1)}, u32[]{:S(2)}, u32[]{:S(2)}) %collective-permute-start.23) | collective-permute-done | bytes 737312 | tf_op jit(solution)/shard_map/ppermute | solution.py:563
  230.3 4.2 %shard_map.238 = (bf16[4,2,48,640]{3,2,1,0:T(8,128)(2,1)}, bf16[4,2,48,640]{3,2,1,0:T(8,128)(2,1)}, bf16[4,2,48,896]{3,2,1,0:T(8,128)(2,1)}, bf16[4,2,48,896]{3,2,1,0:T(8,128)(2,1)}) custom-call(s32[2]{0:T(128)} %pad_add_fusion.bits_ref, bf16[4,2,2,48,1536]{4,3,2,1,0:T(8,128)(2,1)} %bitcast.171, bf16[4,2,2,48,1536]{4,3,2,1,0:T(8,128)(2,1)} %bitcast.45.refs_1_), custom_call_target="tpu_custom_call" | custom-call | flops 2000000000 | bytes 4000000 | tf_op jit(solution)/shard_map/pallas_call | solution.py:686
  236.6 3.4 shard_map.237
  242.1 8.1 %shard_map.236 = (bf16[768,1536]{1,0:T(8,128)(2,1)}, bf16[512,768]{1,0:T(8,128)(2,1)}) custom-call(s32[1]{0:T(128)} %bitcast.4.bit_ref.half_ref, bf16[512,768]{1,0:T(8,128)(2,1)} %copy-done.3, bf16[512,768]{1,0:T(8,128)(2,1)} %bitcast.149, bf16[512,2304]{1,0:T(8,128)(2,1)} %get-tuple-element.245.joint_any, bf16[512,768]{1,0:T(8,128)(2,1)} %get-tuple-element.231.branch_any, ...), custom_call_target="tpu_custom_call" | custom-call | flops 7000000000 | bytes 14000000 | tf_op jit(solution)/shard_map/pallas_call | solution.py:466
  250.3 3.0 shard_map.235
  253.3 4.8 %collective-permute-done.26 = bf16[4,1,48,640]{3,2,1,0:T(8,128)(2,1)} collective-permute-done((bf16[4,1,48,640]{3,2,1,0:T(8,128)(2,1)}, bf16[4,1,48,640]{3,2,1,0:T(8,128)(2,1)}, u32[]{:S(2)}, u32[]{:S(2)}) %collective-permute-start.26) | collective-permute-done | bytes 245792 | tf_op jit(solution)/shard_map/ppermute | solution.py:563
  259.7 4.3 %shard_map.240 = (bf16[4,2,48,640]{3,2,1,0:T(8,128)(2,1)}, bf16[4,2,48,640]{3,2,1,0:T(8,128)(2,1)}, bf16[4,2,48,896]{3,2,1,0:T(8,128)(2,1)}, bf16[4,2,48,896]{3,2,1,0:T(8,128)(2,1)}) custom-call(s32[2]{0:T(128)} %pad_add_fusion.bits_ref, bf16[4,2,2,48,1536]{4,3,2,1,0:T(8,128)(2,1)} %bitcast.175, bf16[4,2,2,48,1536]{4,3,2,1,0:T(8,128)(2,1)} %bitcast.47.refs_1_), custom_call_target="tpu_custom_call" | custom-call | flops 2000000000 | bytes 4000000 | tf_op jit(solution)/shard_map/pallas_call | solution.py:686
  267.5 3.3 shard_map.239
  273.0 6.6 %collective-permute-done.31 = bf16[2,3,48,1536]{3,2,1,0:T(8,128)(2,1)} collective-permute-done((bf16[2,3,48,1536]{3,2,1,0:T(8,128)(2,1)}, bf16[2,3,48,1536]{3,2,1,0:T(8,128)(2,1)}, u32[]{:S(2)}, u32[]{:S(2)}) %collective-permute-start.31) | collective-permute-done | bytes 884768 | tf_op jit(solution)/shard_map/ppermute | solution.py:563
  279.6 6.7 %collective-permute-done.32 = bf16[4,1,48,640]{3,2,1,0:T(8,128)(2,1)S(1)} collective-permute-done((bf16[4,1,48,640]{3,2,1,0:T(8,128)(2,1)}, bf16[4,1,48,640]{3,2,1,0:T(8,128)(2,1)S(1)}, u32[]{:S(2)}, u32[]{:S(2)}) %collective-permute-start.32) | collective-permute-done | bytes 245792 | tf_op jit(solution)/shard_map/ppermute | solution.py:563
  288.3 2.6 pad_maximum_fusion
  290.8 4.4 %all-to-all-start = ((bf16[4,2,128,768]{3,2,1,0:T(8,128)(2,1)}), bf16[4,2,128,768]{3,2,1,0:T(8,128)(2,1)}, u32[]{:S(2)}, u32[]{:S(2)}) async-start(bf16[4,2,128,768]{3,2,1,0:T(8,128)(2,1)} %pad_maximum_fusion), calls=%async_computation | async-start | bytes 3145728 | tf_op jit(solution)/shard_map/all_to_all | solution.py:595
  295.2 2.7 shard_map.243
  303.2 3.3 shard_map.242
  310.2 15.5 %collective-permute-done.40 = f32[2,24,768]{2,1,0:T(8,128)S(1)} collective-permute-done((f32[2,24,768]{2,1,0:T(8,128)S(1)}, f32[2,24,768]{2,1,0:T(8,128)S(1)}, u32[]{:S(2)}, u32[]{:S(2)}) %collective-permute-start.40) | collective-permute-done | bytes 147488 | tf_op jit(solution)/shard_map/ppermute | solution.py:563
  337.1 4.6 %collective-permute-done.43 = f32[2,24,768]{2,1,0:T(8,128)S(1)} collective-permute-done((f32[2,24,768]{2,1,0:T(8,128)S(1)}, f32[2,24,768]{2,1,0:T(8,128)S(1)}, u32[]{:S(2)}, u32[]{:S(2)}) %collective-permute-start.43) | collective-permute-done | bytes 147488 | tf_op jit(solution)/shard_map/ppermute | solution.py:563
  341.7 7.2 %collective-permute-done.44 = bf16[1,2,48,1536]{3,2,1,0:T(8,128)(2,1)S(1)} collective-permute-done((bf16[1,2,48,1536]{3,2,1,0:T(8,128)(2,1)}, bf16[1,2,48,1536]{3,2,1,0:T(8,128)(2,1)S(1)}, u32[]{:S(2)}, u32[]{:S(2)}) %collective-permute-start.44) | collective-permute-done | bytes 294944 | tf_op jit(solution)/shard_map/ppermute | solution.py:563
  354.4 3.8 collective-permute-start.47
  358.9 5.8 %collective-permute-done.49 = bf16[1,1,48,1536]{3,2,1,0:T(8,128)(2,1)S(1)} collective-permute-done((bf16[1,1,48,1536]{3,2,1,0:T(8,128)(2,1)}, bf16[1,1,48,1536]{3,2,1,0:T(8,128)(2,1)S(1)}, u32[]{:S(2)}, u32[]{:S(2)}) %collective-permute-start.49) | collective-permute-done | bytes 147488 | tf_op jit(solution)/shard_map/ppermute | solution.py:563
  369.3 3.0 bitcast_convert_fusion
  375.0 2.7 collective-permute-done.50
  380.9 5.3 %shard_map.247 = (f32[2,96,2304]{2,1,0:T(8,128)}, f32[2,96,768]{2,1,0:T(8,128)}, f32[2,96,3072]{2,1,0:T(8,128)}, f32[2,384,768]{2,1,0:T(8,128)}) custom-call(s32[2]{0:T(128)} %pad_add_fusion.1.bits_ref, bf16[3,96,1536]{2,1,0:T(8,128)(2,1)} %pad_maximum_fusion.1.tall, bf16[3,96,1536]{2,1,0:T(8,128)(2,1)} %collective-permute-done.46.tall_got, ...), custom_call_target="tpu_custom_call" | custom-call | flops 5000000000 | bytes 10000000 | tf_op jit(solution)/shard_map/pallas_call | solution.py:880
  (294 shorter events, 89.9 us)
Async XLA Ops:
  2.6 8.3 %collective-permute-start.1 = (bf16[1,128,768]{2,1,0:T(8,128)(2,1)S(1)}, bf16[1,128,768]{2,1,0:T(8,128)(2,1)S(1)}, u32[]{:S(2)}, u32[]{:S(2)}) collective-permute-start(bf16[1,128,768]{2,1,0:T(8,128)(2,1)S(1)} %get-tuple-element.416), channel_id=1, source_target_pairs={{0,2},{1,3},{2,0},{3,1},{4,6},{5,7},{6,4},{7,5},{8,10},{9,11},{10,... | collective-permute-start | bytes 589832 | tf_op jit(solution)/shard_map/ppermute | solution.py:584
  5.2 9.4 %collective-permute-start.2 = (bf16[1,128,768]{2,1,0:T(8,128)(2,1)S(1)}, bf16[1,128,768]{2,1,0:T(8,128)(2,1)S(1)}, u32[]{:S(2)}, u32[]{:S(2)}) collective-permute-start(bf16[1,128,768]{2,1,0:T(8,128)(2,1)S(1)} %get-tuple-element.413), channel_id=1, source_target_pairs={{0,3},{1,2},{2,1},{3,0},{4,7},{5,6},{6,5},{7,4},{8,11},{9,10},{10,... | collective-permute-start | bytes 589832 | tf_op jit(solution)/shard_map/ppermute | solution.py:584
  66.3 14.9 %collective-permute-start.10 = (bf16[1,128,768]{2,1,0:T(8,128)(2,1)S(1)}, bf16[1,128,768]{2,1,0:T(8,128)(2,1)S(1)}, u32[]{:S(2)}, u32[]{:S(2)}) collective-permute-start(bf16[1,128,768]{2,1,0:T(8,128)(2,1)S(1)} %get-tuple-element.410), channel_id=1, source_target_pairs={{0,3},{1,2},{2,1},{3,0},{4,7},{5,6},{6,5},{7,4},{8,11},{9,10},{10,... | collective-permute-start | bytes 589832 | tf_op jit(solution)/shard_map/ppermute | solution.py:584
  67.5 13.8 %collective-permute-start.8 = (bf16[1,128,768]{2,1,0:T(8,128)(2,1)S(1)}, bf16[1,128,768]{2,1,0:T(8,128)(2,1)S(1)}, u32[]{:S(2)}, u32[]{:S(2)}) collective-permute-start(bf16[1,128,768]{2,1,0:T(8,128)(2,1)S(1)} %get-tuple-element.412), channel_id=1, source_target_pairs={{0,1},{1,0},{2,3},{3,2},{4,5},{5,4},{6,7},{7,6},{8,9},{9,8},{10,11... | collective-permute-start | bytes 589832 | tf_op jit(solution)/shard_map/ppermute | solution.py:584
  68.0 13.3 %collective-permute-start.9 = (bf16[1,128,768]{2,1,0:T(8,128)(2,1)S(1)}, bf16[1,128,768]{2,1,0:T(8,128)(2,1)S(1)}, u32[]{:S(2)}, u32[]{:S(2)}) collective-permute-start(bf16[1,128,768]{2,1,0:T(8,128)(2,1)S(1)} %get-tuple-element.411), channel_id=1, source_target_pairs={{0,2},{1,3},{2,0},{3,1},{4,6},{5,7},{6,4},{7,5},{8,10},{9,11},{10,... | collective-permute-start | bytes 589832 | tf_op jit(solution)/shard_map/ppermute | solution.py:584
  96.0 18.7 %collective-permute-start.11 = (bf16[768,1536]{1,0:T(8,128)(2,1)}, bf16[768,1536]{1,0:T(8,128)(2,1)}, u32[]{:S(2)}, u32[]{:S(2)}) collective-permute-start(bf16[768,1536]{1,0:T(8,128)(2,1)} %get-tuple-element.185), channel_id=1, source_target_pairs={{0,1},{1,0},{2,3},{3,2},{4,5},{5,4},{6,7},{7,6},{8,9},{9,8},{10,11... | collective-permute-start | bytes 7077896 | tf_op jit(solution)/shard_map/ppermute | solution.py:563
  114.6 26.4 %collective-permute-start.14 = (bf16[768,1536]{1,0:T(8,128)(2,1)}, bf16[768,1536]{1,0:T(8,128)(2,1)}, u32[]{:S(2)}, u32[]{:S(2)}) collective-permute-start(bf16[768,1536]{1,0:T(8,128)(2,1)} %get-tuple-element.195), channel_id=1, source_target_pairs={{0,1},{1,0},{2,3},{3,2},{4,5},{5,4},{6,7},{7,6},{8,9},{9,8},{10,11... | collective-permute-start | bytes 7077896 | tf_op jit(solution)/shard_map/ppermute | solution.py:563
  119.9 21.1 %collective-permute-start.13 = (bf16[4,2,48,896]{3,2,1,0:T(8,128)(2,1)}, bf16[4,2,48,896]{3,2,1,0:T(8,128)(2,1)}, u32[]{:S(2)}, u32[]{:S(2)}) collective-permute-start(bf16[4,2,48,896]{3,2,1,0:T(8,128)(2,1)} %get-tuple-element.194), channel_id=1, source_target_pairs={{0,4},{4,0},{8,12},{12,8},{16,20},{20,16},{24,28},{28,24},{1,5},{5... | collective-permute-start | bytes 2064392 | tf_op jit(solution)/shard_map/ppermute | solution.py:563
  121.5 19.5 %collective-permute-start.12 = (bf16[4,2,48,640]{3,2,1,0:T(8,128)(2,1)}, bf16[4,2,48,640]{3,2,1,0:T(8,128)(2,1)}, u32[]{:S(2)}, u32[]{:S(2)}) collective-permute-start(bf16[4,2,48,640]{3,2,1,0:T(8,128)(2,1)} %get-tuple-element.193), channel_id=1, source_target_pairs={{0,2},{1,3},{2,0},{3,1},{4,6},{5,7},{6,4},{7,5},{8,10},{9,11},{10,... | collective-permute-start | bytes 1474568 | tf_op jit(solution)/shard_map/ppermute | solution.py:563
  141.0 22.5 %collective-permute-start.17 = (bf16[768,1536]{1,0:T(8,128)(2,1)}, bf16[768,1536]{1,0:T(8,128)(2,1)}, u32[]{:S(2)}, u32[]{:S(2)}) collective-permute-start(bf16[768,1536]{1,0:T(8,128)(2,1)} %get-tuple-element.210), channel_id=1, source_target_pairs={{0,1},{1,0},{2,3},{3,2},{4,5},{5,4},{6,7},{7,6},{8,9},{9,8},{10,11... | collective-permute-start | bytes 7077896 | tf_op jit(solution)/shard_map/ppermute | solution.py:563
  145.3 18.2 %collective-permute-start.16 = (bf16[4,2,48,896]{3,2,1,0:T(8,128)(2,1)}, bf16[4,2,48,896]{3,2,1,0:T(8,128)(2,1)}, u32[]{:S(2)}, u32[]{:S(2)}) collective-permute-start(bf16[4,2,48,896]{3,2,1,0:T(8,128)(2,1)} %get-tuple-element.209), channel_id=1, source_target_pairs={{0,4},{4,0},{8,12},{12,8},{16,20},{20,16},{24,28},{28,24},{1,5},{5... | collective-permute-start | bytes 2064392 | tf_op jit(solution)/shard_map/ppermute | solution.py:563
  145.9 17.5 %collective-permute-start.15 = (bf16[4,2,48,640]{3,2,1,0:T(8,128)(2,1)}, bf16[4,2,48,640]{3,2,1,0:T(8,128)(2,1)}, u32[]{:S(2)}, u32[]{:S(2)}) collective-permute-start(bf16[4,2,48,640]{3,2,1,0:T(8,128)(2,1)} %get-tuple-element.208), channel_id=1, source_target_pairs={{0,2},{1,3},{2,0},{3,1},{4,6},{5,7},{6,4},{7,5},{8,10},{9,11},{10,... | collective-permute-start | bytes 1474568 | tf_op jit(solution)/shard_map/ppermute | solution.py:563
  163.5 26.1 %collective-permute-start.20 = (bf16[768,1536]{1,0:T(8,128)(2,1)}, bf16[768,1536]{1,0:T(8,128)(2,1)}, u32[]{:S(2)}, u32[]{:S(2)}) collective-permute-start(bf16[768,1536]{1,0:T(8,128)(2,1)} %get-tuple-element.224), channel_id=1, source_target_pairs={{0,1},{1,0},{2,3},{3,2},{4,5},{5,4},{6,7},{7,6},{8,9},{9,8},{10,11... | collective-permute-start | bytes 7077896 | tf_op jit(solution)/shard_map/ppermute | solution.py:563
  167.8 21.9 %collective-permute-start.19 = (bf16[4,2,48,896]{3,2,1,0:T(8,128)(2,1)}, bf16[4,2,48,896]{3,2,1,0:T(8,128)(2,1)}, u32[]{:S(2)}, u32[]{:S(2)}) collective-permute-start(bf16[4,2,48,896]{3,2,1,0:T(8,128)(2,1)} %get-tuple-element.223), channel_id=1, source_target_pairs={{0,4},{4,0},{8,12},{12,8},{16,20},{20,16},{24,28},{28,24},{1,5},{5... | collective-permute-start | bytes 2064392 | tf_op jit(solution)/shard_map/ppermute | solution.py:563
  169.3 20.3 %collective-permute-start.18 = (bf16[4,2,48,640]{3,2,1,0:T(8,128)(2,1)}, bf16[4,2,48,640]{3,2,1,0:T(8,128)(2,1)}, u32[]{:S(2)}, u32[]{:S(2)}) collective-permute-start(bf16[4,2,48,640]{3,2,1,0:T(8,128)(2,1)} %get-tuple-element.222), channel_id=1, source_target_pairs={{0,2},{1,3},{2,0},{3,1},{4,6},{5,7},{6,4},{7,5},{8,10},{9,11},{10,... | collective-permute-start | bytes 1474568 | tf_op jit(solution)/shard_map/ppermute | solution.py:563
  189.6 40.7 %collective-permute-start.25 = (bf16[768,1536]{1,0:T(8,128)(2,1)}, bf16[768,1536]{1,0:T(8,128)(2,1)}, u32[]{:S(2)}, u32[]{:S(2)}) collective-permute-start(bf16[768,1536]{1,0:T(8,128)(2,1)} %get-tuple-element.240), channel_id=1, source_target_pairs={{0,1},{1,0},{2,3},{3,2},{4,5},{5,4},{6,7},{7,6},{8,9},{9,8},{10,11... | collective-permute-start | bytes 7077896 | tf_op jit(solution)/shard_map/ppermute | solution.py:563
  193.9 28.2 %collective-permute-start.22 = (bf16[4,2,48,896]{3,2,1,0:T(8,128)(2,1)}, bf16[4,2,48,896]{3,2,1,0:T(8,128)(2,1)}, u32[]{:S(2)}, u32[]{:S(2)}) collective-permute-start(bf16[4,2,48,896]{3,2,1,0:T(8,128)(2,1)} %get-tuple-element.237), channel_id=1, source_target_pairs={{0,4},{4,0},{8,12},{12,8},{16,20},{20,16},{24,28},{28,24},{1,5},{5... | collective-permute-start | bytes 2064392 | tf_op jit(solution)/shard_map/ppermute | solution.py:563
  194.5 27.6 %collective-permute-start.21 = (bf16[4,2,48,640]{3,2,1,0:T(8,128)(2,1)}, bf16[4,2,48,640]{3,2,1,0:T(8,128)(2,1)}, u32[]{:S(2)}, u32[]{:S(2)}) collective-permute-start(bf16[4,2,48,640]{3,2,1,0:T(8,128)(2,1)} %get-tuple-element.236), channel_id=1, source_target_pairs={{0,2},{1,3},{2,0},{3,1},{4,6},{5,7},{6,4},{7,5},{8,10},{9,11},{10,... | collective-permute-start | bytes 1474568 | tf_op jit(solution)/shard_map/ppermute | solution.py:563
  200.9 29.3 %collective-permute-start.24 = (bf16[4,3,48,896]{3,2,1,0:T(8,128)(2,1)}, bf16[4,3,48,896]{3,2,1,0:T(8,128)(2,1)}, u32[]{:S(2)}, u32[]{:S(2)}) collective-permute-start(bf16[4,3,48,896]{3,2,1,0:T(8,128)(2,1)} %get-tuple-element.239), channel_id=1, source_target_pairs={{0,2},{1,3},{2,0},{3,1},{4,6},{5,7},{6,4},{7,5},{8,10},{9,11},{10,... | collective-permute-start | bytes 3096584 | tf_op jit(solution)/shard_map/ppermute | solution.py:563
  202.5 25.5 %collective-permute-start.23 = (bf16[4,3,48,640]{3,2,1,0:T(8,128)(2,1)}, bf16[4,3,48,640]{3,2,1,0:T(8,128)(2,1)}, u32[]{:S(2)}, u32[]{:S(2)}) collective-permute-start(bf16[4,3,48,640]{3,2,1,0:T(8,128)(2,1)} %get-tuple-element.238), channel_id=1, source_target_pairs={{0,4},{4,0},{8,12},{12,8},{16,20},{20,16},{24,28},{28,24},{1,5},{5... | collective-permute-start | bytes 2211848 | tf_op jit(solution)/shard_map/ppermute | solution.py:563
  230.3 29.3 %collective-permute-start.30 = (bf16[768,1536]{1,0:T(8,128)(2,1)}, bf16[768,1536]{1,0:T(8,128)(2,1)}, u32[]{:S(2)}, u32[]{:S(2)}) collective-permute-start(bf16[768,1536]{1,0:T(8,128)(2,1)} %get-tuple-element.258), channel_id=1, source_target_pairs={{0,1},{1,0},{2,3},{3,2},{4,5},{5,4},{6,7},{7,6},{8,9},{9,8},{10,11... | collective-permute-start | bytes 7077896 | tf_op jit(solution)/shard_map/ppermute | solution.py:563
  234.6 25.1 %collective-permute-start.29 = (bf16[4,2,48,896]{3,2,1,0:T(8,128)(2,1)}, bf16[4,2,48,896]{3,2,1,0:T(8,128)(2,1)}, u32[]{:S(2)}, u32[]{:S(2)}) collective-permute-start(bf16[4,2,48,896]{3,2,1,0:T(8,128)(2,1)} %get-tuple-element.257), channel_id=1, source_target_pairs={{0,4},{4,0},{8,12},{12,8},{16,20},{20,16},{24,28},{28,24},{1,5},{5... | collective-permute-start | bytes 2064392 | tf_op jit(solution)/shard_map/ppermute | solution.py:563
  236.1 23.5 %collective-permute-start.28 = (bf16[4,2,48,640]{3,2,1,0:T(8,128)(2,1)}, bf16[4,2,48,640]{3,2,1,0:T(8,128)(2,1)}, u32[]{:S(2)}, u32[]{:S(2)}) collective-permute-start(bf16[4,2,48,640]{3,2,1,0:T(8,128)(2,1)} %get-tuple-element.256), channel_id=1, source_target_pairs={{0,2},{1,3},{2,0},{3,1},{4,6},{5,7},{6,4},{7,5},{8,10},{9,11},{10,... | collective-permute-start | bytes 1474568 | tf_op jit(solution)/shard_map/ppermute | solution.py:563
  240.0 19.6 %collective-permute-start.27 = (bf16[4,1,48,896]{3,2,1,0:T(8,128)(2,1)}, bf16[4,1,48,896]{3,2,1,0:T(8,128)(2,1)}, u32[]{:S(2)}, u32[]{:S(2)}) collective-permute-start(bf16[4,1,48,896]{3,2,1,0:T(8,128)(2,1)} %get-tuple-element.253), channel_id=1, source_target_pairs={{0,2},{1,3},{2,0},{3,1},{4,6},{5,7},{6,4},{7,5},{8,10},{9,11},{10,... | collective-permute-start | bytes 1032200 | tf_op jit(solution)/shard_map/ppermute | solution.py:563
  241.6 16.4 %collective-permute-start.26 = (bf16[4,1,48,640]{3,2,1,0:T(8,128)(2,1)}, bf16[4,1,48,640]{3,2,1,0:T(8,128)(2,1)}, u32[]{:S(2)}, u32[]{:S(2)}) collective-permute-start(bf16[4,1,48,640]{3,2,1,0:T(8,128)(2,1)} %get-tuple-element.252), channel_id=1, source_target_pairs={{0,4},{4,0},{8,12},{12,8},{16,20},{20,16},{24,28},{28,24},{1,5},{5... | collective-permute-start | bytes 737288 | tf_op jit(solution)/shard_map/ppermute | solution.py:563
  258.0 21.6 %collective-permute-start.31 = (bf16[2,3,48,1536]{3,2,1,0:T(8,128)(2,1)}, bf16[2,3,48,1536]{3,2,1,0:T(8,128)(2,1)}, u32[]{:S(2)}, u32[]{:S(2)}) collective-permute-start(bf16[2,3,48,1536]{3,2,1,0:T(8,128)(2,1)} %get-tuple-element.260), channel_id=1, source_target_pairs={{0,8},{4,12},{8,0},{12,4},{16,24},{20,28},{24,16},{28,20},{1,9},{5... | collective-permute-start | bytes 2654216 | tf_op jit(solution)/shard_map/ppermute | solution.py:563
  264.0 24.2 %collective-permute-start.35 = (bf16[4,2,48,896]{3,2,1,0:T(8,128)(2,1)}, bf16[4,2,48,896]{3,2,1,0:T(8,128)(2,1)}, u32[]{:S(2)}, u32[]{:S(2)}) collective-permute-start(bf16[4,2,48,896]{3,2,1,0:T(8,128)(2,1)} %get-tuple-element.270), channel_id=1, source_target_pairs={{0,4},{4,0},{8,12},{12,8},{16,20},{20,16},{24,28},{28,24},{1,5},{5... | collective-permute-start | bytes 2064392 | tf_op jit(solution)/shard_map/ppermute | solution.py:563
  267.0 21.2 %collective-permute-start.34 = (bf16[4,2,48,640]{3,2,1,0:T(8,128)(2,1)}, bf16[4,2,48,640]{3,2,1,0:T(8,128)(2,1)}, u32[]{:S(2)}, u32[]{:S(2)}) collective-permute-start(bf16[4,2,48,640]{3,2,1,0:T(8,128)(2,1)} %get-tuple-element.269), channel_id=1, source_target_pairs={{0,2},{1,3},{2,0},{3,1},{4,6},{5,7},{6,4},{7,5},{8,10},{9,11},{10,... | collective-permute-start | bytes 1474568 | tf_op jit(solution)/shard_map/ppermute | solution.py:563
  270.9 17.4 %collective-permute-start.33 = (bf16[4,1,48,896]{3,2,1,0:T(8,128)(2,1)}, bf16[4,1,48,896]{3,2,1,0:T(8,128)(2,1)S(1)}, u32[]{:S(2)}, u32[]{:S(2)}) collective-permute-start(bf16[4,1,48,896]{3,2,1,0:T(8,128)(2,1)} %get-tuple-element.266), channel_id=1, source_target_pairs={{0,2},{1,3},{2,0},{3,1},{4,6},{5,7},{6,4},{7,5},{8,10},{9,11},{10,... | collective-permute-start | bytes 1032200 | tf_op jit(solution)/shard_map/ppermute | solution.py:563
  272.5 13.8 %collective-permute-start.32 = (bf16[4,1,48,640]{3,2,1,0:T(8,128)(2,1)}, bf16[4,1,48,640]{3,2,1,0:T(8,128)(2,1)S(1)}, u32[]{:S(2)}, u32[]{:S(2)}) collective-permute-start(bf16[4,1,48,640]{3,2,1,0:T(8,128)(2,1)} %get-tuple-element.265), channel_id=1, source_target_pairs={{0,4},{4,0},{8,12},{12,8},{16,20},{20,16},{24,28},{28,24},{1,5},{5... | collective-permute-start | bytes 737288 | tf_op jit(solution)/shard_map/ppermute | solution.py:563
  290.8 35.8 %all-to-all-start = ((bf16[4,2,128,768]{3,2,1,0:T(8,128)(2,1)}), bf16[4,2,128,768]{3,2,1,0:T(8,128)(2,1)}, u32[]{:S(2)}, u32[]{:S(2)}) async-start(bf16[4,2,128,768]{3,2,1,0:T(8,128)(2,1)} %pad_maximum_fusion), calls=%async_computation | async-start | bytes 3145728 | tf_op jit(solution)/shard_map/all_to_all | solution.py:595
  297.9 28.6 %collective-permute-start.41 = (bf16[2,2,48,1536]{3,2,1,0:T(8,128)(2,1)}, bf16[2,2,48,1536]{3,2,1,0:T(8,128)(2,1)}, u32[]{:S(2)}, u32[]{:S(2)}) collective-permute-start(bf16[2,2,48,1536]{3,2,1,0:T(8,128)(2,1)} %get-tuple-element.294), channel_id=1, source_target_pairs={{0,8},{4,12},{8,0},{12,4},{16,24},{20,28},{24,16},{28,20},{1,9},{5... | collective-permute-start | bytes 1769480 | tf_op jit(solution)/shard_map/ppermute | solution.py:563
  300.8 24.9 %collective-permute-start.37 = (bf16[1,3,48,1536]{3,2,1,0:T(8,128)(2,1)}, bf16[1,3,48,1536]{3,2,1,0:T(8,128)(2,1)S(1)}, u32[]{:S(2)}, u32[]{:S(2)}) collective-permute-start(bf16[1,3,48,1536]{3,2,1,0:T(8,128)(2,1)} %get-tuple-element.278), channel_id=1, source_target_pairs={{0,16},{4,20},{8,24},{12,28},{16,0},{20,4},{24,8},{28,12},{1,17},{... | collective-permute-start | bytes 1327112 | tf_op jit(solution)/shard_map/ppermute | solution.py:563
  306.6 19.2 %collective-permute-start.39 = (bf16[4,1,48,896]{3,2,1,0:T(8,128)(2,1)}, bf16[4,1,48,896]{3,2,1,0:T(8,128)(2,1)S(1)}, u32[]{:S(2)}, u32[]{:S(2)}) collective-permute-start(bf16[4,1,48,896]{3,2,1,0:T(8,128)(2,1)} %get-tuple-element.284), channel_id=1, source_target_pairs={{0,2},{1,3},{2,0},{3,1},{4,6},{5,7},{6,4},{7,5},{8,10},{9,11},{10,... | collective-permute-start | bytes 1032200 | tf_op jit(solution)/shard_map/ppermute | solution.py:563
  308.6 17.1 %collective-permute-start.38 = (bf16[4,1,48,640]{3,2,1,0:T(8,128)(2,1)}, bf16[4,1,48,640]{3,2,1,0:T(8,128)(2,1)S(1)}, u32[]{:S(2)}, u32[]{:S(2)}) collective-permute-start(bf16[4,1,48,640]{3,2,1,0:T(8,128)(2,1)} %get-tuple-element.283), channel_id=1, source_target_pairs={{0,4},{4,0},{8,12},{12,8},{16,20},{20,16},{24,28},{28,24},{1,5},{5... | collective-permute-start | bytes 737288 | tf_op jit(solution)/shard_map/ppermute | solution.py:563
  310.1 15.7 %collective-permute-start.40 = (f32[2,24,768]{2,1,0:T(8,128)S(1)}, f32[2,24,768]{2,1,0:T(8,128)S(1)}, u32[]{:S(2)}, u32[]{:S(2)}) collective-permute-start(f32[2,24,768]{2,1,0:T(8,128)S(1)} %fusion.42), channel_id=1, source_target_pairs={{0,2},{1,3},{2,0},{3,1},{4,6},{5,7},{6,4},{7,5},{8,10},{9,11},{10,... | collective-permute-start | bytes 442376 | tf_op jit(solution)/shard_map/ppermute | solution.py:563
  328.9 12.8 %collective-permute-start.45 = (bf16[2,1,48,1536]{3,2,0,1:T(8,128)(2,1)}, bf16[2,1,48,1536]{3,2,0,1:T(8,128)(2,1)}, u32[]{:S(2)}, u32[]{:S(2)}) collective-permute-start(bf16[2,1,48,1536]{3,2,0,1:T(8,128)(2,1)} %bitcast.167), channel_id=1, source_target_pairs={{0,8},{4,12},{8,0},{12,4},{16,24},{20,28},{24,16},{28,20},{1,9},{5... | collective-permute-start | bytes 884744 | tf_op jit(solution)/shard_map/ppermute | solution.py:563
  330.6 18.4 %collective-permute-start.42 = (bf16[3,48,1536]{2,1,0:T(8,128)(2,1)S(1)}, bf16[3,48,1536]{2,1,0:T(8,128)(2,1)}, u32[]{:S(2)}, u32[]{:S(2)}) collective-permute-start(bf16[3,48,1536]{2,1,0:T(8,128)(2,1)S(1)} %add_bitcast_fusion), channel_id=1, source_target_pairs={{0,2},{1,3},{2,0},{3,1},{4,6},{5,7},{6,4},{7,5},{8,10},{9,11},{10,... | collective-permute-start | bytes 1327112 | tf_op jit(solution)/shard_map/ppermute | solution.py:563
  333.2 15.8 %collective-permute-start.44 = (bf16[1,2,48,1536]{3,2,1,0:T(8,128)(2,1)}, bf16[1,2,48,1536]{3,2,1,0:T(8,128)(2,1)S(1)}, u32[]{:S(2)}, u32[]{:S(2)}) collective-permute-start(bf16[1,2,48,1536]{3,2,1,0:T(8,128)(2,1)} %get-tuple-element.303), channel_id=1, source_target_pairs={{0,16},{4,20},{8,24},{12,28},{16,0},{20,4},{24,8},{28,12},{1,17},{... | collective-permute-start | bytes 884744 | tf_op jit(solution)/shard_map/ppermute | solution.py:563
  351.0 13.7 %collective-permute-start.46 = (bf16[3,96,1536]{2,1,0:T(8,128)(2,1)}, bf16[3,96,1536]{2,1,0:T(8,128)(2,1)}, u32[]{:S(2)}, u32[]{:S(2)}) collective-permute-start(bf16[3,96,1536]{2,1,0:T(8,128)(2,1)} %pad_maximum_fusion.1.tall), channel_id=1, source_target_pairs={{0,1},{1,0},{2,3},{3,2},{4,5},{5,4},{6,7},{7,6},{8,9},{9,8},{10,11... | collective-permute-start | bytes 2654216 | tf_op jit(solution)/shard_map/ppermute | solution.py:563
  351.0 13.7 %collective-permute-start.48 = (bf16[2,48,1536]{2,1,0:T(8,128)(2,1)S(1)}, bf16[2,48,1536]{2,1,0:T(8,128)(2,1)}, u32[]{:S(2)}, u32[]{:S(2)}) collective-permute-start(bf16[2,48,1536]{2,1,0:T(8,128)(2,1)S(1)} %add_bitcast_fusion.1), channel_id=1, source_target_pairs={{0,2},{1,3},{2,0},{3,1},{4,6},{5,7},{6,4},{7,5},{8,10},{9,11},{10,... | collective-permute-start | bytes 884744 | tf_op jit(solution)/shard_map/ppermute | solution.py:563
  354.3 10.4 %collective-permute-start.49 = (bf16[1,1,48,1536]{3,2,1,0:T(8,128)(2,1)}, bf16[1,1,48,1536]{3,2,1,0:T(8,128)(2,1)S(1)}, u32[]{:S(2)}, u32[]{:S(2)}) collective-permute-start(bf16[1,1,48,1536]{3,2,1,0:T(8,128)(2,1)} %get-tuple-element.315), channel_id=1, source_target_pairs={{0,16},{4,20},{8,24},{12,28},{16,0},{20,4},{24,8},{28,12},{1,17},{... | collective-permute-start | bytes 442376 | tf_op jit(solution)/shard_map/ppermute | solution.py:563
  354.4 10.3 %collective-permute-start.47 = (f32[2,24,768]{2,1,0:T(8,128)S(1)}, f32[2,24,768]{2,1,0:T(8,128)S(1)}, u32[]{:S(2)}, u32[]{:S(2)}) collective-permute-start(f32[2,24,768]{2,1,0:T(8,128)S(1)} %add.313), channel_id=1, source_target_pairs={{0,8},{4,12},{8,0},{12,4},{16,24},{20,28},{24,16},{28,20},{1,9},{5... | collective-permute-start | bytes 442376 | tf_op jit(solution)/shard_map/ppermute | solution.py:563
  365.8 11.9 %collective-permute-start.51 = (bf16[2,96,1536]{2,1,0:T(8,128)(2,1)S(1)}, bf16[2,96,1536]{2,1,0:T(8,128)(2,1)S(1)}, u32[]{:S(2)}, u32[]{:S(2)}) collective-permute-start(bf16[2,96,1536]{2,1,0:T(8,128)(2,1)S(1)} %pad_maximum_fusion.2.low), channel_id=1, source_target_pairs={{0,1},{1,0},{2,3},{3,2},{4,5},{5,4},{6,7},{7,6},{8,9},{9,8},{10,11... | collective-permute-start | bytes 1769480 | tf_op jit(solution)/shard_map/ppermute | solution.py:563
  365.9 6.7 %collective-permute-start.52 = (bf16[1,48,1536]{2,1,0:T(8,128)(2,1)S(1)}, bf16[1,48,1536]{2,1,0:T(8,128)(2,1)S(1)}, u32[]{:S(2)}, u32[]{:S(2)}) collective-permute-start(bf16[1,48,1536]{2,1,0:T(8,128)(2,1)S(1)} %add_bitcast_fusion.2.own), channel_id=1, source_target_pairs={{0,2},{1,3},{2,0},{3,1},{4,6},{5,7},{6,4},{7,5},{8,10},{9,11},{10,... | collective-permute-start | bytes 442376 | tf_op jit(solution)/shard_map/ppermute | solution.py:563
  366.6 6.0 %collective-permute-start.53 = (bf16[1,48,1536]{2,1,0:T(8,128)(2,1)S(1)}, bf16[1,48,1536]{2,1,0:T(8,128)(2,1)S(1)}, u32[]{:S(2)}, u32[]{:S(2)}) collective-permute-start(bf16[1,48,1536]{2,1,0:T(8,128)(2,1)S(1)} %add_bitcast_fusion.2.own), channel_id=1, source_target_pairs={{0,1},{1,0},{2,3},{3,2},{4,5},{5,4},{6,7},{7,6},{8,9},{9,8},{10,11... | collective-permute-start | bytes 442376 | tf_op jit(solution)/shard_map/ppermute | solution.py:563
  366.8 8.2 %collective-permute-start.54 = (bf16[1,48,1536]{2,1,0:T(8,128)(2,1)S(1)}, bf16[1,48,1536]{2,1,0:T(8,128)(2,1)S(1)}, u32[]{:S(2)}, u32[]{:S(2)}) collective-permute-start(bf16[1,48,1536]{2,1,0:T(8,128)(2,1)S(1)} %add_bitcast_fusion.2.own), channel_id=1, source_target_pairs={{0,3},{1,2},{2,1},{3,0},{4,7},{5,6},{6,5},{7,4},{8,11},{9,10},{10,... | collective-permute-start | bytes 442376 | tf_op jit(solution)/shard_map/ppermute | solution.py:813
  368.2 9.6 %collective-permute-start.50 = (f32[2,24,768]{2,1,0:T(8,128)S(1)}, f32[2,24,768]{2,1,0:T(8,128)S(1)}, u32[]{:S(2)}, u32[]{:S(2)}) collective-permute-start(f32[2,24,768]{2,1,0:T(8,128)S(1)} %add.315), channel_id=1, source_target_pairs={{0,16},{4,20},{8,24},{12,28},{16,0},{20,4},{24,8},{28,12},{1,17},{... | collective-permute-start | bytes 442376 | tf_op jit(solution)/shard_map/ppermute | solution.py:563
  (68 other events, 547.6 us)
